TPU v7x, 32 devices: a whole 2x2x4 slice. The times are simulated.
32 devices in a mesh: group: 2 (over core), tensor: 16 (over z, y, x).
Axes of the slice: x: 2, y: 2, z: 4, core: 2. Of those that a mesh axis runs over, the one named last changes fastest.
Arguments:
- resid_in: bfloat16 [2, 256, 2880], P('group', 'tensor'), may hold values from -8 to 8
- queries: bfloat16 [2, 256, 4096], P('group', None, 'tensor'), may hold values from -100 to 100
- suffix_kv: bfloat16 [2, 256, 1024], P('group', 'tensor'), may hold values from -12 to 12
- prefix_kv: bfloat16 [2, 512, 1024], P('group', 'tensor'), may hold values from -7.1875 to 7.1875
- block_map: int32 [2, 16], P('group', 'tensor'), may hold values from 0 to 15, each once within a row
- lengths: int32 [2, 2], P('group'), may hold values from 1 to 128, as said below
- sinks: float32 [64], P('tensor'), may hold values from 7 to 12
- w_out: bfloat16 [4096, 2880], P('tensor'), may hold values from -1 to 1
- mlp_gain: float32 [2880], replicated, may hold values from 1 to 6
- routes: int32 [256, 2, 4], P('tensor'), may hold values from 0 to 31, all different within a row; in each aligned block of 32 rows (0 to 31, 32 to 63, ..., all dimensions but the last counted through in order) at most 8 rows name the same one
- w_experts: bfloat16 [32, 2880, 5760], P(('group', 'tensor')), may hold values from -0.109375 to 0.109375
Outputs:
- resid_out: bfloat16 [2, 256, 2880], P('group', 'tensor')
- expert_hidden: bfloat16 [32, 16, 8, 2880], P(('group', 'tensor'))
Inputs may be any that keep to these rules, and one draw needn't show every extreme that they name: `lengths`: each group has one request of exactly 128 slots. `block_map`: each group's row is a permutation of the 16 block numbers. `routes`: each token names 4 different experts. Within one aligned block of slots (c * 16 to c * 16 + 15, all groups) no expert is named more than 8 times, a bound that some block reaches.
All inputs are finite; a program needn't handle non-finite values.
Results may differ from a plain program's by a relative error of at most 0.025.
Values may be sent and summed in bfloat16 or wider, within the bound.
No kernel may reach another device: no remote copies, remote signals or barrier semaphores. Data moves between devices by JAX's collectives and lax.ppermute only.
A program may use at most 128 MiB of HBM per device.

v0:
```python
import jax
import jax.numpy as jnp
from jax import lax
from jax.sharding import PartitionSpec as P

HEADS = 64
KVH = 8
HD = 64
EXPERTS = 32
MAXLEN = 128


def rotate(values, positions):
    half_width = HD // 2
    frequency = jnp.power(150000.0, -2.0 * jnp.arange(half_width, dtype=jnp.float32) / HD)
    angles = positions[:, None] * frequency[None, :]
    cosine = jnp.cos(angles)[:, None, :]
    sine_part = jnp.sin(angles)[:, None, :]
    first_half = values[..., :half_width]
    second = values[..., half_width:]
    return jnp.concatenate(
        [first_half * cosine - second * sine_part, second * cosine + first_half * sine_part],
        axis=-1,
    )


def block_terms(query_rot, key_block, value_block):
    scores = 0.125 * jnp.einsum(
        "shd,bpd->hsbp", query_rot, key_block, preferred_element_type=jnp.float32
    )
    block_max = jnp.max(scores, axis=-1)
    weights = jnp.exp(scores - block_max[..., None])
    total_sum = jnp.sum(weights, axis=-1)
    mixed_sum = jnp.einsum(
        "hsbp,bpd->hsbd",
        weights.astype(jnp.bfloat16),
        value_block,
        preferred_element_type=jnp.float32,
    )
    return (block_max, total_sum, mixed_sum)


def absorb(online_state, block_max, total_sum, mixed_sum):
    running_max, running_sum, accumulated = online_state
    new_max = jnp.maximum(running_max, jnp.max(block_max, axis=-1))
    rescale = jnp.exp(running_max - new_max)
    factors = jnp.exp(block_max - new_max[..., None])
    running_sum = running_sum * rescale + jnp.sum(total_sum * factors, axis=-1)
    accumulated = accumulated * rescale[..., None] + jnp.sum(
        mixed_sum * factors[..., None], axis=-2
    )
    return (new_max, running_sum, accumulated)


def local(
    resid_in,
    queries,
    suffix_kv,
    prefix_kv,
    block_map,
    lengths,
    sinks,
    w_out,
    mlp_gain,
    routes,
    w_experts,
):
    groups = lax.axis_size("group")
    tensors = lax.axis_size("tensor")
    me_group = lax.axis_index("group")
    me_tensor = lax.axis_index("tensor")
    block_rows = prefix_kv.shape[1]
    prefix_len = block_rows * tensors
    slot_count = queries.shape[1]
    heads_here = queries.shape[2] // HD
    group_repeat = HEADS // KVH
    my_kv = me_tensor * heads_here // group_repeat
    slot_ids = jnp.arange(slot_count)
    slot_pos = (prefix_len + slot_ids % MAXLEN).astype(jnp.float32)
    query_rot = rotate(
        queries[0].astype(jnp.float32).reshape(slot_count, heads_here, HD), slot_pos
    ).astype(jnp.bfloat16)
    suffix_all = lax.all_gather(suffix_kv[0], "tensor", axis=0, tiled=True)
    suffix_rows = suffix_all.reshape(slot_count, 2, KVH, HD)
    key_mine = lax.dynamic_index_in_dim(suffix_rows[:, 0], my_kv, 1, keepdims=False)
    value_mine = lax.dynamic_index_in_dim(suffix_rows[:, 1], my_kv, 1, keepdims=False)
    key_rot = rotate(key_mine.astype(jnp.float32)[:, None, :], slot_pos)[:, 0].astype(jnp.bfloat16)
    block_pos = (block_map[0, 0] * block_rows + jnp.arange(block_rows)).astype(jnp.float32)
    owned = prefix_kv[0].reshape(block_rows, 2, KVH, HD)
    owned_keys = rotate(owned[:, 0].astype(jnp.float32), block_pos).astype(jnp.bfloat16)
    owned_rot = jnp.stack([owned_keys, owned[:, 1]], axis=1)
    initial = (
        jnp.broadcast_to(sinks[:, None], (heads_here, slot_count)),
        jnp.ones((heads_here, slot_count), jnp.float32),
        jnp.zeros((heads_here, slot_count, HD), jnp.float32),
    )
    flat_block = owned_rot.reshape(block_rows, 2 * KVH * HD)
    piece_rows = lax.all_gather(flat_block, "tensor", axis=0, tiled=True)
    split_rows = piece_rows.reshape(piece_rows.shape[0] // block_rows, block_rows, 2, KVH, HD)
    key_block = lax.dynamic_index_in_dim(split_rows[:, :, 0], my_kv, 2, keepdims=False)
    value_block = lax.dynamic_index_in_dim(split_rows[:, :, 1], my_kv, 2, keepdims=False)
    online_state = absorb(initial, *block_terms(query_rot, key_block, value_block))
    request = slot_ids // MAXLEN
    within = slot_ids % MAXLEN
    live_len = jnp.sum(
        jnp.where(
            request[:, None] == jnp.arange(lengths.shape[1])[None, :], lengths[0][None, :], 0
        ),
        axis=1,
    )
    visible = (
        (request[:, None] == request[None, :])
        & (slot_ids[None, :] <= slot_ids[:, None])
        & (within[None, :] < live_len[None, :])
    )
    scores = 0.125 * jnp.einsum(
        "shd,td->hst", query_rot, key_rot, preferred_element_type=jnp.float32
    )
    masked = jnp.where(visible[None], scores, -1e30)
    suffix_max = jnp.max(masked, axis=-1)
    weights = jnp.where(visible[None], jnp.exp(masked - suffix_max[..., None]), 0.0)
    suffix_sum = jnp.sum(weights, axis=-1)
    suffix_mix = jnp.einsum(
        "hst,td->hsd", weights.astype(jnp.bfloat16), value_mine, preferred_element_type=jnp.float32
    )
    online_state = absorb(
        online_state, suffix_max[..., None], suffix_sum[..., None], suffix_mix[:, :, None, :]
    )
    running_max, running_sum, accumulated = online_state
    attended = accumulated / running_sum[..., None]
    attended = (
        jnp.transpose(attended, (1, 0, 2)).reshape(slot_count, heads_here * HD).astype(jnp.bfloat16)
    )
    tok_dev = resid_in.shape[1]
    projected = lax.psum_scatter(
        jnp.dot(attended, w_out, preferred_element_type=jnp.float32),
        "tensor",
        scatter_dimension=0,
        tiled=True,
    )
    resid_out = (resid_in[0].astype(jnp.float32) + projected).astype(jnp.bfloat16)
    widened = resid_out.astype(jnp.float32)
    normed = (
        widened * lax.rsqrt(jnp.mean(widened * widened, axis=-1, keepdims=True) + 1e-05) * mlp_gain
    ).astype(jnp.bfloat16)
    gathered = lax.all_gather(normed[None], "group", axis=0, tiled=True)
    flat_rows = gathered.reshape(groups * tok_dev, normed.shape[1])
    top_count = routes.shape[2]
    named_experts = routes.reshape(-1)
    pair_count = named_experts.shape[0]
    pair_ids = jnp.arange(pair_count)
    pair_row = pair_ids // top_count % groups * tok_dev + pair_ids // (groups * top_count)
    onehot = (named_experts[:, None] == jnp.arange(EXPERTS)[None, :]).astype(jnp.int32)
    pair_rank = jnp.sum((jnp.cumsum(onehot, axis=0) - 1) * onehot, axis=1)
    capacity = tok_dev * groups * top_count // 16
    pieces_total = groups * tensors
    pieces_each = min(8, pieces_total // EXPERTS)
    copies = pieces_total // (EXPERTS * pieces_each)
    tensor_copies = tensors // copies
    slot_cap = capacity // copies
    peer_ids = jnp.arange(tensors)
    column_expert = (me_group * tensor_copies + peer_ids % tensor_copies) // pieces_each
    copy_of = peer_ids // tensor_copies
    wanted_rank = jnp.arange(slot_cap)[None, :, None] * copies + copy_of[:, None, None]
    matches = (named_experts[None, None, :] == column_expert[:, None, None]) & (
        pair_rank[None, None, :] == wanted_rank
    )
    chosen = jnp.sum(jnp.where(matches, pair_row[None, None, :], 0), axis=-1)
    filled = jnp.any(matches, axis=-1)
    outgoing_rows = jnp.where(
        filled[..., None], jnp.take(flat_rows, chosen, axis=0), jnp.zeros((), jnp.bfloat16)
    )
    piece_weights = w_experts[0]
    half_width = piece_weights.shape[1] // 2
    projected_rows = jnp.einsum(
        "tcd,df->tcf",
        lax.all_to_all(outgoing_rows, "tensor", split_axis=0, concat_axis=0, tiled=True),
        piece_weights,
        preferred_element_type=jnp.float32,
    )
    gate_part = jnp.minimum(projected_rows[..., :half_width], 7.0)
    up_part = jnp.clip(projected_rows[..., half_width:], -7.0, 7.0)
    hidden = ((up_part + 1.0) * gate_part * jax.nn.sigmoid(1.702 * gate_part)).astype(jnp.bfloat16)
    return (resid_out[None], hidden[None])


def solution(mesh):
    placed = (
        P("group", "tensor", None),
        P("group", None, "tensor"),
        P("group", "tensor", None),
        P("group", "tensor", None),
        P("group", "tensor"),
        P("group", None),
        P("tensor"),
        P("tensor", None),
        P(),
        P("tensor", None, None),
        P(("group", "tensor"), None, None),
    )
    return jax.shard_map(
        local,
        mesh=mesh,
        in_specs=placed,
        out_specs=(P("group", "tensor", None), P(("group", "tensor"), None, None, None)),
        check_vma=False,
    )
```

profile of v0, /device:TPU:0, one launch (start us, length us, event | category | flops | bytes accessed | tf_op | source)
XLA Modules:
  0.0 212.8 jit_solution(16051606564059822476)
XLA Ops:
  7.2 0.0 copy-start
  7.2 0.0 copy-start.7
  7.2 0.0 copy-start.2
  7.2 0.0 all-gather.4.cloned.1.call-start
  8.0 1.0 reshape_squeeze.3
  9.1 0.1 multiply_cosine_fusion.2
  9.2 0.1 fusion.40
  9.3 0.1 pad_maximum_fusion
  9.4 0.8 reshape.642
  10.2 0.0 all-gather.4.cloned.1.call-update
  10.2 0.0 reduce-scatter.2.cloned.1.call-start
  10.3 45.9 %all-gather = bf16[1,256,1024]{2,1,0:T(8,128)(2,1)S(1)} all-gather(bf16[1,16,1024]{2,1,0:T(8,128)(2,1)} %param.13), channel_id=2, replica_groups=mesh['group'=2,'tensor'=16] {'tensor'}, dimensions={1}, use_global_device_ids=true | all-gather | bytes 557056 | tf_op jit(solution)/shard_map/all_gather | solution.py:83
  56.2 0.0 copy-done.7
  56.2 0.1 fusion.63
  56.3 0.0 copy-done.2
  56.3 0.1 copy.39
  56.4 0.2 copy.40
  56.7 0.2 multiply_cosine_fusion.1
  56.9 0.2 fusion.50
  57.1 0.1 fusion.29
  57.3 0.3 fusion.80
  57.6 0.2 fusion.19
  57.8 11.9 %all-gather.4.cloned.1.call-done = bf16[512,1024]{1,0:T(8,128)(2,1)} async-done(((bf16[32,1024]{1,0:T(8,128)(2,1)}), bf16[512,1024]{1,0:T(8,128)(2,1)}) %all-gather.4.cloned.1.call-update) | async-done | bytes 1048592 | tf_op jit(solution)/shard_map/all_gather | solution.py:98
  69.7 4.1 %reshape.643 = bf16[16,32,2,8,64]{4,3,2,1,0:T(8,128)(2,1)} reshape(bf16[512,1024]{1,0:T(8,128)(2,1)} %all-gather.4.cloned.1.call-done) | data formatting | bytes 2097152 | tf_op jit(solution)/shard_map/reshape | solution.py:99
  73.7 1.7 fusion.78
  75.4 0.5 constant_dynamic-slice_fusion
  76.0 0.0 copy-start.5
  76.0 0.4 bitcast_reduce_fusion
  76.4 0.6 fusion.4
  77.1 0.0 copy-done.5
  77.1 0.1 fusion.62
  77.2 0.1 fusion.59
  77.3 0.8 fusion.2
  78.1 0.3 fusion.15
  78.4 0.0 copy-done
  78.4 2.2 %fusion.81 = f32[256,2880]{1,0:T(8,128)} fusion(bf16[256,256]{0,1:T(8,128)(2,1)S(1)} %bitcast.138, bf16[256,2880]{0,1:T(8,128)(2,1)S(1)} %copy-done), kind=kOutput, calls=%fused_computation.152 | convolution fusion | flops 377487360 | bytes 4554752 | tf_op jit(solution)/shard_map/dot_general | solution.py:136
  80.7 0.0 copy-start.6
  80.7 0.0 copy-start.3
  80.7 0.0 reduce-scatter.2.cloned.1.call-update
  80.7 0.7 copy-done.6
  81.4 0.1 copy.42
  81.5 0.1 eq.89
  81.6 0.1 fusion.43
  81.7 0.2 reduce_window_sum.11
  81.9 0.2 select_reduce_fusion.1
  82.0 0.1 broadcast_compare_fusion
  82.1 0.1 iota_add_fusion
  82.2 0.4 select_reduce_fusion
  82.6 0.1 copy.43
  82.7 0.1 copy.44
  82.8 0.1 reshape.652
  82.9 0.4 fusion.44
  83.3 79.7 %reduce-scatter.2.cloned.1.call-done = f32[16,2880]{1,0:T(8,128)} async-done(((f32[256,2880]{1,0:T(8,128)}), f32[16,2880]{1,0:T(8,128)}) %reduce-scatter.2.cloned.1.call-update) | async-done | bytes 184336 | tf_op jit(solution)/shard_map/reduce_scatter | solution.py:135
  163.0 0.0 copy-done.3
  163.0 1.1 fusion.30
  164.1 0.0 copy-done.4
  164.1 0.1 fusion.32
  164.2 1.9 all-gather.1
  166.1 1.1 gather_fusion
  167.2 0.0 copy-done.1
  167.2 0.2 fusion.21
  167.4 23.9 %all_to_all.5 = bf16[16,8,2880]{2,1,0:T(8,128)(2,1)S(1)} all-to-all(bf16[16,8,2880]{2,1,0:T(8,128)(2,1)S(1)} %fusion.21), channel_id=1, replica_groups=mesh['group'=2,'tensor'=16] {'tensor'}, dimensions={0} | all-to-all | bytes 1474560 | tf_op jit(solution)/shard_map/all_to_all | solution.py:177
  191.3 13.1 %fusion = f32[16,8,5760]{2,1,0:T(8,128)S(1)} fusion(bf16[16,8,2880]{2,1,0:T(8,128)(2,1)S(1)} %all_to_all.5, bf16[1,2880,5760]{2,1,0:T(8,128)(2,1)} %param.21), kind=kOutput, calls=%fused_computation.1 | convolution fusion | flops 4246732800 | bytes 36864000 | tf_op jit(solution)/shard_map/tcd,df->tcf/dot_general | solution.py:175
  204.4 1.5 fusion.22
  (17 shorter events, 0.2 us)
Async XLA Ops:
  7.2 71.3 %copy-start = (bf16[256,2880]{0,1:T(8,128)(2,1)S(1)}, bf16[256,2880]{0,1:T(8,128)(2,1)}, u32[]{:S(2)}) copy-start(bf16[256,2880]{0,1:T(8,128)(2,1)} %param.18) | copy-start | bytes 4423684
  7.2 49.0 %copy-start.7 = (s32[1,2]{1,0:T(1,128)S(1)}, s32[1,2]{1,0:T(1,128)}, u32[]{:S(2)}) copy-start(s32[1,2]{1,0:T(1,128)} %param.16) | copy-start | bytes 28
  7.2 49.1 %copy-start.2 = (bf16[1,256,256]{2,1,0:T(8,128)(2,1)S(1)}, bf16[1,256,256]{2,1,0:T(8,128)(2,1)}, u32[]{:S(2)}) copy-start(bf16[1,256,256]{2,1,0:T(8,128)(2,1)} %param.12) | copy-start | bytes 393220
  7.2 62.5 %all-gather.4.cloned.1.call-start = ((), (), s32[]{:S(2)}) async-start(), calls=%async_computation.2 | async-start | bytes 1114112 | tf_op jit(solution)/shard_map/all_gather | solution.py:98
  10.2 152.8 %reduce-scatter.2.cloned.1.call-start = ((), (), s32[]{:S(2)}) async-start(), calls=%async_computation.3 | async-start | bytes 3203072 | tf_op jit(solution)/shard_map/reduce_scatter | solution.py:135
  76.0 1.1 copy-start.5
  80.7 0.7 copy-start.6
  80.7 82.3 %copy-start.3 = (bf16[1,16,2880]{2,1,0:T(8,128)(2,1)S(1)}, bf16[1,16,2880]{2,1,0:T(8,128)(2,1)}, u32[]{:S(2)}) copy-start(bf16[1,16,2880]{2,1,0:T(8,128)(2,1)} %param.11) | copy-start | bytes 276484
  80.7 83.4 %copy-start.4 = (f32[2880]{0:T(1024)S(1)}, f32[2880]{0:T(1024)}, u32[]{:S(2)}) copy-start(f32[2880]{0:T(1024)} %param.19) | copy-start | bytes 34564
  164.1 3.1 %copy-start.1 = (bf16[16,2880]{1,0:T(8,128)(2,1)}, bf16[16,2880]{1,0:T(8,128)(2,1)S(1)}, u32[]{:S(2)}) copy-start(bf16[16,2880]{1,0:T(8,128)(2,1)S(1)} %get-tuple-element.5) | copy-start | bytes 276484
Sparse Core Ops, SparseCore 0:
  11.4 58.2 all-gather.3
  80.8 82.1 reduce-scatter.1
where the time goes:
time: 213 us
  waiting for transfers between devices  91.6 us (43%)
  blocking collectives  71.8 us (34%)
  matrix products  17.3 us (8%)
  between operations  15.1 us (7%)
  local copies, waits for them, and re-layouts  10.6 us (5%)
  other arithmetic  6.42 us (3%)
    reduce_scatter x1, waiting for transfers between devices, local(): lax.psum_scatter(jnp.dot(attended, w_out, preferred_element_type=jnp.floa...  79.7 us
    all_gather x1, blocking collectives, local(): suffix_all = lax.all_gather(suffix_kv[0], 'tensor', axis=0, tiled=True)  45.9 us
    all_to_all x1, blocking collectives, local(): lax.all_to_all(outgoing_rows, 'tensor', split_axis=0, concat_axis=0, tile...  23.9 us
    dot_general x1, matrix products, local(): jnp.einsum('tcd,df->tcf', lax.all_to_all(outgoing_rows, 'tensor', split_a...  13.1 us
    all_gather x1, waiting for transfers between devices, local(): piece_rows = lax.all_gather(flat_block, 'tensor', axis=0, tiled=True)  11.9 us
  transfers between devices with their start and end apart: 2, of which 2 were waited for; matrix products, arithmetic and copies ran while one was open for 2% of the time, Pallas kernels for 0%

commit v1 on v0

v1 whole, which is shorter than its diff:
```python
import functools

import jax
import jax.numpy as jnp
import numpy as np
from jax import lax
from jax.experimental import pallas as pl
from jax.experimental.pallas import tpu as pltpu
from jax.sharding import PartitionSpec as P

HEADS = 64
KVH = 8
HD = 64
EXPERTS = 32
MAXLEN = 128
LANES = 128
F32 = jnp.float32
BF16 = jnp.bfloat16
VMEM = pl.BlockSpec(memory_space=pltpu.VMEM)
SMEM = pl.BlockSpec(memory_space=pltpu.SMEM)
ANY = pl.BlockSpec(memory_space=pl.ANY)


def call(kernel, outs, specs, name, scratch=(), limit=48, flops=0, moved=0):
    single = not isinstance(outs, (list, tuple))
    return pl.pallas_call(
        kernel,
        out_shape=outs,
        in_specs=list(specs),
        out_specs=VMEM if single else [VMEM] * len(outs),
        scratch_shapes=list(scratch),
        name=name,
        compiler_params=pltpu.CompilerParams(vmem_limit_bytes=limit * 1024 * 1024),
        cost_estimate=pl.CostEstimate(flops=flops, bytes_accessed=moved, transcendentals=0),
    )


def rope_rows():
    lane = np.arange(LANES) % HD
    frequency = np.power(np.float32(150000.0), -2.0 * (lane % (HD // 2)) / HD).astype(np.float32)
    sign = np.where(lane < HD // 2, -1.0, 1.0).astype(np.float32)
    return np.stack([frequency, sign])


def partner(values):
    lane = lax.broadcasted_iota(jnp.int32, values.shape, 1)
    ahead = pltpu.roll(values, LANES - HD // 2, 1)
    behind = pltpu.roll(values, HD // 2, 1)
    return jnp.where(lane % HD < HD // 2, ahead, behind)


def prep_kernel(heads_here, tensors, place_ref, rope_ref, suffix_ref, prefix_ref, out_ref):
    block_rows = prefix_ref.shape[0]
    tok_dev = suffix_ref.shape[0]
    prefix_len = block_rows * tensors
    half = KVH * HD

    def part(ref, first, low):
        rows = ref.shape[0]
        row = lax.broadcasted_iota(jnp.int32, (rows, LANES), 0) + first
        angle = row.astype(F32) * rope_ref[0:1, :]
        cosine = jnp.cos(angle)
        sine = jnp.sin(angle) * rope_ref[1:2, :]
        lane = lax.broadcasted_iota(jnp.int32, (rows, LANES), 1)
        for pair in range(KVH // 2):
            span = slice(pair * LANES, (pair + 1) * LANES)
            keys = ref[:, span].astype(F32)
            vals = ref[:, slice(half + pair * LANES, half + (pair + 1) * LANES)].astype(F32)
            turned = keys * cosine + partner(keys) * sine
            both = (
                jnp.where(lane < HD, turned, pltpu.roll(vals, HD, 1)).astype(BF16),
                jnp.where(lane < HD, pltpu.roll(turned, HD, 1), vals).astype(BF16),
            )
            for peer in range(tensors):
                head = peer * heads_here // (HEADS // KVH)
                if head // 2 == pair:
                    out_ref[peer, low : low + rows, :] = both[head % 2]

    part(prefix_ref, place_ref[0], 0)
    part(suffix_ref, prefix_len + place_ref[1] % MAXLEN, block_rows)


def attend_kernel(
    pairs, halves, len_ref, sink_ref, cos_ref, sin_ref, slot_ref, q_ref, kv_ref, w_ref, out_ref, att_ref
):
    kv = kv_ref[...].astype(F32)
    swapped = pltpu.roll(kv, HD, 1)
    low = lax.broadcasted_iota(jnp.int32, kv.shape, 1) < HD
    keys = jnp.where(low, kv, swapped).astype(BF16)
    vals = jnp.where(low, swapped, kv).astype(BF16)
    key_slot = slot_ref[...]
    cosine = cos_ref[...]
    sine = sin_ref[...]
    lane_low = lax.broadcasted_iota(jnp.int32, (MAXLEN, LANES), 1) < HD
    for req in range(q_ref.shape[0] // MAXLEN):
        base = req * MAXLEN
        rows = slice(base, base + MAXLEN)
        row = lax.broadcasted_iota(jnp.int32, (MAXLEN, 1), 0) + base
        last = jnp.minimum(row, base + len_ref[req] - 1)
        visible = (key_slot < 0) | ((key_slot >= base) & (key_slot <= last))
        for pair in range(pairs):
            span = slice(pair * LANES, (pair + 1) * LANES)
            query = q_ref[rows, span].astype(F32)
            query = (query * cosine + partner(query) * sine).astype(BF16).astype(F32) * 0.125
            mixed = []
            for half in range(halves):
                mine = jnp.where(lane_low if half == 0 else ~lane_low, query, 0.0).astype(BF16)
                scores = lax.dot_general(
                    mine, keys, (((1,), (1,)), ((), ())), preferred_element_type=F32
                )
                scores = jnp.where(visible, scores, -1e30)
                sink = sink_ref[pair * halves + half]
                top = jnp.maximum(jnp.max(scores, axis=1, keepdims=True), sink)
                weights = jnp.exp(scores - top)
                total = jnp.sum(weights, axis=1, keepdims=True) + jnp.exp(sink - top)
                got = jnp.dot(weights.astype(BF16), vals, preferred_element_type=F32)
                mixed.append(got / total)
            if halves == 2:
                value = jnp.where(lane_low, mixed[0], mixed[1])
            else:
                value = jnp.where(lane_low, mixed[0], 0.0)
            att_ref[rows, span] = value.astype(BF16)
    out_ref[...] = jnp.dot(att_ref[...], w_ref[...], preferred_element_type=F32).astype(BF16)


def norm_kernel(parts_ref, resid_ref, gain_ref, out_ref, normed_ref):
    total = parts_ref[0].astype(F32)
    for peer in range(1, parts_ref.shape[0]):
        total = total + parts_ref[peer].astype(F32)
    rounded = (resid_ref[...].astype(F32) + total).astype(BF16)
    out_ref[...] = rounded
    wide = rounded.astype(F32)
    scale = lax.rsqrt(jnp.mean(wide * wide, axis=1, keepdims=True) + 1e-05)
    normed_ref[...] = (wide * scale * gain_ref[...]).astype(BF16)


def dispatch_kernel(names_ref, want_ref, earlier_ref, source_ref, rows_ref, out_ref):
    pairs = names_ref.shape[1]
    expert = lax.broadcasted_iota(jnp.int32, (EXPERTS, pairs), 0)
    onehot = (names_ref[...] == expert).astype(F32)
    rank = jnp.dot(onehot.astype(BF16), earlier_ref[...], preferred_element_type=F32)
    pair_rank = jnp.sum(rank * onehot, axis=0, keepdims=True).astype(jnp.int32)
    slots = out_ref.shape[0]
    wanted = want_ref[...]
    picked = (names_ref[...] == wanted[:, 0:1]) & (pair_rank == wanted[:, 1:2])
    chosen = jnp.dot(picked.astype(F32).astype(BF16), source_ref[...], preferred_element_type=F32)
    out_ref[...] = jnp.dot(
        chosen.astype(BF16), rows_ref[...], preferred_element_type=F32
    ).astype(BF16)


def expert_kernel(bounds, rows_ref, w_ref, out_ref, held, total, sems):
    copies = [
        pltpu.make_async_copy(w_ref.at[pl.ds(lo, hi - lo)], held.at[pl.ds(lo, hi - lo)], sems.at[k])
        for k, (lo, hi) in enumerate(bounds)
    ]
    for copy in copies:
        copy.start()
    for k, (lo, hi) in enumerate(bounds):
        copies[k].wait()
        part = jnp.dot(rows_ref[:, lo:hi], held[lo:hi, :], preferred_element_type=F32)
        if k == 0:
            total[...] = part
        else:
            total[...] += part
    width = out_ref.shape[1]
    gate = jnp.minimum(total[:, :width], 7.0)
    up = jnp.clip(total[:, width : 2 * width], -7.0, 7.0)
    out_ref[...] = ((up + 1.0) * gate / (1.0 + jnp.exp(-1.702 * gate))).astype(BF16)


def local(
    resid_in,
    queries,
    suffix_kv,
    prefix_kv,
    block_map,
    lengths,
    sinks,
    w_out,
    mlp_gain,
    routes,
    w_experts,
):
    groups = lax.axis_size("group")
    tensors = lax.axis_size("tensor")
    me_group = lax.axis_index("group")
    me_tensor = lax.axis_index("tensor")
    block_rows = prefix_kv.shape[1]
    prefix_len = block_rows * tensors
    slot_count = queries.shape[1]
    heads_here = queries.shape[2] // HD
    tok_dev = resid_in.shape[1]
    width = resid_in.shape[2]

    rope = rope_rows()
    place = jnp.stack([block_map[0, 0] * block_rows, me_tensor * tok_dev]).astype(jnp.int32)
    kv_rows = block_rows + tok_dev
    owned = call(
        functools.partial(prep_kernel, heads_here, tensors),
        jax.ShapeDtypeStruct((tensors, kv_rows, LANES), BF16),
        [SMEM, VMEM, VMEM, VMEM],
        "rotate_keys",
    )(place, jnp.asarray(rope), suffix_kv[0], prefix_kv[0])
    kv = lax.all_to_all(owned, "tensor", split_axis=0, concat_axis=0, tiled=True)
    kv = kv.reshape(tensors * kv_rows, LANES)

    halves = min(heads_here, 2)
    pairs = heads_here // halves
    flat_queries = queries[0]
    weights = w_out
    if halves == 1:
        flat_queries = jnp.pad(flat_queries, ((0, 0), (0, LANES - HD)))
        weights = jnp.pad(weights, ((0, LANES - HD), (0, 0)))
    angle = (prefix_len + np.arange(MAXLEN)).astype(np.float32)[:, None] * rope[0][None, :]
    cosine = np.cos(angle).astype(np.float32)
    sine = (np.sin(angle) * rope[1][None, :]).astype(np.float32)
    row_ids = np.arange(tensors * kv_rows)
    inside = row_ids % kv_rows - block_rows
    key_slot = np.where(inside < 0, -1, row_ids // kv_rows * tok_dev + inside).astype(np.int32)
    parts = call(
        functools.partial(attend_kernel, pairs, halves),
        jax.ShapeDtypeStruct((slot_count, width), BF16),
        [SMEM, SMEM] + [VMEM] * 6,
        "attend_project",
        scratch=[pltpu.VMEM((slot_count, pairs * LANES), BF16)],
    )(
        lengths[0],
        sinks,
        jnp.asarray(cosine),
        jnp.asarray(sine),
        jnp.asarray(key_slot[None, :]),
        flat_queries,
        kv,
        weights,
    )
    parts = lax.all_to_all(
        parts.reshape(tensors, tok_dev, width), "tensor", split_axis=0, concat_axis=0, tiled=True
    )
    resid_out, normed = call(
        norm_kernel,
        [jax.ShapeDtypeStruct((tok_dev, width), BF16)] * 2,
        [VMEM] * 3,
        "sum_norm",
    )(parts, resid_in[0], mlp_gain[None, :])

    flat_rows = lax.all_gather(normed, "group", axis=0, tiled=True)
    top_count = routes.shape[2]
    pair_count = tok_dev * groups * top_count
    pair_ids = np.arange(pair_count)
    pair_row = pair_ids // top_count % groups * tok_dev + pair_ids // (groups * top_count)
    source = (pair_row[:, None] == np.arange(groups * tok_dev)[None, :]).astype(np.float32)
    earlier = (pair_ids[:, None] < pair_ids[None, :]).astype(np.float32)
    pieces_total = groups * tensors
    pieces_each = min(8, pieces_total // EXPERTS)
    copies = pieces_total // (EXPERTS * pieces_each)
    tensor_copies = tensors // copies
    slot_cap = pair_count // 16 // copies
    slot = np.arange(tensors * slot_cap)
    peer = slot // slot_cap
    expert = (me_group * tensor_copies + peer % tensor_copies) // pieces_each
    rank = slot % slot_cap * copies + peer // tensor_copies
    want = jnp.stack([expert.astype(jnp.int32), jnp.asarray(rank, jnp.int32)], axis=1)
    outgoing = call(
        dispatch_kernel,
        jax.ShapeDtypeStruct((tensors * slot_cap, width), BF16),
        [VMEM] * 5,
        "dispatch",
    )(
        routes.reshape(1, pair_count),
        want,
        jnp.asarray(earlier, BF16),
        jnp.asarray(source, BF16),
        flat_rows,
    )
    arrived = lax.all_to_all(
        outgoing.reshape(tensors, slot_cap, width),
        "tensor",
        split_axis=0,
        concat_axis=0,
        tiled=True,
    )
    piece = w_experts[0]
    columns = piece.shape[1]
    step = 384
    bounds = [(lo, min(lo + step, width)) for lo in range(0, width, step)]
    hidden = call(
        functools.partial(expert_kernel, bounds),
        jax.ShapeDtypeStruct((tensors * slot_cap, columns // 2), BF16),
        [VMEM, ANY],
        "experts",
        scratch=[
            pltpu.VMEM((width, columns), BF16),
            pltpu.VMEM((tensors * slot_cap, columns), F32),
            pltpu.SemaphoreType.DMA((len(bounds),)),
        ],
        limit=56,
    )(arrived.reshape(tensors * slot_cap, width), piece)
    return (resid_out[None], hidden.reshape(1, tensors, slot_cap, columns // 2))


def solution(mesh):
    placed = (
        P("group", "tensor", None),
        P("group", None, "tensor"),
        P("group", "tensor", None),
        P("group", "tensor", None),
        P("group", "tensor"),
        P("group", None),
        P("tensor"),
        P("tensor", None),
        P(),
        P("tensor", None, None),
        P(("group", "tensor"), None, None),
    )
    return jax.shard_map(
        local,
        mesh=mesh,
        in_specs=placed,
        out_specs=(P("group", "tensor", None), P(("group", "tensor"), None, None, None)),
        check_vma=False,
    )
```

time: 213 us -> 110 us (0.52)
  waiting for transfers between devices: 91.6 us -> 38.7 us
  blocking collectives: 71.8 us -> 29.8 us
  Pallas kernels: 0 us -> 22.6 us
  matrix products: 17.3 us -> 0 us
  between operations: 15.1 us -> 1.64 us
  starting transfers between devices: 0.08 us -> 12.2 us
  other arithmetic: 6.42 us -> 0.09 us
  local copies, waits for them, and re-layouts: 10.6 us -> 4.6 us
    reduce_scatter x1 -> x0, waiting for transfers between devices: 79.7 us -> none  [local(): lax.psum_scatter(jnp.dot(attended, w_out, preferred_element_type=jnp.floa...]
    all_gather x2 -> x1, blocking collectives: 47.8 us -> 1.93 us  [local(): flat_rows = lax.all_gather(normed, 'group', axis=0, tiled=True)]
    all_to_all x0 -> x2, waiting for transfers between devices: none -> 38.7 us  [the longest x1 32.1 us: local(): lax.all_to_all(parts.reshape(tensors, tok_dev, width), 'tensor', split_ax...]
    pallas_call x0 -> x5, Pallas kernels: none -> 22.6 us  [the longest x1 14.6 us: local(): call(functools.partial(expert_kernel, bounds), jax.ShapeDtypeStruct((tens...]
    dot_general x6 -> x0, matrix products: 17.3 us -> none  [the longest x1 13.1 us: local(): jnp.einsum('tcd,df->tcf', lax.all_to_all(outgoing_rows, 'tensor', split_a...]
    all_to_all x0 -> x2, starting transfers between devices: none -> 12.2 us  [the longest x1 8.31 us: local(): lax.all_to_all(owned, 'tensor', split_axis=0, concat_axis=0, tiled=True)]
    all_gather x1 -> x0, waiting for transfers between devices: 11.9 us -> none  [local(): piece_rows = lax.all_gather(flat_block, 'tensor', axis=0, tiled=True)]
    reshape x2 -> x1, local copies, waits for them, and re-layouts: 4.83 us -> 0.11 us  [local(): routes.reshape(1, pair_count)]
where the time goes in v1:
time: 110 us
  waiting for transfers between devices  38.7 us (35%)
  blocking collectives  29.8 us (27%)
  Pallas kernels  22.6 us (21%)
  starting transfers between devices  12.2 us (11%)
  local copies, waits for them, and re-layouts  4.6 us (4%)
  between operations  1.64 us (1%)
    all_to_all x1, waiting for transfers between devices, local(): lax.all_to_all(parts.reshape(tensors, tok_dev, width), 'tensor', split_ax...  32.1 us
    all_to_all x1, blocking collectives, local(): lax.all_to_all(outgoing.reshape(tensors, slot_cap, width), 'tensor', spli...  27.9 us
    pallas_call x1, Pallas kernels, local(): call(functools.partial(expert_kernel, bounds), jax.ShapeDtypeStruct((tens...  14.6 us
    all_to_all x1, starting transfers between devices, local(): lax.all_to_all(owned, 'tensor', split_axis=0, concat_axis=0, tiled=True)  8.31 us
    all_to_all x1, waiting for transfers between devices, local(): lax.all_to_all(owned, 'tensor', split_axis=0, concat_axis=0, tiled=True)  6.64 us
    pallas_call x1, Pallas kernels, local(): call(functools.partial(attend_kernel, pairs, halves), jax.ShapeDtypeStruc...  5.07 us
    unnamed x34, local copies, waits for them, and re-layouts  4.37 us
    all_to_all x1, starting transfers between devices, local(): lax.all_to_all(parts.reshape(tensors, tok_dev, width), 'tensor', split_ax...  3.85 us
  transfers between devices with their start and end apart: 2, of which 2 were waited for; matrix products, arithmetic and copies ran while one was open for 2% of the time, Pallas kernels for 0%

profile of v1, /device:TPU:0, one launch (start us, length us, event | category | flops | bytes accessed | tf_op | source)
XLA Modules:
  0.0 109.6 jit_solution(1112472656703454247)
XLA Ops:
  1.3 0.1 pad_add_fusion.1.place_ref
  1.4 0.0 copy-start.4
  1.4 0.8 copy-done.4
  2.2 0.0 copy-start.5
  2.2 0.8 copy-done.5
  3.0 0.0 copy-start.9
  3.0 0.7 copy-done.9
  3.6 1.4 %rotate_keys.1 = bf16[16,48,128]{2,1,0:T(8,128)(2,1)} custom-call(s32[2]{0:T(128)S(1)} %pad_add_fusion.1.place_ref, f32[2,128]{1,0:T(2,128)S(1)} %copy-done.9, bf16[16,1024]{1,0:T(8,128)(2,1)S(1)} %bitcast.21, bf16[32,1024]{1,0:T(8,128)(2,1)S(1)} %bitcast.20), custom_call_target="tpu_custom_call" | custom-call | tf_op jit(solution)/shard_map/rotate_keys/pallas_call | solution.py:199
  5.1 8.3 %all-to-all-start = ((bf16[16,48,128]{2,1,0:T(8,128)(2,1)}), bf16[16,48,128]{2,1,0:T(8,128)(2,1)S(1)}, u32[]{:S(2)}, u32[]{:S(2)}) async-start(bf16[16,48,128]{2,1,0:T(8,128)(2,1)} %rotate_keys.1), calls=%async_computation | async-start | bytes 393216 | tf_op jit(solution)/shard_map/all_to_all | solution.py:205
  13.4 0.0 copy-start
  13.4 0.0 copy-start.2
  13.4 0.0 copy-start.3
  13.4 0.0 copy-start.8
  13.4 0.0 copy-start.10
  13.5 0.0 copy-start.11
  13.5 1.9 %copy.27.w_ref = bf16[256,2880]{1,0:T(8,128)(2,1)S(1)} copy(bf16[256,2880]{0,1:T(8,128)(2,1)} %param.26) | data formatting | bytes 2949120 | tf_op args[7]
  15.4 6.6 %all-to-all-done = bf16[16,48,128]{2,1,0:T(8,128)(2,1)S(1)} async-done(((bf16[16,48,128]{2,1,0:T(8,128)(2,1)}), bf16[16,48,128]{2,1,0:T(8,128)(2,1)S(1)}, u32[]{:S(2)}, u32[]{:S(2)}) %all-to-all-start) | async-done | bytes 196640 | tf_op jit(solution)/shard_map/all_to_all | solution.py:205
  22.0 0.0 copy-done
  22.0 0.0 copy-done.2
  22.0 0.0 copy-done.3
  22.0 0.0 copy-done.8
  22.1 0.0 copy-done.10
  22.1 0.0 copy-done.11
  22.1 5.1 %attend_project.1 = bf16[256,2880]{1,0:T(8,128)(2,1)} custom-call(s32[2]{0:T(128)S(1)} %bitcast.22, f32[4]{0:T(128)S(1)} %copy-done.11, f32[128,128]{1,0:T(8,128)S(1)} %copy-done.2, f32[128,128]{1,0:T(8,128)S(1)} %copy-done.3, s32[1,768]{1,0:T(1,128)S(1)} %copy-done.8, bf16[256,256]{1,0:T(8,128)(2,1)S(1)} %bitcast.18, bf16[768,128]{1,0:T(8,128)(2,1)S(1)} %bitcast.17, ...), custom_call_target="tpu_custom_call" | custom-call | tf_op jit(solution)/shard_map/attend_project/pallas_call | solution.py:221
  27.1 0.0 copy-start.12
  27.2 0.0 copy-start.15
  27.2 0.0 copy-start.14
  27.2 0.0 copy-start.13
  27.2 0.0 copy-start.1
  27.2 3.8 %all-to-all-start.1 = ((bf16[16,16,2880]{2,1,0:T(8,128)(2,1)}), bf16[16,16,2880]{2,1,0:T(8,128)(2,1)S(1)}, u32[]{:S(2)}, u32[]{:S(2)}) async-start(bf16[16,16,2880]{2,1,0:T(8,128)(2,1)} %bitcast.7), calls=%async_computation.1 | async-start | bytes 3014656 | tf_op jit(solution)/shard_map/all_to_all | solution.py:237
  31.0 0.0 copy-done.12
  31.0 0.0 copy-start.6
  31.1 0.0 copy-start.7
  31.1 0.0 copy-done.15
  31.1 0.0 copy-done.14
  31.1 0.1 copy.29.want_ref
  31.2 0.0 copy-done.13
  31.3 0.1 copy.28
  31.3 0.1 reshape.27.names_ref
  31.5 32.1 %all-to-all-done.1.parts_ref = bf16[16,16,2880]{2,1,0:T(8,128)(2,1)S(1)} async-done(((bf16[16,16,2880]{2,1,0:T(8,128)(2,1)}), bf16[16,16,2880]{2,1,0:T(8,128)(2,1)S(1)}, u32[]{:S(2)}, u32[]{:S(2)}) %all-to-all-start.1) | async-done | bytes 1474592 | tf_op jit(solution)/shard_map/all_to_all | solution.py:237
  63.6 0.0 copy-done.1
  63.6 0.9 sum_norm.1
  64.5 1.9 %all_gather.3.rows_ref = bf16[32,2880]{1,0:T(8,128)(2,1)S(1)} all-gather(bf16[16,2880]{1,0:T(8,128)(2,1)S(1)} %get-tuple-element.5), channel_id=1, replica_groups=mesh['group'=2,'tensor'=16] {'group'}, dimensions={0}, use_global_device_ids=true | all-gather | bytes 276480 | tf_op jit(solution)/shard_map/all_gather | solution.py:247
  66.4 0.0 copy-done.6
  66.4 0.0 copy-done.7
  66.4 0.6 dispatch.1
  67.0 27.9 %all_to_all.15 = bf16[16,8,2880]{2,1,0:T(8,128)(2,1)} all-to-all(bf16[16,8,2880]{2,1,0:T(8,128)(2,1)S(1)} %bitcast.16), channel_id=1, replica_groups=mesh['group'=2,'tensor'=16] {'tensor'}, dimensions={0} | all-to-all | bytes 1474560 | tf_op jit(solution)/shard_map/all_to_all | solution.py:276
  94.9 14.6 %experts.1 = bf16[128,2880]{1,0:T(8,128)(2,1)} custom-call(bf16[128,2880]{1,0:T(8,128)(2,1)} %bitcast.24, bf16[2880,5760]{1,0:T(8,128)(2,1)} %bitcast.23), custom_call_target="tpu_custom_call" | custom-call | tf_op jit(solution)/shard_map/experts/pallas_call | solution.py:287
  (3 shorter events, 0.0 us)
Async XLA Ops:
  1.4 0.8 copy-start.4
  2.2 0.8 copy-start.5
  3.0 0.7 copy-start.9
  5.1 17.0 %all-to-all-start = ((bf16[16,48,128]{2,1,0:T(8,128)(2,1)}), bf16[16,48,128]{2,1,0:T(8,128)(2,1)S(1)}, u32[]{:S(2)}, u32[]{:S(2)}) async-start(bf16[16,48,128]{2,1,0:T(8,128)(2,1)} %rotate_keys.1), calls=%async_computation | async-start | bytes 393216 | tf_op jit(solution)/shard_map/all_to_all | solution.py:205
  13.4 8.6 %copy-start = (bf16[1,256,256]{2,1,0:T(8,128)(2,1)S(1)}, bf16[1,256,256]{2,1,0:T(8,128)(2,1)}, u32[]{:S(2)}) copy-start(bf16[1,256,256]{2,1,0:T(8,128)(2,1)} %param.20) | copy-start | bytes 393220
  13.4 8.6 %copy-start.2 = (f32[128,128]{1,0:T(8,128)S(1)}, f32[128,128]{1,0:T(8,128)}, u32[]{:S(2)}) copy-start(f32[128,128]{1,0:T(8,128)} %constant.42.clone.cos_ref) | copy-start | bytes 196612
  13.4 8.6 %copy-start.3 = (f32[128,128]{1,0:T(8,128)S(1)}, f32[128,128]{1,0:T(8,128)}, u32[]{:S(2)}) copy-start(f32[128,128]{1,0:T(8,128)} %constant.43.clone.sin_ref) | copy-start | bytes 196612
  13.4 8.6 %copy-start.8 = (s32[1,768]{1,0:T(1,128)S(1)}, s32[1,768]{1,0:T(1,128)}, u32[]{:S(2)}) copy-start(s32[1,768]{1,0:T(1,128)} %constant.44.clone.slot_ref) | copy-start | bytes 9220
  13.4 8.6 %copy-start.10 = (s32[1,2]{1,0:T(1,128)S(1)}, s32[1,2]{1,0:T(1,128)}, u32[]{:S(2)}) copy-start(s32[1,2]{1,0:T(1,128)} %param.24) | copy-start | bytes 28
  13.5 8.6 %copy-start.11 = (f32[4]{0:T(128)S(1)}, f32[4]{0:T(128)}, u32[]{:S(2)}) copy-start(f32[4]{0:T(128)} %sink_ref.1) | copy-start | bytes 52
  27.1 3.9 %copy-start.12 = (f32[2880]{0:T(1024)S(1)}, f32[2880]{0:T(1024)}, u32[]{:S(2)}) copy-start(f32[2880]{0:T(1024)} %param.27) | copy-start | bytes 34564
  27.2 3.9 %copy-start.15 = (s32[128]{0:T(128)S(1)}, s32[128]{0:T(128)}, u32[]{:S(2)}) copy-start(s32[128]{0:T(128)} %constant.45.clone) | copy-start | bytes 1540
  27.2 4.0 %copy-start.14 = (s32[128,1]{0,1:T(1,128)S(1)}, s32[128,1]{0,1:T(1,128)}, u32[]{:S(2)}) copy-start(s32[128,1]{0,1:T(1,128)} %constant.57) | copy-start | bytes 1540
  27.2 4.1 %copy-start.13 = (s32[16,2,4]{0,2,1:T(4,128)S(1)}, s32[16,2,4]{0,2,1:T(4,128)}, u32[]{:S(2)}) copy-start(s32[16,2,4]{0,2,1:T(4,128)} %param.28) | copy-start | bytes 1540
  27.2 36.4 %copy-start.1 = (bf16[1,16,2880]{2,1,0:T(8,128)(2,1)S(1)}, bf16[1,16,2880]{2,1,0:T(8,128)(2,1)}, u32[]{:S(2)}) copy-start(bf16[1,16,2880]{2,1,0:T(8,128)(2,1)} %param.19) | copy-start | bytes 276484
  27.2 36.4 %all-to-all-start.1 = ((bf16[16,16,2880]{2,1,0:T(8,128)(2,1)}), bf16[16,16,2880]{2,1,0:T(8,128)(2,1)S(1)}, u32[]{:S(2)}, u32[]{:S(2)}) async-start(bf16[16,16,2880]{2,1,0:T(8,128)(2,1)} %bitcast.7), calls=%async_computation.1 | async-start | bytes 3014656 | tf_op jit(solution)/shard_map/all_to_all | solution.py:237
  31.0 35.3 %copy-start.6 = (bf16[128,128]{1,0:T(8,128)(2,1)S(1)}, bf16[128,128]{1,0:T(8,128)(2,1)}, u32[]{:S(2)}) copy-start(bf16[128,128]{1,0:T(8,128)(2,1)} %constant.47.clone.earlier_ref) | copy-start | bytes 98308
  31.1 35.3 %copy-start.7 = (bf16[128,32]{1,0:T(8,128)(2,1)S(1)}, bf16[128,32]{1,0:T(8,128)(2,1)}, u32[]{:S(2)}) copy-start(bf16[128,32]{1,0:T(8,128)(2,1)} %constant.48.clone.source_ref) | copy-start | bytes 24580

commit v2 on v1

v2 whole, which is shorter than its diff:
```python
import functools
import math

import jax
import jax.numpy as jnp
import numpy as np
from jax import lax
from jax.experimental import pallas as pl
from jax.experimental.pallas import tpu as pltpu
from jax.sharding import PartitionSpec as P

HEADS = 64
KVH = 8
HD = 64
EXPERTS = 32
MAXLEN = 128
LANES = 128
F32 = jnp.float32
BF16 = jnp.bfloat16
VMEM = pl.BlockSpec(memory_space=pltpu.VMEM)
SMEM = pl.BlockSpec(memory_space=pltpu.SMEM)
ANY = pl.BlockSpec(memory_space=pl.ANY)
PLANE = 4


def call(kernel, outs, specs, name, scratch=(), limit=12, moved=0, space=VMEM):
    single = not isinstance(outs, (list, tuple))
    return pl.pallas_call(
        kernel,
        out_shape=outs,
        in_specs=list(specs),
        out_specs=space if single else [space] * len(outs),
        scratch_shapes=list(scratch),
        name=name,
        compiler_params=pltpu.CompilerParams(vmem_limit_bytes=limit * 1024 * 1024),
        cost_estimate=pl.CostEstimate(flops=0, bytes_accessed=moved, transcendentals=0),
    )


def log2(number):
    assert number & (number - 1) == 0
    return number.bit_length() - 1


def rope_rows():
    lane = np.arange(LANES) % HD
    frequency = np.power(np.float32(150000.0), -2.0 * (lane % (HD // 2)) / HD).astype(np.float32)
    sign = np.where(lane < HD // 2, -1.0, 1.0).astype(np.float32)
    return np.stack([frequency, sign])


def partner(values):
    lane = lax.broadcasted_iota(jnp.int32, values.shape, 1)
    ahead = pltpu.roll(values, LANES - HD // 2, 1)
    behind = pltpu.roll(values, HD // 2, 1)
    return jnp.where(lane % HD < HD // 2, ahead, behind)


def keys_kernel(heads_here, tensors, block_ref, suffix_ref, prefix_ref, out_ref):
    block_rows = prefix_ref.shape[0]
    tok_dev = suffix_ref.shape[0]
    prefix_len = block_rows * tensors
    half = KVH * HD
    share = HEADS // KVH

    def part(ref, first, low):
        rows = ref.shape[0]
        row = lax.broadcasted_iota(jnp.int32, (rows, LANES), 0) + first
        lane = lax.broadcasted_iota(jnp.int32, (1, LANES), 1) & (HD - 1)
        exponent = (lane & (HD // 2 - 1)).astype(F32) * (-2.0 * math.log(150000.0) / HD)
        angle = row.astype(F32) * jnp.exp(exponent)
        cosine = jnp.cos(angle)
        sine = jnp.sin(angle) * jnp.where(lane < HD // 2, -1.0, 1.0)
        left = lax.broadcasted_iota(jnp.int32, (rows, LANES), 1) < HD
        made = {}
        for peer in range(tensors):
            one = peer * heads_here // share
            two = (peer ^ 2) * heads_here // share
            if (one, two) not in made:
                pair = one // 2
                keys = ref[:, pair * LANES : (pair + 1) * LANES].astype(F32)
                vals = ref[:, half + pair * LANES : half + (pair + 1) * LANES].astype(F32)
                turned = keys * cosine + partner(keys) * sine

                def ordered(values):
                    swapped = pltpu.roll(values, HD, 1)
                    first_half = values if one % 2 == 0 else swapped
                    second_half = values if two % 2 == 1 else swapped
                    return jnp.where(left, first_half, second_half).astype(BF16)

                made[one, two] = ordered(turned), ordered(vals)
            out_ref[peer, low : low + rows, :LANES] = made[one, two][0]
            out_ref[peer, low : low + rows, LANES:] = made[one, two][1]

    part(prefix_ref, block_ref[0, 0] * block_rows, 0)
    part(suffix_ref, prefix_len + lax.axis_index("tensor") * tok_dev % MAXLEN, block_rows)


def queries_kernel(tok_dev, sink_ref, turn_ref, q_ref, *out_refs):
    me = lax.axis_index("tensor")
    planes = q_ref.shape[0] // tok_dev // PLANE
    width = q_ref.shape[1]
    lane = lax.broadcasted_iota(jnp.int32, (16, width), 1)
    row = lax.broadcasted_iota(jnp.int32, (16, width), 0)
    sink = jnp.zeros((16, width), F32)
    for head in range(width // HD):
        sink = jnp.where((lane >= head * HD) & (lane < head * HD + HD), sink_ref[head], sink)
    high = sink.astype(BF16).astype(F32)
    middle = (sink - high).astype(BF16).astype(F32)
    low = sink - high - middle
    terms = jnp.where(row == 0, high, jnp.where(row == 1, middle, jnp.where(row == 2, low, 0.0)))
    for peer in range(PLANE):
        for plane in range(planes):
            block = me ^ (plane * PLANE + peer)
            rows = pl.ds(pl.multiple_of(block * tok_dev, tok_dev), tok_dev)
            turn = block * tok_dev % MAXLEN
            cosine = turn_ref[pl.ds(pl.multiple_of(turn, tok_dev), tok_dev), :]
            sine = turn_ref[pl.ds(pl.multiple_of(turn + MAXLEN, tok_dev), tok_dev), :]
            for pair in range(width // LANES):
                span = slice(pair * LANES, (pair + 1) * LANES)
                query = q_ref[rows, span].astype(F32)
                turned = query * cosine + partner(query) * sine
                out_refs[peer][plane * tok_dev : (plane + 1) * tok_dev, span] = turned.astype(BF16)
        out_refs[peer][planes * tok_dev : planes * tok_dev + 16, :] = terms.astype(BF16)


def rotate_kernel(turn_ref, q_ref, out_ref):
    for req in range(q_ref.shape[0] // MAXLEN):
        rows = slice(req * MAXLEN, (req + 1) * MAXLEN)
        query = q_ref[rows, :].astype(F32)
        turned = query * turn_ref[:MAXLEN] + partner(query) * turn_ref[MAXLEN:]
        out_ref[rows, :] = turned.astype(BF16)


def attend_kernel(blocks, tok_dev, kv_rows, len_ref, *refs):
    q_refs, kv_ref, resid_refs, out_ref = refs[:blocks], refs[blocks], refs[blocks + 1 : -1], refs[-1]
    rows = q_refs[0].shape[0] - 16
    inner = lax.axis_index("tensor") & (PLANE - 1)
    plane = lax.axis_index("tensor") >> log2(PLANE)
    low = lax.broadcasted_iota(jnp.int32, (kv_ref.shape[0], LANES), 1) < HD

    def doubled(values):
        swapped = pltpu.roll(values, HD, 1)
        return (
            jnp.where(low, values, swapped).astype(BF16),
            jnp.where(low, swapped, values).astype(BF16),
        )

    keys = doubled(kv_ref[:, :LANES].astype(F32))
    vals = doubled(kv_ref[:, LANES:].astype(F32))
    row = lax.broadcasted_iota(jnp.int32, (2 * rows, 1), 0)
    row = row & (rows - 1)
    shift = tok_dev.bit_length() - 1
    slot = (((row >> shift) ^ plane) * PLANE + inner) * tok_dev + (row & (tok_dev - 1))
    request = slot >> (MAXLEN.bit_length() - 1)
    length = jnp.zeros_like(slot)
    for number in range(len_ref.shape[1]):
        length = jnp.where(request == number, len_ref[0, number], length)
    base = request * MAXLEN
    last = jnp.minimum(slot, base + length - 1)
    key_row = lax.broadcasted_iota(jnp.int32, (1, kv_ref.shape[0]), 1)
    source = jnp.floor((key_row.astype(F32) + 0.5) * (1.0 / kv_rows)).astype(jnp.int32)
    inside = key_row - source * kv_rows - (kv_rows - tok_dev)
    key_slot = jnp.where(inside < 0, -1, source * tok_dev + inside)
    visible = (key_slot < 0) | ((key_slot >= base) & (key_slot <= last))
    left = lax.broadcasted_iota(jnp.int32, (rows, LANES), 1) < HD
    for block in range(blocks):
        for pair in range(2):
            half = block // 2 if blocks == PLANE else pair
            span = slice(pair * LANES, (pair + 1) * LANES)
            query = q_refs[block][:rows, span].astype(F32) * 0.125
            stack = jnp.concatenate(
                [jnp.where(left, query, 0.0), jnp.where(left, 0.0, query)], axis=0
            ).astype(BF16)
            scores = lax.dot_general(
                stack, keys[half], (((1,), (1,)), ((), ())), preferred_element_type=F32
            )
            scores = jnp.where(visible, scores, -1e30)
            terms = q_refs[block][rows : rows + 16, span].astype(F32)
            sinks = terms[0:1] + terms[1:2] + terms[2:3]
            sink = jnp.concatenate(
                [
                    jnp.broadcast_to(sinks[:, 0:1], (rows, 1)),
                    jnp.broadcast_to(sinks[:, HD : HD + 1], (rows, 1)),
                ],
                axis=0,
            )
            top = jnp.maximum(jnp.max(scores, axis=1, keepdims=True), sink)
            weights = jnp.exp(scores - top)
            total = jnp.sum(weights, axis=1, keepdims=True) + jnp.exp(sink - top)
            got = jnp.dot(weights.astype(BF16), vals[half], preferred_element_type=F32) / total
            at = block * 2 * LANES + pair * LANES
            out_ref[:rows, at : at + LANES] = jnp.where(left, got[:rows], got[rows:]).astype(BF16)
    for resid_ref in resid_refs:
        step = out_ref.shape[1]
        for number, first in enumerate(range(0, resid_ref.shape[1], step)):
            size = min(step, resid_ref.shape[1] - first)
            at = rows + number * tok_dev
            out_ref[at : at + tok_dev, :size] = resid_ref[:, first : first + size]


def project_kernel(tok_dev, groups, att_ref, *refs):
    w_refs, out_refs = refs[: PLANE + 1], refs[PLANE + 1 :]
    depth = w_refs[0].shape[1]
    slots = att_ref.shape[0] // groups
    taken = out_refs[0].shape[0] * len(out_refs) // groups
    rows = jnp.concatenate(
        [att_ref[group * slots : group * slots + taken, :] for group in range(groups)], axis=0
    )

    def times(peer, w_ref):
        return lax.dot_general(
            rows[:, peer * depth : (peer + 1) * depth],
            w_ref[...],
            (((1,), (1,)), ((), ())),
            preferred_element_type=F32,
        )

    far = jnp.concatenate([times(3, w_refs[3]), times(3, w_refs[4])], axis=1)
    whole = times(0, w_refs[0]) + times(1, w_refs[1]) + times(2, w_refs[2]) + far
    slots = taken
    if len(out_refs) == 1:
        out_refs[0][...] = whole
        return
    for plane, out_ref in enumerate(out_refs):
        for group in range(groups):
            first = group * slots + plane * tok_dev
            out_ref[group * tok_dev : (group + 1) * tok_dev, :] = whole[
                first : first + tok_dev
            ].astype(out_ref.dtype)


def split_kernel(top_ref, bottom_ref, top_out, bottom_out, sems):
    first, last = top_out.shape[0], bottom_out.shape[0]
    copies = [
        pltpu.make_async_copy(top_ref.at[pl.ds(0, first)], top_out, sems.at[0]),
        pltpu.make_async_copy(bottom_ref.at[pl.ds(first, last)], bottom_out, sems.at[1]),
    ]
    for copy in copies:
        copy.start()
    for copy in copies:
        copy.wait()


def load_kernel(w_ref, out_ref, sem):
    copy = pltpu.make_async_copy(w_ref.at[pl.ds(0, out_ref.shape[0])], out_ref, sem)
    copy.start()
    copy.wait()


def sum_kernel(*refs):
    total = refs[0][...].astype(F32)
    for ref in refs[1:-1]:
        total = total + ref[...].astype(F32)
    refs[-1][...] = total


def dispatch_kernel(
    groups,
    slot_cap,
    tensor_copies,
    pieces_each,
    copies,
    names_ref,
    earlier_ref,
    source_ref,
    gain_ref,
    resid_ref,
    sums_ref,
    resid_out_ref,
    out_ref,
    held,
):
    rows = held.shape[0]
    tok_dev = rows // groups
    width = sums_ref.shape[1]
    for part in range(groups):
        held[:, part * width : (part + 1) * width] = sums_ref[part * rows : (part + 1) * rows, :]
    if resid_ref.shape == held.shape:
        resid = resid_ref[...].astype(F32)
    else:
        each = resid_ref.shape[0] // groups
        step = resid_ref.shape[1]
        count = -(-held.shape[1] // step)
        first = each - count * tok_dev
        resid = jnp.concatenate(
            [
                jnp.concatenate(
                    [
                        resid_ref[
                            group * each + first + number * tok_dev :
                            group * each + first + (number + 1) * tok_dev,
                            : min(step, held.shape[1] - number * step),
                        ].astype(F32)
                        for number in range(count)
                    ],
                    axis=1,
                )
                for group in range(groups)
            ],
            axis=0,
        )
    rounded = (resid + held[...]).astype(BF16)
    wide = rounded.astype(F32)
    own = wide[:tok_dev]
    me_group = lax.axis_index("group")
    for group in range(1, groups):
        own = jnp.where(
            me_group == group, wide[group * tok_dev : (group + 1) * tok_dev], own
        )
    resid_out_ref[...] = own.astype(BF16)
    scale = lax.rsqrt(jnp.mean(wide * wide, axis=1, keepdims=True) + 1e-05)
    normed = (wide * scale * gain_ref[...]).astype(BF16)

    pairs = names_ref.shape[1]
    expert = lax.broadcasted_iota(jnp.int32, (EXPERTS, pairs), 0)
    onehot = (names_ref[...] == expert).astype(F32)
    rank = jnp.dot(onehot.astype(BF16), earlier_ref[...], preferred_element_type=F32)
    pair_rank = jnp.sum(rank * onehot, axis=0, keepdims=True).astype(jnp.int32)
    slot = lax.broadcasted_iota(jnp.int32, (out_ref.shape[0], 1), 0)
    peer = slot >> log2(slot_cap)
    piece = me_group * tensor_copies + (peer & (tensor_copies - 1))
    wanted_rank = (slot & (slot_cap - 1)) * copies + (peer >> log2(tensor_copies))
    picked = (names_ref[...] == piece >> log2(pieces_each)) & (pair_rank == wanted_rank)
    chosen = jnp.dot(picked.astype(F32).astype(BF16), source_ref[...], preferred_element_type=F32)
    out_ref[...] = jnp.dot(chosen.astype(BF16), normed, preferred_element_type=F32).astype(BF16)


def expert_kernel(bounds, rows_ref, early_ref, w_ref, out_ref, held, total, sems):
    start = early_ref.shape[0]
    copies = [
        pltpu.make_async_copy(
            w_ref.at[pl.ds(lo, hi - lo)], held.at[pl.ds(lo - start, hi - lo)], sems.at[k]
        )
        for k, (lo, hi) in enumerate(bounds)
    ]
    for copy in copies:
        copy.start()
    total[...] = jnp.dot(rows_ref[:, :start], early_ref[...], preferred_element_type=F32)
    for k, (lo, hi) in enumerate(bounds):
        copies[k].wait()
        total[...] += jnp.dot(
            rows_ref[:, lo:hi], held[lo - start : hi - start, :], preferred_element_type=F32
        )
    width = out_ref.shape[1]
    gate = jnp.minimum(total[:, :width], 7.0)
    up = jnp.clip(total[:, width : 2 * width], -7.0, 7.0)
    out_ref[...] = ((up + 1.0) * gate / (1.0 + jnp.exp(-1.702 * gate))).astype(BF16)


def local(
    resid_in,
    queries,
    suffix_kv,
    prefix_kv,
    block_map,
    lengths,
    sinks,
    w_out,
    mlp_gain,
    routes,
    w_experts,
):
    groups = lax.axis_size("group")
    tensors = lax.axis_size("tensor")
    me_group = lax.axis_index("group")
    me_tensor = lax.axis_index("tensor")
    block_rows = prefix_kv.shape[1]
    prefix_len = block_rows * tensors
    slot_count = queries.shape[1]
    heads_here = queries.shape[2] // HD
    tok_dev = resid_in.shape[1]
    width = resid_in.shape[2]
    planes = tensors // PLANE
    slots_here = planes * tok_dev
    aligned = tok_dev % 16 == 0 and heads_here % 2 == 0

    def swap(values, bits):
        return lax.ppermute(values, "tensor", [(i, i ^ bits) for i in range(tensors)])

    columns_here = width // groups
    cut = columns_here // 2
    held = lax.dynamic_slice_in_dim(w_out.T, me_group * columns_here, columns_here, 0)
    beside, across = swap(held, 1), swap(held, 2)

    kv_rows = block_rows + tok_dev
    rope = rope_rows()
    angle = (prefix_len + np.arange(MAXLEN)).astype(np.float32)[:, None] * rope[0][None, :]
    turns = np.concatenate([np.cos(angle), np.sin(angle) * rope[1][None, :]], axis=0)
    turns = jnp.asarray(turns.astype(np.float32))
    query_cols = heads_here * HD
    top_count = routes.shape[2]
    pair_count = tok_dev * groups * top_count

    def exchange(suffix, prefix, mine, sink_logits, block, named, gains):
        owned = call(
            functools.partial(keys_kernel, heads_here, tensors),
            jax.ShapeDtypeStruct((tensors, kv_rows, 2 * LANES), BF16),
            [SMEM, VMEM, VMEM],
            "rotate_keys",
        )(block, suffix, prefix)
        kv = lax.all_to_all(owned, "tensor", split_axis=0, concat_axis=0, tiled=True)
        if aligned:
            sent = call(
                functools.partial(queries_kernel, tok_dev),
                [jax.ShapeDtypeStruct((slots_here + 16, query_cols), BF16)] * PLANE,
                [SMEM, VMEM, VMEM],
                "rotate_queries",
            )(sink_logits, turns, mine)
        else:
            padded = jnp.pad(mine, ((0, 0), (0, LANES - query_cols)))
            turned = call(
                rotate_kernel,
                jax.ShapeDtypeStruct(padded.shape, BF16),
                [VMEM, VMEM],
                "rotate_queries",
            )(turns, padded)[:, :query_cols]
            turned = turned.reshape(tensors, tok_dev, query_cols)
            turned = jnp.take(turned, me_tensor ^ jnp.arange(tensors), axis=0)
            turned = turned.reshape(planes, PLANE, tok_dev, query_cols)
            spread = jnp.repeat(sink_logits, HD)
            high = lax.reduce_precision(spread, 8, 7)
            middle = lax.reduce_precision(spread - high, 8, 7)
            terms = jnp.pad(jnp.stack([high, middle, spread - high - middle]), ((0, 13), (0, 0)))
            sent = [
                jnp.concatenate(
                    [turned[:, peer].reshape(slots_here, query_cols), terms.astype(BF16)], axis=0
                )
                for peer in range(PLANE)
            ]
        moved = [swap(sent[peer], peer) for peer in range(1, PLANE)]
        return (kv, named.reshape(1, pair_count), gains[None, :], sent[0], *moved)

    def nothing(*operands):
        shape = (slots_here + 16, query_cols)
        kv = jnp.zeros((tensors, kv_rows, 2 * LANES), BF16)
        names, gain = jnp.zeros((1, pair_count), jnp.int32), jnp.zeros((1, width), F32)
        return (kv, names, gain, *(jnp.zeros(shape, BF16) for _ in range(PLANE)))

    kv, names, gain, *received = lax.cond(
        lengths[0, 0] > 0,
        exchange,
        nothing,
        suffix_kv[0],
        prefix_kv[0],
        queries[0],
        sinks,
        block_map,
        routes,
        mlp_gain,
    )
    kv, beside, across = lax.optimization_barrier((kv, beside, across))
    halves = call(
        split_kernel,
        [
            jax.ShapeDtypeStruct((cut, held.shape[1]), BF16),
            jax.ShapeDtypeStruct((columns_here - cut, held.shape[1]), BF16),
        ],
        [ANY, ANY],
        "split",
        scratch=[pltpu.SemaphoreType.DMA((2,))],
        limit=2,
        space=ANY,
    )(beside, across)
    far = [swap(halves[0], 2), swap(halves[1], 1)]
    projections = [held, beside, across, *far]
    kv = kv.reshape(tensors * kv_rows, 2 * LANES)
    if not aligned:
        received = [jnp.concatenate(received, axis=1)]

    packed = [resid_in[0]] if aligned else []
    extra = -(-width // (PLANE * query_cols)) * tok_dev if aligned else 0
    attended = call(
        functools.partial(attend_kernel, len(received), tok_dev, kv_rows),
        jax.ShapeDtypeStruct((slots_here + extra, PLANE * query_cols), BF16),
        [SMEM] + [VMEM] * (1 + len(received) + int(aligned)),
        "attend",
    )(lengths, *received, kv, *packed)

    attended = lax.all_gather(attended, "group", axis=0, tiled=True)
    rows_here = groups * tok_dev
    if aligned:
        outs = [
            jax.ShapeDtypeStruct((rows_here, columns_here), F32 if plane == 0 else BF16)
            for plane in range(planes)
        ]
    else:
        outs = [jax.ShapeDtypeStruct((groups * slots_here, columns_here), F32)]
    parts = call(
        functools.partial(project_kernel, tok_dev, groups),
        outs,
        [VMEM] * (2 + PLANE),
        "project",
    )(attended, *projections)
    if not aligned:
        split = parts[0].reshape(groups, planes, tok_dev, columns_here)
        parts = [split[:, plane].reshape(rows_here, columns_here) for plane in range(planes)]
        parts = [parts[0]] + [part.astype(BF16) for part in parts[1:]]
    pair_ids = np.arange(pair_count)
    pair_row = pair_ids // top_count % groups * tok_dev + pair_ids // (groups * top_count)
    source = (pair_row[:, None] == np.arange(groups * tok_dev)[None, :]).astype(np.float32)
    earlier = (pair_ids[:, None] < pair_ids[None, :]).astype(np.float32)
    pieces_total = groups * tensors
    pieces_each = min(8, pieces_total // EXPERTS)
    copies = pieces_total // (EXPERTS * pieces_each)
    tensor_copies = tensors // copies
    slot_cap = pair_count // 16 // copies
    resid_all = attended if aligned else lax.all_gather(resid_in[0], "group", axis=0, tiled=True)
    *parts, piece = lax.optimization_barrier((*parts, w_experts[0]))
    arrived = [parts[0]] + [swap(parts[plane], plane * PLANE) for plane in range(1, planes)]
    columns = piece.shape[1]
    step = 384
    early_rows = 5 * step
    early = call(
        load_kernel,
        jax.ShapeDtypeStruct((early_rows, columns), BF16),
        [ANY],
        "load_expert",
        scratch=[pltpu.SemaphoreType.DMA],
        limit=12,
        moved=2 * early_rows * columns * 2,
    )(piece)
    *arrived, early = lax.optimization_barrier((*arrived, early))
    sums = call(
        sum_kernel,
        jax.ShapeDtypeStruct((rows_here, columns_here), F32),
        [VMEM] * planes,
        "sum_planes",
    )(*arrived)
    sums = lax.all_gather(sums, "group", axis=0, tiled=True)

    resid_out, outgoing = call(
        functools.partial(
            dispatch_kernel, groups, slot_cap, tensor_copies, pieces_each, copies
        ),
        [
            jax.ShapeDtypeStruct((tok_dev, width), BF16),
            jax.ShapeDtypeStruct((tensors * slot_cap, width), BF16),
        ],
        [VMEM] * 6,
        "norm_dispatch",
        scratch=[pltpu.VMEM((rows_here, width), F32)],
    )(
        names,
        jnp.asarray(earlier, BF16),
        jnp.asarray(source, BF16),
        gain,
        resid_all,
        sums,
    )
    rows = lax.all_to_all(
        outgoing.reshape(tensors, slot_cap, width),
        "tensor",
        split_axis=0,
        concat_axis=0,
        tiled=True,
    )
    bounds = [(lo, min(lo + step, width)) for lo in range(early_rows, width, step)]
    hidden = call(
        functools.partial(expert_kernel, bounds),
        jax.ShapeDtypeStruct((tensors * slot_cap, columns // 2), BF16),
        [VMEM, VMEM, ANY],
        "experts",
        scratch=[
            pltpu.VMEM((width - early_rows, columns), BF16),
            pltpu.VMEM((tensors * slot_cap, columns), F32),
            pltpu.SemaphoreType.DMA((len(bounds),)),
        ],
        limit=24,
    )(rows.reshape(tensors * slot_cap, width), early, piece)
    return (resid_out[None], hidden.reshape(1, tensors, slot_cap, columns // 2))


def solution(mesh):
    placed = (
        P("group", "tensor", None),
        P("group", None, "tensor"),
        P("group", "tensor", None),
        P("group", "tensor", None),
        P("group", "tensor"),
        P("group", None),
        P("tensor"),
        P("tensor", None),
        P(),
        P("tensor", None, None),
        P(("group", "tensor"), None, None),
    )
    return jax.shard_map(
        local,
        mesh=mesh,
        in_specs=placed,
        out_specs=(P("group", "tensor", None), P(("group", "tensor"), None, None, None)),
        check_vma=False,
    )
```

time: 110 us -> 93.3 us (0.85)
  waiting for transfers between devices: 38.7 us -> 7.56 us
  starting transfers between devices: 12.2 us -> 20.8 us
  Pallas kernels: 22.6 us -> 27.9 us
    all_to_all x2 -> x1, waiting for transfers between devices: 38.7 us -> 0.01 us  [exchange(): lax.all_to_all(owned, 'tensor', split_axis=0, concat_axis=0, tiled=True)]
    ppermute x0 -> x10, starting transfers between devices: none -> 15.8 us  [swap(): lax.ppermute(values, 'tensor', [(i, i ^ bits) for i in range(tensors)])]
    pallas_call x4 -> x8, Pallas kernels: 8.01 us -> 19.4 us  [the longest x1 7.3 us: local(): call(load_kernel, jax.ShapeDtypeStruct((early_rows, columns), BF16), [ANY...]
    ppermute x0 -> x10, waiting for transfers between devices: none -> 7.56 us  [swap(): lax.ppermute(values, 'tensor', [(i, i ^ bits) for i in range(tensors)])]
    all_to_all x2 -> x1, starting transfers between devices: 12.2 us -> 5.03 us  [exchange(): lax.all_to_all(owned, 'tensor', split_axis=0, concat_axis=0, tiled=True)]
    pallas_call x1, Pallas kernels: 14.6 us -> 8.56 us  [local(): call(functools.partial(expert_kernel, bounds), jax.ShapeDtypeStruct((tens...]
    all_to_all x1, blocking collectives: 27.9 us -> 25.2 us  [local(): lax.all_to_all(outgoing.reshape(tensors, slot_cap, width), 'tensor', spli...]
    all_gather x1 -> x2, blocking collectives: 1.93 us -> 4.22 us  [the longest x1 2.13 us: local(): attended = lax.all_gather(attended, 'group', axis=0, tiled=True)]
  transfers between devices with their start and end apart: 2 -> 11, of which waited for: 2 -> 3; matrix products, arithmetic and copies ran while one was open for 2% -> 2% of each run, Pallas kernels for 0% -> 17%
where the time goes in v2:
time: 93.3 us; the launch traced here: 92.6 us
  blocking collectives  29.4 us (32%)
  Pallas kernels  27.9 us (30%)
  starting transfers between devices  20.8 us (22%)
  waiting for transfers between devices  7.56 us (8%)
  local copies, waits for them, and re-layouts  5.48 us (6%)
  between operations  1.37 us (1%)
    all_to_all x1, blocking collectives, local(): lax.all_to_all(outgoing.reshape(tensors, slot_cap, width), 'tensor', spli...  25.2 us
    ppermute x10, starting transfers between devices, swap(): lax.ppermute(values, 'tensor', [(i, i ^ bits) for i in range(tensors)])  15.8 us
    pallas_call x1, Pallas kernels, local(): call(functools.partial(expert_kernel, bounds), jax.ShapeDtypeStruct((tens...  8.56 us
    ppermute x10, waiting for transfers between devices, swap(): lax.ppermute(values, 'tensor', [(i, i ^ bits) for i in range(tensors)])  7.56 us
    pallas_call x1, Pallas kernels, local(): call(load_kernel, jax.ShapeDtypeStruct((early_rows, columns), BF16), [ANY...  7.3 us
    all_to_all x1, starting transfers between devices, exchange(): lax.all_to_all(owned, 'tensor', split_axis=0, concat_axis=0, tiled=True)  5.03 us
    pallas_call x1, Pallas kernels, local(): call(functools.partial(attend_kernel, len(received), tok_dev, kv_rows), j...  4.59 us
    unnamed x10, local copies, waits for them, and re-layouts  2.93 us
  transfers between devices with their start and end apart: 11, of which 3 were waited for; matrix products, arithmetic and copies ran while one was open for 2% of the time, Pallas kernels for 17%

profile of v2, /device:TPU:0, one launch (start us, length us, event | category | flops | bytes accessed | tf_op | source)
XLA Modules:
  0.0 92.6 jit_solution(4287000724094580824)
XLA Ops:
  0.6 0.0 copy-start
  0.6 1.4 %copy-done = bf16[256,2880]{0,1:T(8,128)(2,1)S(1)} copy-done((bf16[256,2880]{0,1:T(8,128)(2,1)S(1)}, bf16[256,2880]{0,1:T(8,128)(2,1)}, u32[]{:S(2)}) %copy-start) | copy-done | bytes 1474584
  2.1 3.0 %collective-permute-start.4 = (bf16[1440,256]{1,0:T(8,128)(2,1)S(1)}, bf16[1440,256]{1,0:T(8,128)(2,1)S(1)}, u32[]{:S(2)}, u32[]{:S(2)}) collective-permute-start(bf16[1440,256]{1,0:T(8,128)(2,1)S(1)} %dynamic-slice_bitcast_fusion.refs_0_), channel_id=1, source_target_pairs={{0,2},{1,3},{2,0},{3,1},{4,6},{5,7},{6,4},{7,5},{8,10},{9,11},{10,... | collective-permute-start | bytes 2211848 | tf_op jit(solution)/shard_map/ppermute | solution.py:379
  5.1 1.5 %collective-permute-start.3 = (bf16[1440,256]{1,0:T(8,128)(2,1)S(1)}, bf16[1440,256]{1,0:T(8,128)(2,1)}, u32[]{:S(2)}, u32[]{:S(2)}) collective-permute-start(bf16[1440,256]{1,0:T(8,128)(2,1)S(1)} %dynamic-slice_bitcast_fusion.refs_0_), channel_id=1, source_target_pairs={{0,1},{1,0},{2,3},{3,2},{4,5},{5,4},{6,7},{7,6},{8,9},{9,8},{10,11... | collective-permute-start | bytes 2211848 | tf_op jit(solution)/shard_map/ppermute | solution.py:379
  7.2 21.7 %conditional.1 = (bf16[16,48,256]{2,1,0:T(8,128)(2,1)}, s32[1,128]{1,0:T(1,128)S(1)}, f32[1,2880]{1,0:T(1,128)S(1)}, bf16[80,256]{1,0:T(8,128)(2,1)S(1)}, bf16[8...) conditional(s32[]{:T(128)} %bitcast.3, () %tuple.19, (s32[1,1]{1,0:T(1,128)}, ...), branch_computations={%region_0.0_spmd, %region_1.0_spmd} | conditional | bytes 2220780 | solution.py:440
  7.3 2.5 %rotate_keys.1 = bf16[16,48,256]{2,1,0:T(8,128)(2,1)} custom-call(s32[1,1]{1,0:T(1,128)} %get-tuple-element.94.block_ref, bf16[16,1024]{1,0:T(8,128)(2,1)} %bitcast.23, bf16[32,1024]{1,0:T(8,128)(2,1)} %bitcast.22), custom_call_target="tpu_custom_call" | custom-call | tf_op jit(solution)/shard_map/cond/branch_1_fun/rotate_keys/pallas_call | solution.py:396
  9.7 5.0 %all-to-all-start = ((bf16[16,48,256]{2,1,0:T(8,128)(2,1)}), bf16[16,48,256]{2,1,0:T(8,128)(2,1)}, u32[]{:S(2)}, u32[]{:S(2)}) async-start(bf16[16,48,256]{2,1,0:T(8,128)(2,1)} %rotate_keys.1), calls=%async_computation | async-start | bytes 786432 | tf_op jit(solution)/shard_map/cond/branch_1_fun/all_to_all | solution.py:402
  14.8 0.0 copy-start.1
  14.8 0.9 copy-done.1
  15.7 1.1 %rotate_queries.1 = (bf16[80,256]{1,0:T(8,128)(2,1)S(1)}, bf16[80,256]{1,0:T(8,128)(2,1)S(1)}, bf16[80,256]{1,0:T(8,128)(2,1)S(1)}, bf16[80,256]{1,0:T(8,128)(2,1)S(1)}) custom-call(f32[4]{0:T(128)} %get-tuple-element.99.sink_ref, f32[256,128]{1,0:T(8,128)S(1)} %copy-done.1, bf16[256,256]{1,0:T(8,128)(2,1)} %bitcast.21), custom_call_target="tpu_custom_call" | custom-call | tf_op jit(solution)/shard_map/cond/branch_1_fun/rotate_queries/pallas_call | solution.py:404
  16.7 1.9 %collective-permute-start = (bf16[80,256]{1,0:T(8,128)(2,1)S(1)}, bf16[80,256]{1,0:T(8,128)(2,1)}, u32[]{:S(2)}, u32[]{:S(2)}) collective-permute-start(bf16[80,256]{1,0:T(8,128)(2,1)S(1)} %get-tuple-element.25), channel_id=1, source_target_pairs={{0,1},{1,0},{2,3},{3,2},{4,5},{5,4},{6,7},{7,6},{8,9},{9,8},{10,11... | collective-permute-start | bytes 122888 | tf_op jit(solution)/shard_map/cond/branch_1_fun/ppermute | solution.py:379
  18.7 1.5 %collective-permute-start.1 = (bf16[80,256]{1,0:T(8,128)(2,1)S(1)}, bf16[80,256]{1,0:T(8,128)(2,1)}, u32[]{:S(2)}, u32[]{:S(2)}) collective-permute-start(bf16[80,256]{1,0:T(8,128)(2,1)S(1)} %get-tuple-element.26), channel_id=1, source_target_pairs={{0,2},{1,3},{2,0},{3,1},{4,6},{5,7},{6,4},{7,5},{8,10},{9,11},{10,... | collective-permute-start | bytes 122888 | tf_op jit(solution)/shard_map/cond/branch_1_fun/ppermute | solution.py:379
  20.1 0.1 collective-permute-start.2
  20.3 0.7 broadcast_in_dim.4
  21.0 0.8 copy.25
  21.8 0.1 reshape.18
  21.9 6.8 %collective-permute-done = bf16[80,256]{1,0:T(8,128)(2,1)} collective-permute-done((bf16[80,256]{1,0:T(8,128)(2,1)S(1)}, bf16[80,256]{1,0:T(8,128)(2,1)}, u32[]{:S(2)}, u32[]{:S(2)}) %collective-permute-start) | collective-permute-done | bytes 40992 | tf_op jit(solution)/shard_map/cond/branch_1_fun/ppermute | solution.py:379
  28.7 0.0 collective-permute-done.1
  28.7 0.2 collective-permute-done.2
  28.9 0.0 all-to-all-done
  28.9 0.0 collective-permute-done.4.bottom_ref.refs_2_
  28.9 0.0 collective-permute-done.3.top_ref.refs_1_
  28.9 1.0 %split.1 = (bf16[720,256]{1,0:T(8,128)(2,1)S(1)}, bf16[720,256]{1,0:T(8,128)(2,1)S(1)}) custom-call(bf16[1440,256]{1,0:T(8,128)(2,1)} %collective-permute-done.3.top_ref.refs_1_, bf16[1440,256]{1,0:T(8,128)(2,1)S(1)} %collective-permute-done.4.bottom_ref.refs_2_), custom_call_target="tpu_custom_call" | custom-call | tf_op jit(solution)/shard_map/split/pallas_call | solution.py:453
  29.9 1.7 %collective-permute-start.5 = (bf16[720,256]{1,0:T(8,128)(2,1)S(1)}, bf16[720,256]{1,0:T(8,128)(2,1)S(1)}, u32[]{:S(2)}, u32[]{:S(2)}) collective-permute-start(bf16[720,256]{1,0:T(8,128)(2,1)S(1)} %get-tuple-element.68), channel_id=1, source_target_pairs={{0,2},{1,3},{2,0},{3,1},{4,6},{5,7},{6,4},{7,5},{8,10},{9,11},{10,... | collective-permute-start | bytes 1105928 | tf_op jit(solution)/shard_map/ppermute | solution.py:379
  31.7 1.5 %collective-permute-start.6 = (bf16[720,256]{1,0:T(8,128)(2,1)S(1)}, bf16[720,256]{1,0:T(8,128)(2,1)S(1)}, u32[]{:S(2)}, u32[]{:S(2)}) collective-permute-start(bf16[720,256]{1,0:T(8,128)(2,1)S(1)} %get-tuple-element.69), channel_id=1, source_target_pairs={{0,1},{1,0},{2,3},{3,2},{4,5},{5,4},{6,7},{7,6},{8,9},{9,8},{10,11... | collective-permute-start | bytes 1105928 | tf_op jit(solution)/shard_map/ppermute | solution.py:379
  33.2 0.0 copy-start.2
  33.2 0.9 copy-done.2
  34.1 0.0 copy-start.5
  34.1 0.7 copy-done.5
  34.7 4.6 %attend.1 = bf16[112,1024]{1,0:T(8,128)(2,1)S(1)} custom-call(s32[1,2]{1,0:T(1,128)S(1)} %copy-done.5, bf16[80,256]{1,0:T(8,128)(2,1)S(1)} %get-tuple-element.60.refs_0_, bf16[80,256]{1,0:T(8,128)(2,1)} %get-tuple-element.61.refs_1_, bf16[80,256]{1,0:T(8,128)(2,1)} %get-tuple-element.62.refs_2_, bf16[80,256]{1,0:T(8,128)(2,1)} %get-tuple-element.63.refs_3_, ...), custom_call_target="tpu_custom_call" | custom-call | tf_op jit(solution)/shard_map/attend/pallas_call | solution.py:473
  39.3 2.1 %all_gather.6.att_ref.resid_ref = bf16[224,1024]{1,0:T(8,128)(2,1)S(1)} all-gather(bf16[112,1024]{1,0:T(8,128)(2,1)S(1)} %attend.1), channel_id=1, replica_groups=mesh['group'=2,'tensor'=16] {'group'}, dimensions={0}, use_global_device_ids=true | all-gather | bytes 688128 | tf_op jit(solution)/shard_map/all_gather | solution.py:480
  41.5 0.0 collective-permute-done.5.refs_3_
  41.5 0.0 collective-permute-done.6.refs_4_
  41.5 2.1 %project.1 = (f32[32,1440]{1,0:T(8,128)S(1)}, bf16[32,1440]{1,0:T(8,128)(2,1)S(1)}, bf16[32,1440]{1,0:T(8,128)(2,1)S(1)}, bf16[32,1440]{1,0:T(8,128)(2,1)S(1)}) custom-call(bf16[224,1024]{1,0:T(8,128)(2,1)S(1)} %all_gather.6.att_ref.resid_ref, bf16[1440,256]{1,0:T(8,128)(2,1)S(1)} %dynamic-slice_bitcast_fusion.refs_0_, ...), custom_call_target="tpu_custom_call" | custom-call | tf_op jit(solution)/shard_map/project/pallas_call | solution.py:489
  43.6 0.0 copy-start.3
  43.6 0.0 copy-start.4
  43.6 1.6 %collective-permute-start.7 = (bf16[32,1440]{1,0:T(8,128)(2,1)S(1)}, bf16[32,1440]{1,0:T(8,128)(2,1)S(1)}, u32[]{:S(2)}, u32[]{:S(2)}) collective-permute-start(bf16[32,1440]{1,0:T(8,128)(2,1)S(1)} %get-tuple-element.75), channel_id=1, source_target_pairs={{0,4},{1,5},{2,6},{3,7},{4,0},{5,1},{6,2},{7,3},{8,12},{9,13},{10,... | collective-permute-start | bytes 276488 | tf_op jit(solution)/shard_map/ppermute | solution.py:379
  45.2 2.6 %collective-permute-start.8 = (bf16[32,1440]{1,0:T(8,128)(2,1)S(1)}, bf16[32,1440]{1,0:T(8,128)(2,1)S(1)}, u32[]{:S(2)}, u32[]{:S(2)}) collective-permute-start(bf16[32,1440]{1,0:T(8,128)(2,1)S(1)} %get-tuple-element.76), channel_id=1, source_target_pairs={{0,8},{1,9},{2,10},{3,11},{4,12},{5,13},{6,14},{7,15},{8,0},{9,1},... | collective-permute-start | bytes 276488 | tf_op jit(solution)/shard_map/ppermute | solution.py:379
  47.8 0.2 collective-permute-start.9
  48.0 7.3 %load_expert.1.early_ref = bf16[1920,5760]{1,0:T(8,128)(2,1)S(1)} custom-call(bf16[2880,5760]{1,0:T(8,128)(2,1)} %bitcast.18), custom_call_target="tpu_custom_call" | custom-call | bytes 44236800 | tf_op jit(solution)/shard_map/load_expert/pallas_call | solution.py:514
  55.4 0.0 collective-permute-done.7.refs_1_
  55.4 0.5 collective-permute-done.8.refs_2_
  55.9 0.0 collective-permute-done.9.refs_3_
  55.9 2.1 %all_gather.7.sums_ref = f32[64,1440]{1,0:T(8,128)S(1)} all-gather(f32[32,1440]{1,0:T(8,128)S(1)} %sum_planes.1), channel_id=1, replica_groups=mesh['group'=2,'tensor'=16] {'group'}, dimensions={0}, use_global_device_ids=true | all-gather | bytes 552960 | tf_op jit(solution)/shard_map/all_gather | solution.py:530
  58.0 0.0 copy-done.3
  58.0 0.0 copy-done.4
  58.0 0.8 norm_dispatch.1
  58.8 25.2 %all_to_all.9 = bf16[16,8,2880]{2,1,0:T(8,128)(2,1)S(1)} all-to-all(bf16[16,8,2880]{2,1,0:T(8,128)(2,1)S(1)} %bitcast.15), channel_id=1, replica_groups=mesh['group'=2,'tensor'=16] {'tensor'}, dimensions={0} | all-to-all | bytes 1474560 | tf_op jit(solution)/shard_map/all_to_all | solution.py:551
  84.0 8.6 %experts.1 = bf16[128,2880]{1,0:T(8,128)(2,1)} custom-call(bf16[128,2880]{1,0:T(8,128)(2,1)S(1)} %bitcast.14, bf16[1920,5760]{1,0:T(8,128)(2,1)S(1)} %load_expert.1.early_ref, bf16[2880,5760]{1,0:T(8,128)(2,1)} %bitcast.19), custom_call_target="tpu_custom_call" | custom-call | tf_op jit(solution)/shard_map/experts/pallas_call | solution.py:559
  (2 shorter events, 0.1 us)
Async XLA Ops:
  0.6 1.4 %copy-start = (bf16[256,2880]{0,1:T(8,128)(2,1)S(1)}, bf16[256,2880]{0,1:T(8,128)(2,1)}, u32[]{:S(2)}) copy-start(bf16[256,2880]{0,1:T(8,128)(2,1)} %param.23) | copy-start | bytes 4423684
  2.1 26.9 %collective-permute-start.4 = (bf16[1440,256]{1,0:T(8,128)(2,1)S(1)}, bf16[1440,256]{1,0:T(8,128)(2,1)S(1)}, u32[]{:S(2)}, u32[]{:S(2)}) collective-permute-start(bf16[1440,256]{1,0:T(8,128)(2,1)S(1)} %dynamic-slice_bitcast_fusion.refs_0_), channel_id=1, source_target_pairs={{0,2},{1,3},{2,0},{3,1},{4,6},{5,7},{6,4},{7,5},{8,10},{9,11},{10,... | collective-permute-start | bytes 2211848 | tf_op jit(solution)/shard_map/ppermute | solution.py:379
  5.1 23.8 %collective-permute-start.3 = (bf16[1440,256]{1,0:T(8,128)(2,1)S(1)}, bf16[1440,256]{1,0:T(8,128)(2,1)}, u32[]{:S(2)}, u32[]{:S(2)}) collective-permute-start(bf16[1440,256]{1,0:T(8,128)(2,1)S(1)} %dynamic-slice_bitcast_fusion.refs_0_), channel_id=1, source_target_pairs={{0,1},{1,0},{2,3},{3,2},{4,5},{5,4},{6,7},{7,6},{8,9},{9,8},{10,11... | collective-permute-start | bytes 2211848 | tf_op jit(solution)/shard_map/ppermute | solution.py:379
  9.7 19.2 %all-to-all-start = ((bf16[16,48,256]{2,1,0:T(8,128)(2,1)}), bf16[16,48,256]{2,1,0:T(8,128)(2,1)}, u32[]{:S(2)}, u32[]{:S(2)}) async-start(bf16[16,48,256]{2,1,0:T(8,128)(2,1)} %rotate_keys.1), calls=%async_computation | async-start | bytes 786432 | tf_op jit(solution)/shard_map/cond/branch_1_fun/all_to_all | solution.py:402
  14.8 0.9 copy-start.1
  16.7 11.9 %collective-permute-start = (bf16[80,256]{1,0:T(8,128)(2,1)S(1)}, bf16[80,256]{1,0:T(8,128)(2,1)}, u32[]{:S(2)}, u32[]{:S(2)}) collective-permute-start(bf16[80,256]{1,0:T(8,128)(2,1)S(1)} %get-tuple-element.25), channel_id=1, source_target_pairs={{0,1},{1,0},{2,3},{3,2},{4,5},{5,4},{6,7},{7,6},{8,9},{9,8},{10,11... | collective-permute-start | bytes 122888 | tf_op jit(solution)/shard_map/cond/branch_1_fun/ppermute | solution.py:379
  18.7 10.0 %collective-permute-start.1 = (bf16[80,256]{1,0:T(8,128)(2,1)S(1)}, bf16[80,256]{1,0:T(8,128)(2,1)}, u32[]{:S(2)}, u32[]{:S(2)}) collective-permute-start(bf16[80,256]{1,0:T(8,128)(2,1)S(1)} %get-tuple-element.26), channel_id=1, source_target_pairs={{0,2},{1,3},{2,0},{3,1},{4,6},{5,7},{6,4},{7,5},{8,10},{9,11},{10,... | collective-permute-start | bytes 122888 | tf_op jit(solution)/shard_map/cond/branch_1_fun/ppermute | solution.py:379
  20.1 8.8 %collective-permute-start.2 = (bf16[80,256]{1,0:T(8,128)(2,1)S(1)}, bf16[80,256]{1,0:T(8,128)(2,1)}, u32[]{:S(2)}, u32[]{:S(2)}) collective-permute-start(bf16[80,256]{1,0:T(8,128)(2,1)S(1)} %get-tuple-element.27), channel_id=1, source_target_pairs={{0,3},{1,2},{2,1},{3,0},{4,7},{5,6},{6,5},{7,4},{8,11},{9,10},{10,... | collective-permute-start | bytes 122888 | tf_op jit(solution)/shard_map/cond/branch_1_fun/ppermute | solution.py:379
  29.9 11.5 %collective-permute-start.5 = (bf16[720,256]{1,0:T(8,128)(2,1)S(1)}, bf16[720,256]{1,0:T(8,128)(2,1)S(1)}, u32[]{:S(2)}, u32[]{:S(2)}) collective-permute-start(bf16[720,256]{1,0:T(8,128)(2,1)S(1)} %get-tuple-element.68), channel_id=1, source_target_pairs={{0,2},{1,3},{2,0},{3,1},{4,6},{5,7},{6,4},{7,5},{8,10},{9,11},{10,... | collective-permute-start | bytes 1105928 | tf_op jit(solution)/shard_map/ppermute | solution.py:379
  31.7 9.8 %collective-permute-start.6 = (bf16[720,256]{1,0:T(8,128)(2,1)S(1)}, bf16[720,256]{1,0:T(8,128)(2,1)S(1)}, u32[]{:S(2)}, u32[]{:S(2)}) collective-permute-start(bf16[720,256]{1,0:T(8,128)(2,1)S(1)} %get-tuple-element.69), channel_id=1, source_target_pairs={{0,1},{1,0},{2,3},{3,2},{4,5},{5,4},{6,7},{7,6},{8,9},{9,8},{10,11... | collective-permute-start | bytes 1105928 | tf_op jit(solution)/shard_map/ppermute | solution.py:379
  33.2 0.9 copy-start.2
  34.1 0.7 copy-start.5
  43.6 14.5 %copy-start.3 = (bf16[128,32]{1,0:T(8,128)(2,1)S(1)}, bf16[128,32]{1,0:T(8,128)(2,1)}, u32[]{:S(2)}) copy-start(bf16[128,32]{1,0:T(8,128)(2,1)} %constant.29.clone.source_ref) | copy-start | bytes 24580
  43.6 14.5 %copy-start.4 = (bf16[128,128]{1,0:T(8,128)(2,1)S(1)}, bf16[128,128]{1,0:T(8,128)(2,1)}, u32[]{:S(2)}) copy-start(bf16[128,128]{1,0:T(8,128)(2,1)} %constant.28.clone.earlier_ref) | copy-start | bytes 98308
  43.6 11.8 %collective-permute-start.7 = (bf16[32,1440]{1,0:T(8,128)(2,1)S(1)}, bf16[32,1440]{1,0:T(8,128)(2,1)S(1)}, u32[]{:S(2)}, u32[]{:S(2)}) collective-permute-start(bf16[32,1440]{1,0:T(8,128)(2,1)S(1)} %get-tuple-element.75), channel_id=1, source_target_pairs={{0,4},{1,5},{2,6},{3,7},{4,0},{5,1},{6,2},{7,3},{8,12},{9,13},{10,... | collective-permute-start | bytes 276488 | tf_op jit(solution)/shard_map/ppermute | solution.py:379
  45.2 10.7 %collective-permute-start.8 = (bf16[32,1440]{1,0:T(8,128)(2,1)S(1)}, bf16[32,1440]{1,0:T(8,128)(2,1)S(1)}, u32[]{:S(2)}, u32[]{:S(2)}) collective-permute-start(bf16[32,1440]{1,0:T(8,128)(2,1)S(1)} %get-tuple-element.76), channel_id=1, source_target_pairs={{0,8},{1,9},{2,10},{3,11},{4,12},{5,13},{6,14},{7,15},{8,0},{9,1},... | collective-permute-start | bytes 276488 | tf_op jit(solution)/shard_map/ppermute | solution.py:379
  47.8 8.1 %collective-permute-start.9 = (bf16[32,1440]{1,0:T(8,128)(2,1)S(1)}, bf16[32,1440]{1,0:T(8,128)(2,1)S(1)}, u32[]{:S(2)}, u32[]{:S(2)}) collective-permute-start(bf16[32,1440]{1,0:T(8,128)(2,1)S(1)} %get-tuple-element.77), channel_id=1, source_target_pairs={{0,12},{1,13},{2,14},{3,15},{4,8},{5,9},{6,10},{7,11},{8,4},{9,5},... | collective-permute-start | bytes 276488 | tf_op jit(solution)/shard_map/ppermute | solution.py:379

commit v3 on v2

--- a/solution.py
+++ b/solution.py
@@ -23,7 +23,7 @@
 PLANE = 4
 
 
-def call(kernel, outs, specs, name, scratch=(), limit=12, moved=0, space=VMEM):
+def call(kernel, outs, specs, name, scratch=(), limit=12, moved=0, space=VMEM, flops=0):
     single = not isinstance(outs, (list, tuple))
     return pl.pallas_call(
         kernel,
@@ -33,7 +33,7 @@
         scratch_shapes=list(scratch),
         name=name,
         compiler_params=pltpu.CompilerParams(vmem_limit_bytes=limit * 1024 * 1024),
-        cost_estimate=pl.CostEstimate(flops=0, bytes_accessed=moved, transcendentals=0),
+        cost_estimate=pl.CostEstimate(flops=flops, bytes_accessed=moved, transcendentals=0),
     )
 
 
@@ -56,7 +56,15 @@
     return jnp.where(lane % HD < HD // 2, ahead, behind)
 
 
-def keys_kernel(heads_here, tensors, block_ref, suffix_ref, prefix_ref, out_ref):
+def keys_kernel(
+    heads_here, tensors, block_ref, suffix_hbm, prefix_hbm, out_ref, suffix_ref, prefix_ref, sems
+):
+    copies = [
+        pltpu.make_async_copy(prefix_hbm, prefix_ref, sems.at[0]),
+        pltpu.make_async_copy(suffix_hbm, suffix_ref, sems.at[1]),
+    ]
+    for copy in copies:
+        copy.start()
     block_rows = prefix_ref.shape[0]
     tok_dev = suffix_ref.shape[0]
     prefix_len = block_rows * tensors
@@ -92,11 +100,13 @@
             out_ref[peer, low : low + rows, :LANES] = made[one, two][0]
             out_ref[peer, low : low + rows, LANES:] = made[one, two][1]
 
+    copies[0].wait()
     part(prefix_ref, block_ref[0, 0] * block_rows, 0)
+    copies[1].wait()
     part(suffix_ref, prefix_len + lax.axis_index("tensor") * tok_dev % MAXLEN, block_rows)
 
 
-def queries_kernel(tok_dev, sink_ref, turn_ref, q_ref, *out_refs):
+def queries_kernel(tok_dev, len_ref, sink_ref, turn_ref, q_ref, resid_ref, *out_refs):
     me = lax.axis_index("tensor")
     planes = q_ref.shape[0] // tok_dev // PLANE
     width = q_ref.shape[1]
@@ -109,6 +119,8 @@
     middle = (sink - high).astype(BF16).astype(F32)
     low = sink - high - middle
     terms = jnp.where(row == 0, high, jnp.where(row == 1, middle, jnp.where(row == 2, low, 0.0)))
+    for number in range(len_ref.shape[1]):
+        terms = jnp.where(row == 3 + number, len_ref[0, number].astype(F32), terms)
     for peer in range(PLANE):
         for plane in range(planes):
             block = me ^ (plane * PLANE + peer)
@@ -122,6 +134,11 @@
                 turned = query * cosine + partner(query) * sine
                 out_refs[peer][plane * tok_dev : (plane + 1) * tok_dev, span] = turned.astype(BF16)
         out_refs[peer][planes * tok_dev : planes * tok_dev + 16, :] = terms.astype(BF16)
+    step = out_refs[-1].shape[1]
+    for number, first in enumerate(range(0, resid_ref.shape[1], step)):
+        size = min(step, resid_ref.shape[1] - first)
+        rows = slice(number * tok_dev, (number + 1) * tok_dev)
+        out_refs[-1][rows, :size] = resid_ref[:, first : first + size]
 
 
 def rotate_kernel(turn_ref, q_ref, out_ref):
@@ -132,9 +149,25 @@
         out_ref[rows, :] = turned.astype(BF16)
 
 
-def attend_kernel(blocks, tok_dev, kv_rows, len_ref, *refs):
-    q_refs, kv_ref, resid_refs, out_ref = refs[:blocks], refs[blocks], refs[blocks + 1 : -1], refs[-1]
-    rows = q_refs[0].shape[0] - 16
+def attend_kernel(blocks, requests, tok_dev, kv_rows, *refs):
+    q_refs, kv_ref, w_ref = refs[:blocks], refs[blocks], refs[blocks + 1]
+    resid_refs, (out_ref, early_ref, own_ref, sems) = refs[blocks + 2 : -4], refs[-4:]
+    own = pltpu.make_async_copy(q_refs[0], own_ref, sems.at[0])
+    own.start()
+    rows = own_ref.shape[0] - 16
+    loads = [
+        pltpu.make_async_copy(resid_ref, out_ref.at[pl.ds(rows, resid_ref.shape[0])], sems.at[1])
+        for resid_ref in resid_refs
+    ]
+    loads.append(
+        pltpu.make_async_copy(w_ref.at[pl.ds(0, early_ref.shape[0])], early_ref, sems.at[2])
+    )
+    for load in loads:
+        load.start()
+    q_refs = [own_ref, *q_refs[1:]]
+    told_ref = q_refs[-1]
+    if blocks == 1:
+        own.wait()
     inner = lax.axis_index("tensor") & (PLANE - 1)
     plane = lax.axis_index("tensor") >> log2(PLANE)
     low = lax.broadcasted_iota(jnp.int32, (kv_ref.shape[0], LANES), 1) < HD
@@ -154,8 +187,10 @@
     slot = (((row >> shift) ^ plane) * PLANE + inner) * tok_dev + (row & (tok_dev - 1))
     request = slot >> (MAXLEN.bit_length() - 1)
     length = jnp.zeros_like(slot)
-    for number in range(len_ref.shape[1]):
-        length = jnp.where(request == number, len_ref[0, number], length)
+    told = told_ref[rows : rows + 16, :LANES].astype(F32)
+    for number in range(requests):
+        live = told[3 + number : 4 + number, 0:1].astype(jnp.int32)
+        length = jnp.where(request == number, live, length)
     base = request * MAXLEN
     last = jnp.minimum(slot, base + length - 1)
     key_row = lax.broadcasted_iota(jnp.int32, (1, kv_ref.shape[0]), 1)
@@ -164,7 +199,9 @@
     key_slot = jnp.where(inside < 0, -1, source * tok_dev + inside)
     visible = (key_slot < 0) | ((key_slot >= base) & (key_slot <= last))
     left = lax.broadcasted_iota(jnp.int32, (rows, LANES), 1) < HD
-    for block in range(blocks):
+    for block in reversed(range(blocks)):
+        if block == 0 and blocks > 1:
+            own.wait()
         for pair in range(2):
             half = block // 2 if blocks == PLANE else pair
             span = slice(pair * LANES, (pair + 1) * LANES)
@@ -191,12 +228,8 @@
             got = jnp.dot(weights.astype(BF16), vals[half], preferred_element_type=F32) / total
             at = block * 2 * LANES + pair * LANES
             out_ref[:rows, at : at + LANES] = jnp.where(left, got[:rows], got[rows:]).astype(BF16)
-    for resid_ref in resid_refs:
-        step = out_ref.shape[1]
-        for number, first in enumerate(range(0, resid_ref.shape[1], step)):
-            size = min(step, resid_ref.shape[1] - first)
-            at = rows + number * tok_dev
-            out_ref[at : at + tok_dev, :size] = resid_ref[:, first : first + size]
+    for load in loads:
+        load.wait()
 
 
 def project_kernel(tok_dev, groups, att_ref, *refs):
@@ -243,7 +276,8 @@
 
 
 def load_kernel(w_ref, out_ref, sem):
-    copy = pltpu.make_async_copy(w_ref.at[pl.ds(0, out_ref.shape[0])], out_ref, sem)
+    count = out_ref.shape[0]
+    copy = pltpu.make_async_copy(w_ref.at[pl.ds(w_ref.shape[0] - count, count)], out_ref, sem)
     copy.start()
     copy.wait()
 
@@ -326,23 +360,11 @@
     out_ref[...] = jnp.dot(chosen.astype(BF16), normed, preferred_element_type=F32).astype(BF16)
 
 
-def expert_kernel(bounds, rows_ref, early_ref, w_ref, out_ref, held, total, sems):
+def expert_kernel(rows_ref, early_ref, late_ref, out_ref):
     start = early_ref.shape[0]
-    copies = [
-        pltpu.make_async_copy(
-            w_ref.at[pl.ds(lo, hi - lo)], held.at[pl.ds(lo - start, hi - lo)], sems.at[k]
-        )
-        for k, (lo, hi) in enumerate(bounds)
-    ]
-    for copy in copies:
-        copy.start()
-    total[...] = jnp.dot(rows_ref[:, :start], early_ref[...], preferred_element_type=F32)
-    for k, (lo, hi) in enumerate(bounds):
-        copies[k].wait()
-        total[...] += jnp.dot(
-            rows_ref[:, lo:hi], held[lo - start : hi - start, :], preferred_element_type=F32
-        )
     width = out_ref.shape[1]
+    total = jnp.dot(rows_ref[:, :start], early_ref[...], preferred_element_type=F32)
+    total = total + jnp.dot(rows_ref[:, start:], late_ref[...], preferred_element_type=F32)
     gate = jnp.minimum(total[:, :width], 7.0)
     up = jnp.clip(total[:, width : 2 * width], -7.0, 7.0)
     out_ref[...] = ((up + 1.0) * gate / (1.0 + jnp.exp(-1.702 * gate))).astype(BF16)
@@ -392,64 +414,53 @@
     top_count = routes.shape[2]
     pair_count = tok_dev * groups * top_count
 
-    def exchange(suffix, prefix, mine, sink_logits, block, named, gains):
-        owned = call(
-            functools.partial(keys_kernel, heads_here, tensors),
-            jax.ShapeDtypeStruct((tensors, kv_rows, 2 * LANES), BF16),
-            [SMEM, VMEM, VMEM],
-            "rotate_keys",
-        )(block, suffix, prefix)
-        kv = lax.all_to_all(owned, "tensor", split_axis=0, concat_axis=0, tiled=True)
-        if aligned:
-            sent = call(
-                functools.partial(queries_kernel, tok_dev),
-                [jax.ShapeDtypeStruct((slots_here + 16, query_cols), BF16)] * PLANE,
-                [SMEM, VMEM, VMEM],
-                "rotate_queries",
-            )(sink_logits, turns, mine)
-        else:
-            padded = jnp.pad(mine, ((0, 0), (0, LANES - query_cols)))
-            turned = call(
-                rotate_kernel,
-                jax.ShapeDtypeStruct(padded.shape, BF16),
-                [VMEM, VMEM],
-                "rotate_queries",
-            )(turns, padded)[:, :query_cols]
-            turned = turned.reshape(tensors, tok_dev, query_cols)
-            turned = jnp.take(turned, me_tensor ^ jnp.arange(tensors), axis=0)
-            turned = turned.reshape(planes, PLANE, tok_dev, query_cols)
-            spread = jnp.repeat(sink_logits, HD)
-            high = lax.reduce_precision(spread, 8, 7)
-            middle = lax.reduce_precision(spread - high, 8, 7)
-            terms = jnp.pad(jnp.stack([high, middle, spread - high - middle]), ((0, 13), (0, 0)))
-            sent = [
-                jnp.concatenate(
-                    [turned[:, peer].reshape(slots_here, query_cols), terms.astype(BF16)], axis=0
-                )
-                for peer in range(PLANE)
-            ]
-        moved = [swap(sent[peer], peer) for peer in range(1, PLANE)]
-        return (kv, named.reshape(1, pair_count), gains[None, :], sent[0], *moved)
-
-    def nothing(*operands):
-        shape = (slots_here + 16, query_cols)
-        kv = jnp.zeros((tensors, kv_rows, 2 * LANES), BF16)
-        names, gain = jnp.zeros((1, pair_count), jnp.int32), jnp.zeros((1, width), F32)
-        return (kv, names, gain, *(jnp.zeros(shape, BF16) for _ in range(PLANE)))
-
-    kv, names, gain, *received = lax.cond(
-        lengths[0, 0] > 0,
-        exchange,
-        nothing,
-        suffix_kv[0],
-        prefix_kv[0],
-        queries[0],
-        sinks,
-        block_map,
-        routes,
-        mlp_gain,
-    )
-    kv, beside, across = lax.optimization_barrier((kv, beside, across))
+    owned = call(
+        functools.partial(keys_kernel, heads_here, tensors),
+        jax.ShapeDtypeStruct((tensors, kv_rows, 2 * LANES), BF16),
+        [SMEM, ANY, ANY],
+        "rotate_keys",
+        scratch=[
+            pltpu.VMEM(suffix_kv.shape[1:], BF16),
+            pltpu.VMEM(prefix_kv.shape[1:], BF16),
+            pltpu.SemaphoreType.DMA((2,)),
+        ],
+    )(block_map, suffix_kv[0], prefix_kv[0])
+    if aligned:
+        extra = -(-width // (PLANE * query_cols)) * tok_dev
+        *sent, packed = call(
+            functools.partial(queries_kernel, tok_dev),
+            [jax.ShapeDtypeStruct((slots_here + 16, query_cols), BF16)] * PLANE
+            + [jax.ShapeDtypeStruct((extra, PLANE * query_cols), BF16)],
+            [SMEM, SMEM, VMEM, VMEM, VMEM],
+            "rotate_queries",
+        )(lengths, sinks, turns, queries[0], resid_in[0])
+        packed = [packed]
+    else:
+        extra, packed = 0, []
+        padded = jnp.pad(queries[0], ((0, 0), (0, LANES - query_cols)))
+        turned = call(
+            rotate_kernel,
+            jax.ShapeDtypeStruct(padded.shape, BF16),
+            [VMEM, VMEM],
+            "rotate_queries",
+        )(turns, padded)[:, :query_cols]
+        turned = turned.reshape(tensors, tok_dev, query_cols)
+        turned = jnp.take(turned, me_tensor ^ jnp.arange(tensors), axis=0)
+        turned = turned.reshape(planes, PLANE, tok_dev, query_cols)
+        spread = jnp.repeat(sinks, HD)
+        high = lax.reduce_precision(spread, 8, 7)
+        middle = lax.reduce_precision(spread - high, 8, 7)
+        told = jnp.broadcast_to(lengths[0].astype(F32)[:, None], (lengths.shape[1], query_cols))
+        terms = jnp.concatenate([jnp.stack([high, middle, spread - high - middle]), told], axis=0)
+        terms = jnp.pad(terms, ((0, 16 - terms.shape[0]), (0, 0))).astype(BF16)
+        sent = [
+            jnp.concatenate([turned[:, peer].reshape(slots_here, query_cols), terms], axis=0)
+            for peer in range(PLANE)
+        ]
+    kv = lax.all_to_all(owned, "tensor", split_axis=0, concat_axis=0, tiled=True)
+    received = [sent[0]] + [swap(sent[peer], peer) for peer in range(1, PLANE)]
+    names, gain = routes.reshape(1, pair_count), mlp_gain[None, :]
+    beside, across, names, gain = lax.optimization_barrier((beside, across, names, gain))
     halves = call(
         split_kernel,
         [
@@ -468,14 +479,24 @@
     if not aligned:
         received = [jnp.concatenate(received, axis=1)]
 
-    packed = [resid_in[0]] if aligned else []
-    extra = -(-width // (PLANE * query_cols)) * tok_dev if aligned else 0
-    attended = call(
-        functools.partial(attend_kernel, len(received), tok_dev, kv_rows),
-        jax.ShapeDtypeStruct((slots_here + extra, PLANE * query_cols), BF16),
-        [SMEM] + [VMEM] * (1 + len(received) + int(aligned)),
+    columns = w_experts.shape[2]
+    early_rows = min(width // 2, 768)
+    attended, early = call(
+        functools.partial(attend_kernel, len(received), lengths.shape[1], tok_dev, kv_rows),
+        [
+            jax.ShapeDtypeStruct((slots_here + extra, PLANE * query_cols), BF16),
+            jax.ShapeDtypeStruct((early_rows, columns), BF16),
+        ],
+        [ANY] + [VMEM] * len(received) + [ANY] * (1 + len(packed)),
         "attend",
-    )(lengths, *received, kv, *packed)
+        scratch=[
+            pltpu.VMEM(received[0].shape, BF16),
+            pltpu.SemaphoreType.DMA((3,)),
+        ],
+        limit=26,
+        moved=15000000,
+        flops=5000000000,
+    )(*received, kv, w_experts[0], *packed)
 
     attended = lax.all_gather(attended, "group", axis=0, tiled=True)
     rows_here = groups * tok_dev
@@ -507,20 +528,18 @@
     slot_cap = pair_count // 16 // copies
     resid_all = attended if aligned else lax.all_gather(resid_in[0], "group", axis=0, tiled=True)
     *parts, piece = lax.optimization_barrier((*parts, w_experts[0]))
-    arrived = [parts[0]] + [swap(parts[plane], plane * PLANE) for plane in range(1, planes)]
-    columns = piece.shape[1]
-    step = 384
-    early_rows = 5 * step
-    early = call(
+    arrived = [swap(parts[plane], plane * PLANE) for plane in reversed(range(1, planes))]
+    arrived = [parts[0]] + arrived
+    late = call(
         load_kernel,
-        jax.ShapeDtypeStruct((early_rows, columns), BF16),
+        jax.ShapeDtypeStruct((width - early_rows, columns), BF16),
         [ANY],
         "load_expert",
         scratch=[pltpu.SemaphoreType.DMA],
-        limit=12,
-        moved=2 * early_rows * columns * 2,
+        limit=4,
+        moved=2 * (width - early_rows) * columns * 2,
     )(piece)
-    *arrived, early = lax.optimization_barrier((*arrived, early))
+    *arrived, late = lax.optimization_barrier((*arrived, late))
     sums = call(
         sum_kernel,
         jax.ShapeDtypeStruct((rows_here, columns_here), F32),
@@ -555,19 +574,13 @@
         concat_axis=0,
         tiled=True,
     )
-    bounds = [(lo, min(lo + step, width)) for lo in range(early_rows, width, step)]
     hidden = call(
-        functools.partial(expert_kernel, bounds),
+        expert_kernel,
         jax.ShapeDtypeStruct((tensors * slot_cap, columns // 2), BF16),
-        [VMEM, VMEM, ANY],
+        [VMEM] * 3,
         "experts",
-        scratch=[
-            pltpu.VMEM((width - early_rows, columns), BF16),
-            pltpu.VMEM((tensors * slot_cap, columns), F32),
-            pltpu.SemaphoreType.DMA((len(bounds),)),
-        ],
-        limit=24,
-    )(rows.reshape(tensors * slot_cap, width), early, piece)
+        limit=16,
+    )(rows.reshape(tensors * slot_cap, width), early, late)
     return (resid_out[None], hidden.reshape(1, tensors, slot_cap, columns // 2))
 
 

time: 93.3 us -> 87.5 us (0.938)
  waiting for transfers between devices: 7.56 us -> 2.16 us
  Pallas kernels: 27.9 us -> 23.9 us
  local copies, waits for them, and re-layouts: 5.48 us -> 8.63 us
  blocking collectives: 29.4 us -> 31.2 us
  starting transfers between devices: 20.8 us -> 19.5 us
    ppermute x10, waiting for transfers between devices: 7.56 us -> 2.16 us  [swap(): lax.ppermute(values, 'tensor', [(i, i ^ bits) for i in range(tensors)])]
    unnamed x10 -> x23, local copies, waits for them, and re-layouts: 2.93 us -> 7.76 us
    pallas_call x5, Pallas kernels: 24 us -> 21.2 us  [the longest x1 7.93 us: local(): call(load_kernel, jax.ShapeDtypeStruct((width - early_rows, columns), BF1...]
    all_to_all x1, blocking collectives: 25.2 us -> 26.9 us  [local(): lax.all_to_all(outgoing.reshape(tensors, slot_cap, width), 'tensor', spli...]
    ppermute x10, starting transfers between devices: 15.8 us -> 14.5 us  [swap(): lax.ppermute(values, 'tensor', [(i, i ^ bits) for i in range(tensors)])]
    pallas_call x1, Pallas kernels: 2.1 us -> 0.99 us  [local(): call(functools.partial(project_kernel, tok_dev, groups), outs, [VMEM] * (...]
  transfers between devices with their start and end apart: 11 -> 11, of which waited for: 3 -> 1; matrix products, arithmetic and copies ran while one was open for 2% -> 2% of each run, Pallas kernels for 17% -> 18%
where the time goes in v3:
time: 87.5 us; the launch traced here: 86.8 us
  blocking collectives  31.2 us (36%)
  Pallas kernels  23.9 us (27%)
  starting transfers between devices  19.5 us (22%)
  local copies, waits for them, and re-layouts  8.63 us (10%)
  waiting for transfers between devices  2.16 us (2%)
  between operations  1.46 us (2%)
    all_to_all x1, blocking collectives, local(): lax.all_to_all(outgoing.reshape(tensors, slot_cap, width), 'tensor', spli...  26.9 us
    ppermute x10, starting transfers between devices, swap(): lax.ppermute(values, 'tensor', [(i, i ^ bits) for i in range(tensors)])  14.5 us
    pallas_call x1, Pallas kernels, local(): call(load_kernel, jax.ShapeDtypeStruct((width - early_rows, columns), BF1...  7.93 us
    unnamed x23, local copies, waits for them, and re-layouts  7.76 us
    pallas_call x1, Pallas kernels, local(): call(expert_kernel, jax.ShapeDtypeStruct((tensors * slot_cap, columns //...  6.04 us
    all_to_all x1, starting transfers between devices, local(): lax.all_to_all(owned, 'tensor', split_axis=0, concat_axis=0, tiled=True)  4.99 us
    pallas_call x1, Pallas kernels, local(): call(functools.partial(attend_kernel, len(received), lengths.shape[1], to...  4.72 us
    ppermute x10, waiting for transfers between devices, swap(): lax.ppermute(values, 'tensor', [(i, i ^ bits) for i in range(tensors)])  2.16 us
  transfers between devices with their start and end apart: 11, of which 1 were waited for; matrix products, arithmetic and copies ran while one was open for 2% of the time, Pallas kernels for 18%

profile of v3, /device:TPU:0, one launch (start us, length us, event | category | flops | bytes accessed | tf_op | source)
XLA Modules:
  0.0 86.8 jit_solution(1728736033774094224)
XLA Ops:
  0.6 0.0 copy-start
  0.7 1.4 %copy-done = bf16[256,2880]{0,1:T(8,128)(2,1)S(1)} copy-done((bf16[256,2880]{0,1:T(8,128)(2,1)S(1)}, bf16[256,2880]{0,1:T(8,128)(2,1)}, u32[]{:S(2)}) %copy-start) | copy-done | bytes 1474584
  2.1 3.0 %collective-permute-start.1 = (bf16[1440,256]{1,0:T(8,128)(2,1)S(1)}, bf16[1440,256]{1,0:T(8,128)(2,1)S(1)}, u32[]{:S(2)}, u32[]{:S(2)}) collective-permute-start(bf16[1440,256]{1,0:T(8,128)(2,1)S(1)} %dynamic-slice_bitcast_fusion.refs_0_), channel_id=1, source_target_pairs={{0,2},{1,3},{2,0},{3,1},{4,6},{5,7},{6,4},{7,5},{8,10},{9,11},{10,... | collective-permute-start | bytes 2211848 | tf_op jit(solution)/shard_map/ppermute | solution.py:401
  5.1 1.5 %collective-permute-start = (bf16[1440,256]{1,0:T(8,128)(2,1)S(1)}, bf16[1440,256]{1,0:T(8,128)(2,1)S(1)}, u32[]{:S(2)}, u32[]{:S(2)}) collective-permute-start(bf16[1440,256]{1,0:T(8,128)(2,1)S(1)} %dynamic-slice_bitcast_fusion.refs_0_), channel_id=1, source_target_pairs={{0,1},{1,0},{2,3},{3,2},{4,5},{5,4},{6,7},{7,6},{8,9},{9,8},{10,11... | collective-permute-start | bytes 2211848 | tf_op jit(solution)/shard_map/ppermute | solution.py:401
  7.2 0.0 copy-start.5
  7.2 0.8 copy-done.5
  8.1 0.0 copy-start.6
  8.1 0.8 copy-done.6
  8.8 1.2 %rotate_keys.1 = bf16[16,48,256]{2,1,0:T(8,128)(2,1)} custom-call(s32[1,1]{1,0:T(1,128)S(6)} %copy.18.block_ref, bf16[16,1024]{1,0:T(8,128)(2,1)S(1)} %bitcast.18, bf16[32,1024]{1,0:T(8,128)(2,1)S(1)} %bitcast.17), custom_call_target="tpu_custom_call" | custom-call | tf_op jit(solution)/shard_map/rotate_keys/pallas_call | solution.py:417
  10.0 5.0 %all-to-all-start = ((bf16[16,48,256]{2,1,0:T(8,128)(2,1)}), bf16[16,48,256]{2,1,0:T(8,128)(2,1)S(1)}, u32[]{:S(2)}, u32[]{:S(2)}) async-start(bf16[16,48,256]{2,1,0:T(8,128)(2,1)} %rotate_keys.1), calls=%async_computation | async-start | bytes 786432 | tf_op jit(solution)/shard_map/all_to_all | solution.py:460
  15.0 0.0 copy-start.2
  15.1 0.9 %copy-done.2 = bf16[1,256,256]{2,1,0:T(8,128)(2,1)S(1)} copy-done((bf16[1,256,256]{2,1,0:T(8,128)(2,1)S(1)}, bf16[1,256,256]{2,1,0:T(8,128)(2,1)}, u32[]{:S(2)}) %copy-start.2) | copy-done | bytes 131096
  16.0 0.0 copy-start.3
  16.0 0.9 %copy-done.3 = f32[256,128]{1,0:T(8,128)S(1)} copy-done((f32[256,128]{1,0:T(8,128)S(1)}, f32[256,128]{1,0:T(8,128)}, u32[]{:S(2)}) %copy-start.3) | copy-done | bytes 131096
  16.9 0.0 copy-start.4
  16.9 0.9 %copy-done.4 = bf16[1,16,2880]{2,1,0:T(8,128)(2,1)S(1)} copy-done((bf16[1,16,2880]{2,1,0:T(8,128)(2,1)S(1)}, bf16[1,16,2880]{2,1,0:T(8,128)(2,1)}, u32[]{:S(2)}) %copy-start.4) | copy-done | bytes 92184
  17.7 0.0 copy-start.9
  17.8 0.7 copy-done.9
  18.4 0.0 copy-start.10
  18.4 0.7 copy-done.10
  19.1 1.3 %rotate_queries.1 = (bf16[80,256]{1,0:T(8,128)(2,1)S(1)}, bf16[80,256]{1,0:T(8,128)(2,1)}, bf16[80,256]{1,0:T(8,128)(2,1)}, bf16[80,256]{1,0:T(8,128)(2,1)}, bf16[48,1024]{1,0:T(8,128)(2,1)S(1)}) custom-call(s32[1,2]{1,0:T(1,128)S(1)} %copy-done.9, f32[4]{0:T(128)S(1)} %copy-done.10, f32[256,128]{1,0:T(8,128)S(1)} %copy-done.3, ...), custom_call_target="tpu_custom_call" | custom-call | tf_op jit(solution)/shard_map/rotate_queries/pallas_call | solution.py:430
  20.4 1.9 %collective-permute-start.2 = (bf16[80,256]{1,0:T(8,128)(2,1)}, bf16[80,256]{1,0:T(8,128)(2,1)S(1)}, u32[]{:S(2)}, u32[]{:S(2)}) collective-permute-start(bf16[80,256]{1,0:T(8,128)(2,1)} %get-tuple-element.34), channel_id=1, source_target_pairs={{0,1},{1,0},{2,3},{3,2},{4,5},{5,4},{6,7},{7,6},{8,9},{9,8},{10,11... | collective-permute-start | bytes 122888 | tf_op jit(solution)/shard_map/ppermute | solution.py:401
  22.3 1.5 %collective-permute-start.3 = (bf16[80,256]{1,0:T(8,128)(2,1)}, bf16[80,256]{1,0:T(8,128)(2,1)}, u32[]{:S(2)}, u32[]{:S(2)}) collective-permute-start(bf16[80,256]{1,0:T(8,128)(2,1)} %get-tuple-element.35), channel_id=1, source_target_pairs={{0,2},{1,3},{2,0},{3,1},{4,6},{5,7},{6,4},{7,5},{8,10},{9,11},{10,... | collective-permute-start | bytes 122888 | tf_op jit(solution)/shard_map/ppermute | solution.py:401
  23.8 0.1 collective-permute-start.4
  23.9 0.7 broadcast_in_dim.6.gain_ref
  24.6 0.8 copy.17
  25.3 0.1 reshape.19.names_ref
  25.5 0.0 collective-permute-done.1.bottom_ref.refs_2_
  25.5 2.1 %collective-permute-done.top_ref.refs_1_ = bf16[1440,256]{1,0:T(8,128)(2,1)S(1)} collective-permute-done((bf16[1440,256]{1,0:T(8,128)(2,1)S(1)}, bf16[1440,256]{1,0:T(8,128)(2,1)S(1)}, u32[]{:S(2)}, u32[]{:S(2)}) %collective-permute-start) | collective-permute-done | bytes 737312 | tf_op jit(solution)/shard_map/ppermute | solution.py:401
  27.6 0.9 %split.1 = (bf16[720,256]{1,0:T(8,128)(2,1)}, bf16[720,256]{1,0:T(8,128)(2,1)}) custom-call(bf16[1440,256]{1,0:T(8,128)(2,1)S(1)} %collective-permute-done.top_ref.refs_1_, bf16[1440,256]{1,0:T(8,128)(2,1)S(1)} %collective-permute-done.1.bottom_ref.refs_2_), custom_call_target="tpu_custom_call" | custom-call | tf_op jit(solution)/shard_map/split/pallas_call | solution.py:464
  28.5 0.1 collective-permute-start.5
  28.6 2.0 %collective-permute-start.6 = (bf16[720,256]{1,0:T(8,128)(2,1)}, bf16[720,256]{1,0:T(8,128)(2,1)S(1)}, u32[]{:S(2)}, u32[]{:S(2)}) collective-permute-start(bf16[720,256]{1,0:T(8,128)(2,1)} %get-tuple-element.42), channel_id=1, source_target_pairs={{0,1},{1,0},{2,3},{3,2},{4,5},{5,4},{6,7},{7,6},{8,9},{9,8},{10,11... | collective-permute-start | bytes 1105928 | tf_op jit(solution)/shard_map/ppermute | solution.py:401
  30.6 0.0 collective-permute-done.2.refs_1_
  30.6 0.0 collective-permute-done.3.refs_2_
  30.6 0.0 collective-permute-done.4.refs_3_
  30.6 0.0 all-to-all-done
  30.6 4.7 %attend.1 = (bf16[112,1024]{1,0:T(8,128)(2,1)S(1)}, bf16[768,5760]{1,0:T(8,128)(2,1)S(1)}) custom-call(bf16[80,256]{1,0:T(8,128)(2,1)S(1)} %get-tuple-element.33.refs_0_, bf16[80,256]{1,0:T(8,128)(2,1)S(1)} %collective-permute-done.2.refs_1_, bf16[80,256]{1,0:T(8,128)(2,1)} %collective-permute-done.3.refs_2_, ...), custom_call_target="tpu_custom_call" | custom-call | flops 5000000000 | bytes 15000000 | tf_op jit(solution)/shard_map/attend/pallas_call | solution.py:484
  35.3 2.1 %all_gather.6.att_ref.resid_ref = bf16[224,1024]{1,0:T(8,128)(2,1)S(1)} all-gather(bf16[112,1024]{1,0:T(8,128)(2,1)S(1)} %get-tuple-element.38), channel_id=1, replica_groups=mesh['group'=2,'tensor'=16] {'group'}, dimensions={0}, use_global_device_ids=true | all-gather | bytes 688128 | tf_op jit(solution)/shard_map/all_gather | solution.py:501
  37.4 0.0 collective-permute-done.5.refs_3_
  37.5 0.0 collective-permute-done.6.refs_4_
  37.5 1.0 %project.1 = (f32[32,1440]{1,0:T(8,128)S(1)}, bf16[32,1440]{1,0:T(8,128)(2,1)S(1)}, bf16[32,1440]{1,0:T(8,128)(2,1)S(1)}, bf16[32,1440]{1,0:T(8,128)(2,1)S(1)}) custom-call(bf16[224,1024]{1,0:T(8,128)(2,1)S(1)} %all_gather.6.att_ref.resid_ref, bf16[1440,256]{1,0:T(8,128)(2,1)S(1)} %dynamic-slice_bitcast_fusion.refs_0_, ...), custom_call_target="tpu_custom_call" | custom-call | tf_op jit(solution)/shard_map/project/pallas_call | solution.py:510
  38.5 0.0 copy-start.7
  38.5 0.0 copy-start.8
  38.5 3.7 %collective-permute-start.7 = (bf16[32,1440]{1,0:T(8,128)(2,1)S(1)}, bf16[32,1440]{1,0:T(8,128)(2,1)S(1)}, u32[]{:S(2)}, u32[]{:S(2)}) collective-permute-start(bf16[32,1440]{1,0:T(8,128)(2,1)S(1)} %get-tuple-element.48), channel_id=1, source_target_pairs={{0,12},{1,13},{2,14},{3,15},{4,8},{5,9},{6,10},{7,11},{8,4},{9,5},... | collective-permute-start | bytes 276488 | tf_op jit(solution)/shard_map/ppermute | solution.py:401
  42.1 0.0 collective-permute-start.8
  42.2 0.8 collective-permute-start.9
  42.9 7.9 %load_expert.1.late_ref = bf16[2112,5760]{1,0:T(8,128)(2,1)S(1)} custom-call(bf16[2880,5760]{1,0:T(8,128)(2,1)} %bitcast.20), custom_call_target="tpu_custom_call" | custom-call | bytes 48660480 | tf_op jit(solution)/shard_map/load_expert/pallas_call | solution.py:533
  50.9 0.0 collective-permute-done.7.refs_1_
  50.9 0.0 collective-permute-done.8.refs_2_
  50.9 0.0 collective-permute-done.9.refs_3_
  51.0 2.1 %all_gather.7.sums_ref = f32[64,1440]{1,0:T(8,128)S(1)} all-gather(f32[32,1440]{1,0:T(8,128)S(1)} %sum_planes.1), channel_id=1, replica_groups=mesh['group'=2,'tensor'=16] {'group'}, dimensions={0}, use_global_device_ids=true | all-gather | bytes 552960 | tf_op jit(solution)/shard_map/all_gather | solution.py:549
  53.0 0.0 copy-done.7
  53.0 0.0 copy-done.8
  53.0 0.8 norm_dispatch.1
  53.8 26.9 %all_to_all.10 = bf16[16,8,2880]{2,1,0:T(8,128)(2,1)S(1)} all-to-all(bf16[16,8,2880]{2,1,0:T(8,128)(2,1)S(1)} %bitcast.14), channel_id=1, replica_groups=mesh['group'=2,'tensor'=16] {'tensor'}, dimensions={0} | all-to-all | bytes 1474560 | tf_op jit(solution)/shard_map/all_to_all | solution.py:570
  80.8 0.0 copy-start.1
  80.8 6.0 %experts.1 = bf16[128,2880]{1,0:T(8,128)(2,1)} custom-call(bf16[128,2880]{1,0:T(8,128)(2,1)S(1)} %bitcast.12, bf16[768,5760]{1,0:T(8,128)(2,1)S(1)} %get-tuple-element.58.early_ref, bf16[2112,5760]{1,0:T(8,128)(2,1)S(1)} %load_expert.1.late_ref), custom_call_target="tpu_custom_call" | custom-call | tf_op jit(solution)/shard_map/experts/pallas_call | solution.py:577
  86.8 0.0 copy-done.1
  (2 shorter events, 0.1 us)
Async XLA Ops:
  0.6 1.4 %copy-start = (bf16[256,2880]{0,1:T(8,128)(2,1)S(1)}, bf16[256,2880]{0,1:T(8,128)(2,1)}, u32[]{:S(2)}) copy-start(bf16[256,2880]{0,1:T(8,128)(2,1)} %param.21) | copy-start | bytes 4423684
  2.1 23.4 %collective-permute-start.1 = (bf16[1440,256]{1,0:T(8,128)(2,1)S(1)}, bf16[1440,256]{1,0:T(8,128)(2,1)S(1)}, u32[]{:S(2)}, u32[]{:S(2)}) collective-permute-start(bf16[1440,256]{1,0:T(8,128)(2,1)S(1)} %dynamic-slice_bitcast_fusion.refs_0_), channel_id=1, source_target_pairs={{0,2},{1,3},{2,0},{3,1},{4,6},{5,7},{6,4},{7,5},{8,10},{9,11},{10,... | collective-permute-start | bytes 2211848 | tf_op jit(solution)/shard_map/ppermute | solution.py:401
  5.1 22.5 %collective-permute-start = (bf16[1440,256]{1,0:T(8,128)(2,1)S(1)}, bf16[1440,256]{1,0:T(8,128)(2,1)S(1)}, u32[]{:S(2)}, u32[]{:S(2)}) collective-permute-start(bf16[1440,256]{1,0:T(8,128)(2,1)S(1)} %dynamic-slice_bitcast_fusion.refs_0_), channel_id=1, source_target_pairs={{0,1},{1,0},{2,3},{3,2},{4,5},{5,4},{6,7},{7,6},{8,9},{9,8},{10,11... | collective-permute-start | bytes 2211848 | tf_op jit(solution)/shard_map/ppermute | solution.py:401
  7.2 0.8 copy-start.5
  8.1 0.8 copy-start.6
  10.0 20.5 %all-to-all-start = ((bf16[16,48,256]{2,1,0:T(8,128)(2,1)}), bf16[16,48,256]{2,1,0:T(8,128)(2,1)S(1)}, u32[]{:S(2)}, u32[]{:S(2)}) async-start(bf16[16,48,256]{2,1,0:T(8,128)(2,1)} %rotate_keys.1), calls=%async_computation | async-start | bytes 786432 | tf_op jit(solution)/shard_map/all_to_all | solution.py:460
  15.0 0.9 %copy-start.2 = (bf16[1,256,256]{2,1,0:T(8,128)(2,1)S(1)}, bf16[1,256,256]{2,1,0:T(8,128)(2,1)}, u32[]{:S(2)}) copy-start(bf16[1,256,256]{2,1,0:T(8,128)(2,1)} %param.15) | copy-start | bytes 393220
  16.0 0.9 %copy-start.3 = (f32[256,128]{1,0:T(8,128)S(1)}, f32[256,128]{1,0:T(8,128)}, u32[]{:S(2)}) copy-start(f32[256,128]{1,0:T(8,128)} %constant.18.clone.turn_ref) | copy-start | bytes 393220
  16.9 0.9 %copy-start.4 = (bf16[1,16,2880]{2,1,0:T(8,128)(2,1)S(1)}, bf16[1,16,2880]{2,1,0:T(8,128)(2,1)}, u32[]{:S(2)}) copy-start(bf16[1,16,2880]{2,1,0:T(8,128)(2,1)} %param.14) | copy-start | bytes 276484
  17.7 0.7 copy-start.9
  18.4 0.7 copy-start.10
  20.4 10.2 %collective-permute-start.2 = (bf16[80,256]{1,0:T(8,128)(2,1)}, bf16[80,256]{1,0:T(8,128)(2,1)S(1)}, u32[]{:S(2)}, u32[]{:S(2)}) collective-permute-start(bf16[80,256]{1,0:T(8,128)(2,1)} %get-tuple-element.34), channel_id=1, source_target_pairs={{0,1},{1,0},{2,3},{3,2},{4,5},{5,4},{6,7},{7,6},{8,9},{9,8},{10,11... | collective-permute-start | bytes 122888 | tf_op jit(solution)/shard_map/ppermute | solution.py:401
  22.3 8.3 %collective-permute-start.3 = (bf16[80,256]{1,0:T(8,128)(2,1)}, bf16[80,256]{1,0:T(8,128)(2,1)}, u32[]{:S(2)}, u32[]{:S(2)}) collective-permute-start(bf16[80,256]{1,0:T(8,128)(2,1)} %get-tuple-element.35), channel_id=1, source_target_pairs={{0,2},{1,3},{2,0},{3,1},{4,6},{5,7},{6,4},{7,5},{8,10},{9,11},{10,... | collective-permute-start | bytes 122888 | tf_op jit(solution)/shard_map/ppermute | solution.py:401
  23.8 6.8 %collective-permute-start.4 = (bf16[80,256]{1,0:T(8,128)(2,1)}, bf16[80,256]{1,0:T(8,128)(2,1)}, u32[]{:S(2)}, u32[]{:S(2)}) collective-permute-start(bf16[80,256]{1,0:T(8,128)(2,1)} %get-tuple-element.36), channel_id=1, source_target_pairs={{0,3},{1,2},{2,1},{3,0},{4,7},{5,6},{6,5},{7,4},{8,11},{9,10},{10,... | collective-permute-start | bytes 122888 | tf_op jit(solution)/shard_map/ppermute | solution.py:401
  28.5 9.0 %collective-permute-start.5 = (bf16[720,256]{1,0:T(8,128)(2,1)}, bf16[720,256]{1,0:T(8,128)(2,1)S(1)}, u32[]{:S(2)}, u32[]{:S(2)}) collective-permute-start(bf16[720,256]{1,0:T(8,128)(2,1)} %get-tuple-element.41), channel_id=1, source_target_pairs={{0,2},{1,3},{2,0},{3,1},{4,6},{5,7},{6,4},{7,5},{8,10},{9,11},{10,... | collective-permute-start | bytes 1105928 | tf_op jit(solution)/shard_map/ppermute | solution.py:401
  28.6 8.9 %collective-permute-start.6 = (bf16[720,256]{1,0:T(8,128)(2,1)}, bf16[720,256]{1,0:T(8,128)(2,1)S(1)}, u32[]{:S(2)}, u32[]{:S(2)}) collective-permute-start(bf16[720,256]{1,0:T(8,128)(2,1)} %get-tuple-element.42), channel_id=1, source_target_pairs={{0,1},{1,0},{2,3},{3,2},{4,5},{5,4},{6,7},{7,6},{8,9},{9,8},{10,11... | collective-permute-start | bytes 1105928 | tf_op jit(solution)/shard_map/ppermute | solution.py:401
  38.5 14.6 %copy-start.7 = (bf16[128,32]{1,0:T(8,128)(2,1)S(1)}, bf16[128,32]{1,0:T(8,128)(2,1)}, u32[]{:S(2)}) copy-start(bf16[128,32]{1,0:T(8,128)(2,1)} %constant.20.clone.source_ref) | copy-start | bytes 24580
  38.5 14.6 %copy-start.8 = (bf16[128,128]{1,0:T(8,128)(2,1)S(1)}, bf16[128,128]{1,0:T(8,128)(2,1)}, u32[]{:S(2)}) copy-start(bf16[128,128]{1,0:T(8,128)(2,1)} %constant.19.clone.earlier_ref) | copy-start | bytes 98308
  38.5 12.4 %collective-permute-start.7 = (bf16[32,1440]{1,0:T(8,128)(2,1)S(1)}, bf16[32,1440]{1,0:T(8,128)(2,1)S(1)}, u32[]{:S(2)}, u32[]{:S(2)}) collective-permute-start(bf16[32,1440]{1,0:T(8,128)(2,1)S(1)} %get-tuple-element.48), channel_id=1, source_target_pairs={{0,12},{1,13},{2,14},{3,15},{4,8},{5,9},{6,10},{7,11},{8,4},{9,5},... | collective-permute-start | bytes 276488 | tf_op jit(solution)/shard_map/ppermute | solution.py:401
  42.1 8.7 %collective-permute-start.8 = (bf16[32,1440]{1,0:T(8,128)(2,1)S(1)}, bf16[32,1440]{1,0:T(8,128)(2,1)S(1)}, u32[]{:S(2)}, u32[]{:S(2)}) collective-permute-start(bf16[32,1440]{1,0:T(8,128)(2,1)S(1)} %get-tuple-element.49), channel_id=1, source_target_pairs={{0,8},{1,9},{2,10},{3,11},{4,12},{5,13},{6,14},{7,15},{8,0},{9,1},... | collective-permute-start | bytes 276488 | tf_op jit(solution)/shard_map/ppermute | solution.py:401
  42.2 8.7 %collective-permute-start.9 = (bf16[32,1440]{1,0:T(8,128)(2,1)S(1)}, bf16[32,1440]{1,0:T(8,128)(2,1)S(1)}, u32[]{:S(2)}, u32[]{:S(2)}) collective-permute-start(bf16[32,1440]{1,0:T(8,128)(2,1)S(1)} %get-tuple-element.50), channel_id=1, source_target_pairs={{0,4},{1,5},{2,6},{3,7},{4,0},{5,1},{6,2},{7,3},{8,12},{9,13},{10,... | collective-permute-start | bytes 276488 | tf_op jit(solution)/shard_map/ppermute | solution.py:401
  80.8 6.0 %copy-start.1 = (bf16[256,2880]{0,1:T(8,128)(2,1)S(1)}, bf16[256,2880]{0,1:T(8,128)(2,1)}, u32[]{:S(2)}) copy-start(bf16[256,2880]{0,1:T(8,128)(2,1)} %param.21) | copy-start | bytes 4423684

commit v4 on v3

--- a/solution.py
+++ b/solution.py
@@ -32,7 +32,7 @@
         out_specs=space if single else [space] * len(outs),
         scratch_shapes=list(scratch),
         name=name,
-        compiler_params=pltpu.CompilerParams(vmem_limit_bytes=limit * 1024 * 1024),
+        compiler_params=pltpu.CompilerParams(vmem_limit_bytes=int(limit * 1024 * 1024)),
         cost_estimate=pl.CostEstimate(flops=flops, bytes_accessed=moved, transcendentals=0),
     )
 
@@ -151,23 +151,10 @@
 
 def attend_kernel(blocks, requests, tok_dev, kv_rows, *refs):
     q_refs, kv_ref, w_ref = refs[:blocks], refs[blocks], refs[blocks + 1]
-    resid_refs, (out_ref, early_ref, own_ref, sems) = refs[blocks + 2 : -4], refs[-4:]
-    own = pltpu.make_async_copy(q_refs[0], own_ref, sems.at[0])
-    own.start()
-    rows = own_ref.shape[0] - 16
-    loads = [
-        pltpu.make_async_copy(resid_ref, out_ref.at[pl.ds(rows, resid_ref.shape[0])], sems.at[1])
-        for resid_ref in resid_refs
-    ]
-    loads.append(
-        pltpu.make_async_copy(w_ref.at[pl.ds(0, early_ref.shape[0])], early_ref, sems.at[2])
-    )
-    for load in loads:
-        load.start()
-    q_refs = [own_ref, *q_refs[1:]]
-    told_ref = q_refs[-1]
-    if blocks == 1:
-        own.wait()
+    resid_refs, (out_ref, early_ref, sem) = refs[blocks + 2 : -3], refs[-3:]
+    load = pltpu.make_async_copy(w_ref.at[pl.ds(0, early_ref.shape[0])], early_ref, sem)
+    load.start()
+    rows = q_refs[0].shape[0] - 16
     inner = lax.axis_index("tensor") & (PLANE - 1)
     plane = lax.axis_index("tensor") >> log2(PLANE)
     low = lax.broadcasted_iota(jnp.int32, (kv_ref.shape[0], LANES), 1) < HD
@@ -181,13 +168,12 @@
 
     keys = doubled(kv_ref[:, :LANES].astype(F32))
     vals = doubled(kv_ref[:, LANES:].astype(F32))
-    row = lax.broadcasted_iota(jnp.int32, (2 * rows, 1), 0)
-    row = row & (rows - 1)
+    row = lax.broadcasted_iota(jnp.int32, (rows, 1), 0)
     shift = tok_dev.bit_length() - 1
     slot = (((row >> shift) ^ plane) * PLANE + inner) * tok_dev + (row & (tok_dev - 1))
     request = slot >> (MAXLEN.bit_length() - 1)
     length = jnp.zeros_like(slot)
-    told = told_ref[rows : rows + 16, :LANES].astype(F32)
+    told = q_refs[0][rows : rows + 16, :LANES].astype(F32)
     for number in range(requests):
         live = told[3 + number : 4 + number, 0:1].astype(jnp.int32)
         length = jnp.where(request == number, live, length)
@@ -199,37 +185,41 @@
     key_slot = jnp.where(inside < 0, -1, source * tok_dev + inside)
     visible = (key_slot < 0) | ((key_slot >= base) & (key_slot <= last))
     left = lax.broadcasted_iota(jnp.int32, (rows, LANES), 1) < HD
-    for block in reversed(range(blocks)):
-        if block == 0 and blocks > 1:
-            own.wait()
-        for pair in range(2):
-            half = block // 2 if blocks == PLANE else pair
-            span = slice(pair * LANES, (pair + 1) * LANES)
-            query = q_refs[block][:rows, span].astype(F32) * 0.125
-            stack = jnp.concatenate(
-                [jnp.where(left, query, 0.0), jnp.where(left, 0.0, query)], axis=0
+    spans = [slice(pair * LANES, (pair + 1) * LANES) for pair in range(2)]
+    if blocks == PLANE:
+        sets = [[(block, pair) for block in some for pair in range(2)] for some in ([0], [1], [2], [3])]
+    else:
+        sets = [[(0, pair)] for pair in range(2)]
+    for places in sets:
+        half = places[0][0] // 2 if blocks == PLANE else places[0][1]
+        stack, sink = [], []
+        for block, pair in places:
+            query = q_refs[block][:rows, spans[pair]].astype(F32) * 0.125
+            stack += [jnp.where(left, query, 0.0), jnp.where(left, 0.0, query)]
+            terms = q_refs[block][rows : rows + 16, spans[pair]].astype(F32)
+            terms = terms[0:1] + terms[1:2] + terms[2:3]
+            sink += [jnp.broadcast_to(terms[:, at : at + 1], (rows, 1)) for at in (0, HD)]
+        scores = lax.dot_general(
+            jnp.concatenate(stack, axis=0).astype(BF16),
+            keys[half],
+            (((1,), (1,)), ((), ())),
+            preferred_element_type=F32,
+        )
+        sink = jnp.concatenate(sink, axis=0)
+        scores = jnp.where(jnp.concatenate([visible] * len(stack), axis=0), scores, -1e30)
+        top = jnp.maximum(jnp.max(scores, axis=1, keepdims=True), sink)
+        weights = jnp.exp(scores - top)
+        total = jnp.sum(weights, axis=1, keepdims=True) + jnp.exp(sink - top)
+        got = jnp.dot(weights.astype(BF16), vals[half], preferred_element_type=F32) / total
+        for number, (block, pair) in enumerate(places):
+            at = block * 2 * LANES + pair * LANES
+            first = 2 * number * rows
+            out_ref[:rows, at : at + LANES] = jnp.where(
+                left, got[first : first + rows], got[first + rows : first + 2 * rows]
             ).astype(BF16)
-            scores = lax.dot_general(
-                stack, keys[half], (((1,), (1,)), ((), ())), preferred_element_type=F32
-            )
-            scores = jnp.where(visible, scores, -1e30)
-            terms = q_refs[block][rows : rows + 16, span].astype(F32)
-            sinks = terms[0:1] + terms[1:2] + terms[2:3]
-            sink = jnp.concatenate(
-                [
-                    jnp.broadcast_to(sinks[:, 0:1], (rows, 1)),
-                    jnp.broadcast_to(sinks[:, HD : HD + 1], (rows, 1)),
-                ],
-                axis=0,
-            )
-            top = jnp.maximum(jnp.max(scores, axis=1, keepdims=True), sink)
-            weights = jnp.exp(scores - top)
-            total = jnp.sum(weights, axis=1, keepdims=True) + jnp.exp(sink - top)
-            got = jnp.dot(weights.astype(BF16), vals[half], preferred_element_type=F32) / total
-            at = block * 2 * LANES + pair * LANES
-            out_ref[:rows, at : at + LANES] = jnp.where(left, got[:rows], got[rows:]).astype(BF16)
-    for load in loads:
-        load.wait()
+    for resid_ref in resid_refs:
+        out_ref[rows:, :] = resid_ref[...]
+    load.wait()
 
 
 def project_kernel(tok_dev, groups, att_ref, *refs):
@@ -424,6 +414,7 @@
             pltpu.VMEM(prefix_kv.shape[1:], BF16),
             pltpu.SemaphoreType.DMA((2,)),
         ],
+        limit=60.5,
     )(block_map, suffix_kv[0], prefix_kv[0])
     if aligned:
         extra = -(-width // (PLANE * query_cols)) * tok_dev
@@ -487,14 +478,10 @@
             jax.ShapeDtypeStruct((slots_here + extra, PLANE * query_cols), BF16),
             jax.ShapeDtypeStruct((early_rows, columns), BF16),
         ],
-        [ANY] + [VMEM] * len(received) + [ANY] * (1 + len(packed)),
+        [VMEM] * (1 + len(received)) + [ANY] + [VMEM] * len(packed),
         "attend",
-        scratch=[
-            pltpu.VMEM(received[0].shape, BF16),
-            pltpu.SemaphoreType.DMA((3,)),
-        ],
+        scratch=[pltpu.SemaphoreType.DMA],
         limit=26,
-        moved=15000000,
         flops=5000000000,
     )(*received, kv, w_experts[0], *packed)
 

time: 87.5 us -> 87.5 us (level)
  local copies, waits for them, and re-layouts: 8.63 us -> 7.04 us
    unnamed x23 -> x19, local copies, waits for them, and re-layouts: 7.76 us -> 6.16 us
  transfers between devices with their start and end apart: 11 -> 11, of which waited for: 1 -> 2; matrix products, arithmetic and copies ran while one was open for 2% -> 2% of each run, Pallas kernels for 18% -> 19%
where the time goes in v4:
time: 87.5 us; the launch traced here: 86.8 us
  blocking collectives  31.5 us (36%)
  Pallas kernels  24.3 us (28%)
  starting transfers between devices  19.5 us (22%)
  local copies, waits for them, and re-layouts  7.04 us (8%)
  waiting for transfers between devices  3.02 us (3%)
  between operations  1.43 us (2%)
    all_to_all x1, blocking collectives, local(): lax.all_to_all(outgoing.reshape(tensors, slot_cap, width), 'tensor', spli...  27.3 us
    ppermute x10, starting transfers between devices, swap(): lax.ppermute(values, 'tensor', [(i, i ^ bits) for i in range(tensors)])  14.5 us
    pallas_call x1, Pallas kernels, local(): call(load_kernel, jax.ShapeDtypeStruct((width - early_rows, columns), BF1...  7.93 us
    unnamed x19, local copies, waits for them, and re-layouts  6.16 us
    pallas_call x1, Pallas kernels, local(): call(expert_kernel, jax.ShapeDtypeStruct((tensors * slot_cap, columns //...  6.04 us
    all_to_all x1, starting transfers between devices, local(): lax.all_to_all(owned, 'tensor', split_axis=0, concat_axis=0, tiled=True)  4.99 us
    pallas_call x1, Pallas kernels, local(): call(functools.partial(attend_kernel, len(received), lengths.shape[1], to...  4.33 us
    ppermute x10, waiting for transfers between devices, swap(): lax.ppermute(values, 'tensor', [(i, i ^ bits) for i in range(tensors)])  3.02 us
  transfers between devices with their start and end apart: 11, of which 2 were waited for; matrix products, arithmetic and copies ran while one was open for 2% of the time, Pallas kernels for 19%

profile of v4, /device:TPU:0, one launch (start us, length us, event | category | flops | bytes accessed | tf_op | source)
XLA Modules:
  0.0 86.8 jit_solution(6708755519074219606)
XLA Ops:
  0.6 0.0 copy-start
  0.7 1.4 %copy-done = bf16[256,2880]{0,1:T(8,128)(2,1)S(1)} copy-done((bf16[256,2880]{0,1:T(8,128)(2,1)S(1)}, bf16[256,2880]{0,1:T(8,128)(2,1)}, u32[]{:S(2)}) %copy-start) | copy-done | bytes 1474584
  2.1 3.0 %collective-permute-start.1 = (bf16[1440,256]{1,0:T(8,128)(2,1)S(1)}, bf16[1440,256]{1,0:T(8,128)(2,1)S(1)}, u32[]{:S(2)}, u32[]{:S(2)}) collective-permute-start(bf16[1440,256]{1,0:T(8,128)(2,1)S(1)} %dynamic-slice_bitcast_fusion.refs_0_), channel_id=1, source_target_pairs={{0,2},{1,3},{2,0},{3,1},{4,6},{5,7},{6,4},{7,5},{8,10},{9,11},{10,... | collective-permute-start | bytes 2211848 | tf_op jit(solution)/shard_map/ppermute | solution.py:391
  5.1 1.5 %collective-permute-start = (bf16[1440,256]{1,0:T(8,128)(2,1)S(1)}, bf16[1440,256]{1,0:T(8,128)(2,1)S(1)}, u32[]{:S(2)}, u32[]{:S(2)}) collective-permute-start(bf16[1440,256]{1,0:T(8,128)(2,1)S(1)} %dynamic-slice_bitcast_fusion.refs_0_), channel_id=1, source_target_pairs={{0,1},{1,0},{2,3},{3,2},{4,5},{5,4},{6,7},{7,6},{8,9},{9,8},{10,11... | collective-permute-start | bytes 2211848 | tf_op jit(solution)/shard_map/ppermute | solution.py:391
  7.2 1.9 %rotate_keys.1 = bf16[16,48,256]{2,1,0:T(8,128)(2,1)} custom-call(s32[1,1]{1,0:T(1,128)S(6)} %copy.18.block_ref, bf16[16,1024]{1,0:T(8,128)(2,1)} %bitcast.21, bf16[32,1024]{1,0:T(8,128)(2,1)} %bitcast.20), custom_call_target="tpu_custom_call" | custom-call | tf_op jit(solution)/shard_map/rotate_keys/pallas_call | solution.py:407
  9.2 5.0 %all-to-all-start = ((bf16[16,48,256]{2,1,0:T(8,128)(2,1)}), bf16[16,48,256]{2,1,0:T(8,128)(2,1)S(1)}, u32[]{:S(2)}, u32[]{:S(2)}) async-start(bf16[16,48,256]{2,1,0:T(8,128)(2,1)} %rotate_keys.1), calls=%async_computation | async-start | bytes 786432 | tf_op jit(solution)/shard_map/all_to_all | solution.py:451
  14.2 0.0 copy-start.2
  14.2 0.9 %copy-done.2 = bf16[1,256,256]{2,1,0:T(8,128)(2,1)S(1)} copy-done((bf16[1,256,256]{2,1,0:T(8,128)(2,1)S(1)}, bf16[1,256,256]{2,1,0:T(8,128)(2,1)}, u32[]{:S(2)}) %copy-start.2) | copy-done | bytes 131096
  15.1 0.0 copy-start.3
  15.1 0.9 %copy-done.3 = f32[256,128]{1,0:T(8,128)S(1)} copy-done((f32[256,128]{1,0:T(8,128)S(1)}, f32[256,128]{1,0:T(8,128)}, u32[]{:S(2)}) %copy-start.3) | copy-done | bytes 131096
  16.0 0.0 copy-start.4
  16.0 0.9 %copy-done.4 = bf16[1,16,2880]{2,1,0:T(8,128)(2,1)S(1)} copy-done((bf16[1,16,2880]{2,1,0:T(8,128)(2,1)S(1)}, bf16[1,16,2880]{2,1,0:T(8,128)(2,1)}, u32[]{:S(2)}) %copy-start.4) | copy-done | bytes 92184
  16.9 0.0 copy-start.7
  16.9 0.7 copy-done.7
  17.5 0.0 copy-start.8
  17.6 0.7 copy-done.8
  18.2 1.3 %rotate_queries.1 = (bf16[80,256]{1,0:T(8,128)(2,1)S(1)}, bf16[80,256]{1,0:T(8,128)(2,1)}, bf16[80,256]{1,0:T(8,128)(2,1)}, bf16[80,256]{1,0:T(8,128)(2,1)}, bf16[48,1024]{1,0:T(8,128)(2,1)S(1)}) custom-call(s32[1,2]{1,0:T(1,128)S(1)} %copy-done.7, f32[4]{0:T(128)S(1)} %copy-done.8, f32[256,128]{1,0:T(8,128)S(1)} %copy-done.3, ...), custom_call_target="tpu_custom_call" | custom-call | tf_op jit(solution)/shard_map/rotate_queries/pallas_call | solution.py:421
  19.5 1.9 %collective-permute-start.2 = (bf16[80,256]{1,0:T(8,128)(2,1)}, bf16[80,256]{1,0:T(8,128)(2,1)S(1)}, u32[]{:S(2)}, u32[]{:S(2)}) collective-permute-start(bf16[80,256]{1,0:T(8,128)(2,1)} %get-tuple-element.34), channel_id=1, source_target_pairs={{0,1},{1,0},{2,3},{3,2},{4,5},{5,4},{6,7},{7,6},{8,9},{9,8},{10,11... | collective-permute-start | bytes 122888 | tf_op jit(solution)/shard_map/ppermute | solution.py:391
  21.4 1.5 %collective-permute-start.3 = (bf16[80,256]{1,0:T(8,128)(2,1)}, bf16[80,256]{1,0:T(8,128)(2,1)}, u32[]{:S(2)}, u32[]{:S(2)}) collective-permute-start(bf16[80,256]{1,0:T(8,128)(2,1)} %get-tuple-element.35), channel_id=1, source_target_pairs={{0,2},{1,3},{2,0},{3,1},{4,6},{5,7},{6,4},{7,5},{8,10},{9,11},{10,... | collective-permute-start | bytes 122888 | tf_op jit(solution)/shard_map/ppermute | solution.py:391
  22.9 0.1 collective-permute-start.4
  23.0 0.7 broadcast_in_dim.6.gain_ref
  23.7 0.8 copy.17
  24.5 0.1 reshape.19.names_ref
  24.6 0.8 collective-permute-done.1.bottom_ref.refs_2_
  25.4 2.2 %collective-permute-done.top_ref.refs_1_ = bf16[1440,256]{1,0:T(8,128)(2,1)S(1)} collective-permute-done((bf16[1440,256]{1,0:T(8,128)(2,1)S(1)}, bf16[1440,256]{1,0:T(8,128)(2,1)S(1)}, u32[]{:S(2)}, u32[]{:S(2)}) %collective-permute-start) | collective-permute-done | bytes 737312 | tf_op jit(solution)/shard_map/ppermute | solution.py:391
  27.6 0.9 %split.1 = (bf16[720,256]{1,0:T(8,128)(2,1)}, bf16[720,256]{1,0:T(8,128)(2,1)}) custom-call(bf16[1440,256]{1,0:T(8,128)(2,1)S(1)} %collective-permute-done.top_ref.refs_1_, bf16[1440,256]{1,0:T(8,128)(2,1)S(1)} %collective-permute-done.1.bottom_ref.refs_2_), custom_call_target="tpu_custom_call" | custom-call | tf_op jit(solution)/shard_map/split/pallas_call | solution.py:455
  28.5 0.2 collective-permute-start.5
  28.7 1.9 %collective-permute-start.6 = (bf16[720,256]{1,0:T(8,128)(2,1)}, bf16[720,256]{1,0:T(8,128)(2,1)S(1)}, u32[]{:S(2)}, u32[]{:S(2)}) collective-permute-start(bf16[720,256]{1,0:T(8,128)(2,1)} %get-tuple-element.42), channel_id=1, source_target_pairs={{0,1},{1,0},{2,3},{3,2},{4,5},{5,4},{6,7},{7,6},{8,9},{9,8},{10,11... | collective-permute-start | bytes 1105928 | tf_op jit(solution)/shard_map/ppermute | solution.py:391
  30.6 0.0 collective-permute-done.2.refs_1_
  30.6 0.0 collective-permute-done.3.refs_2_
  30.6 0.0 collective-permute-done.4.refs_3_
  30.6 0.0 all-to-all-done
  30.6 4.3 %attend.1 = (bf16[112,1024]{1,0:T(8,128)(2,1)S(1)}, bf16[768,5760]{1,0:T(8,128)(2,1)S(1)}) custom-call(bf16[80,256]{1,0:T(8,128)(2,1)S(1)} %get-tuple-element.33.refs_0_, bf16[80,256]{1,0:T(8,128)(2,1)S(1)} %collective-permute-done.2.refs_1_, bf16[80,256]{1,0:T(8,128)(2,1)} %collective-permute-done.3.refs_2_, ...), custom_call_target="tpu_custom_call" | custom-call | flops 5000000000 | tf_op jit(solution)/shard_map/attend/pallas_call | solution.py:475
  34.9 2.1 %all_gather.6.att_ref.resid_ref = bf16[224,1024]{1,0:T(8,128)(2,1)S(1)} all-gather(bf16[112,1024]{1,0:T(8,128)(2,1)S(1)} %get-tuple-element.38), channel_id=1, replica_groups=mesh['group'=2,'tensor'=16] {'group'}, dimensions={0}, use_global_device_ids=true | all-gather | bytes 688128 | tf_op jit(solution)/shard_map/all_gather | solution.py:488
  37.1 0.0 collective-permute-done.5.refs_3_
  37.1 0.0 collective-permute-done.6.refs_4_
  37.1 1.0 %project.1 = (f32[32,1440]{1,0:T(8,128)S(1)}, bf16[32,1440]{1,0:T(8,128)(2,1)S(1)}, bf16[32,1440]{1,0:T(8,128)(2,1)S(1)}, bf16[32,1440]{1,0:T(8,128)(2,1)S(1)}) custom-call(bf16[224,1024]{1,0:T(8,128)(2,1)S(1)} %all_gather.6.att_ref.resid_ref, bf16[1440,256]{1,0:T(8,128)(2,1)S(1)} %dynamic-slice_bitcast_fusion.refs_0_, ...), custom_call_target="tpu_custom_call" | custom-call | tf_op jit(solution)/shard_map/project/pallas_call | solution.py:497
  38.1 0.0 copy-start.5
  38.1 0.0 copy-start.6
  38.1 3.7 %collective-permute-start.7 = (bf16[32,1440]{1,0:T(8,128)(2,1)S(1)}, bf16[32,1440]{1,0:T(8,128)(2,1)S(1)}, u32[]{:S(2)}, u32[]{:S(2)}) collective-permute-start(bf16[32,1440]{1,0:T(8,128)(2,1)S(1)} %get-tuple-element.48), channel_id=1, source_target_pairs={{0,12},{1,13},{2,14},{3,15},{4,8},{5,9},{6,10},{7,11},{8,4},{9,5},... | collective-permute-start | bytes 276488 | tf_op jit(solution)/shard_map/ppermute | solution.py:391
  41.8 0.0 collective-permute-start.8
  41.8 0.8 collective-permute-start.9
  42.6 7.9 %load_expert.1.late_ref = bf16[2112,5760]{1,0:T(8,128)(2,1)S(1)} custom-call(bf16[2880,5760]{1,0:T(8,128)(2,1)} %bitcast.18), custom_call_target="tpu_custom_call" | custom-call | bytes 48660480 | tf_op jit(solution)/shard_map/load_expert/pallas_call | solution.py:520
  50.5 0.0 collective-permute-done.7.refs_1_
  50.5 0.0 collective-permute-done.8.refs_2_
  50.5 0.0 collective-permute-done.9.refs_3_
  50.6 2.1 %all_gather.7.sums_ref = f32[64,1440]{1,0:T(8,128)S(1)} all-gather(f32[32,1440]{1,0:T(8,128)S(1)} %sum_planes.1), channel_id=1, replica_groups=mesh['group'=2,'tensor'=16] {'group'}, dimensions={0}, use_global_device_ids=true | all-gather | bytes 552960 | tf_op jit(solution)/shard_map/all_gather | solution.py:536
  52.7 0.0 copy-done.5
  52.7 0.0 copy-done.6
  52.7 0.8 norm_dispatch.1
  53.5 27.3 %all_to_all.10 = bf16[16,8,2880]{2,1,0:T(8,128)(2,1)S(1)} all-to-all(bf16[16,8,2880]{2,1,0:T(8,128)(2,1)S(1)} %bitcast.14), channel_id=1, replica_groups=mesh['group'=2,'tensor'=16] {'tensor'}, dimensions={0} | all-to-all | bytes 1474560 | tf_op jit(solution)/shard_map/all_to_all | solution.py:557
  80.8 0.0 copy-start.1
  80.8 6.0 %experts.1 = bf16[128,2880]{1,0:T(8,128)(2,1)} custom-call(bf16[128,2880]{1,0:T(8,128)(2,1)S(1)} %bitcast.12, bf16[768,5760]{1,0:T(8,128)(2,1)S(1)} %get-tuple-element.58.early_ref, bf16[2112,5760]{1,0:T(8,128)(2,1)S(1)} %load_expert.1.late_ref), custom_call_target="tpu_custom_call" | custom-call | tf_op jit(solution)/shard_map/experts/pallas_call | solution.py:564
  86.8 0.0 copy-done.1
  (2 shorter events, 0.1 us)
Async XLA Ops:
  0.6 1.4 %copy-start = (bf16[256,2880]{0,1:T(8,128)(2,1)S(1)}, bf16[256,2880]{0,1:T(8,128)(2,1)}, u32[]{:S(2)}) copy-start(bf16[256,2880]{0,1:T(8,128)(2,1)} %param.21) | copy-start | bytes 4423684
  2.1 23.4 %collective-permute-start.1 = (bf16[1440,256]{1,0:T(8,128)(2,1)S(1)}, bf16[1440,256]{1,0:T(8,128)(2,1)S(1)}, u32[]{:S(2)}, u32[]{:S(2)}) collective-permute-start(bf16[1440,256]{1,0:T(8,128)(2,1)S(1)} %dynamic-slice_bitcast_fusion.refs_0_), channel_id=1, source_target_pairs={{0,2},{1,3},{2,0},{3,1},{4,6},{5,7},{6,4},{7,5},{8,10},{9,11},{10,... | collective-permute-start | bytes 2211848 | tf_op jit(solution)/shard_map/ppermute | solution.py:391
  5.1 22.5 %collective-permute-start = (bf16[1440,256]{1,0:T(8,128)(2,1)S(1)}, bf16[1440,256]{1,0:T(8,128)(2,1)S(1)}, u32[]{:S(2)}, u32[]{:S(2)}) collective-permute-start(bf16[1440,256]{1,0:T(8,128)(2,1)S(1)} %dynamic-slice_bitcast_fusion.refs_0_), channel_id=1, source_target_pairs={{0,1},{1,0},{2,3},{3,2},{4,5},{5,4},{6,7},{7,6},{8,9},{9,8},{10,11... | collective-permute-start | bytes 2211848 | tf_op jit(solution)/shard_map/ppermute | solution.py:391
  9.2 21.4 %all-to-all-start = ((bf16[16,48,256]{2,1,0:T(8,128)(2,1)}), bf16[16,48,256]{2,1,0:T(8,128)(2,1)S(1)}, u32[]{:S(2)}, u32[]{:S(2)}) async-start(bf16[16,48,256]{2,1,0:T(8,128)(2,1)} %rotate_keys.1), calls=%async_computation | async-start | bytes 786432 | tf_op jit(solution)/shard_map/all_to_all | solution.py:451
  14.2 0.9 %copy-start.2 = (bf16[1,256,256]{2,1,0:T(8,128)(2,1)S(1)}, bf16[1,256,256]{2,1,0:T(8,128)(2,1)}, u32[]{:S(2)}) copy-start(bf16[1,256,256]{2,1,0:T(8,128)(2,1)} %param.15) | copy-start | bytes 393220
  15.1 0.9 %copy-start.3 = (f32[256,128]{1,0:T(8,128)S(1)}, f32[256,128]{1,0:T(8,128)}, u32[]{:S(2)}) copy-start(f32[256,128]{1,0:T(8,128)} %constant.18.clone.turn_ref) | copy-start | bytes 393220
  16.0 0.9 %copy-start.4 = (bf16[1,16,2880]{2,1,0:T(8,128)(2,1)S(1)}, bf16[1,16,2880]{2,1,0:T(8,128)(2,1)}, u32[]{:S(2)}) copy-start(bf16[1,16,2880]{2,1,0:T(8,128)(2,1)} %param.14) | copy-start | bytes 276484
  16.9 0.7 copy-start.7
  17.5 0.7 copy-start.8
  19.5 11.1 %collective-permute-start.2 = (bf16[80,256]{1,0:T(8,128)(2,1)}, bf16[80,256]{1,0:T(8,128)(2,1)S(1)}, u32[]{:S(2)}, u32[]{:S(2)}) collective-permute-start(bf16[80,256]{1,0:T(8,128)(2,1)} %get-tuple-element.34), channel_id=1, source_target_pairs={{0,1},{1,0},{2,3},{3,2},{4,5},{5,4},{6,7},{7,6},{8,9},{9,8},{10,11... | collective-permute-start | bytes 122888 | tf_op jit(solution)/shard_map/ppermute | solution.py:391
  21.4 9.1 %collective-permute-start.3 = (bf16[80,256]{1,0:T(8,128)(2,1)}, bf16[80,256]{1,0:T(8,128)(2,1)}, u32[]{:S(2)}, u32[]{:S(2)}) collective-permute-start(bf16[80,256]{1,0:T(8,128)(2,1)} %get-tuple-element.35), channel_id=1, source_target_pairs={{0,2},{1,3},{2,0},{3,1},{4,6},{5,7},{6,4},{7,5},{8,10},{9,11},{10,... | collective-permute-start | bytes 122888 | tf_op jit(solution)/shard_map/ppermute | solution.py:391
  22.9 7.7 %collective-permute-start.4 = (bf16[80,256]{1,0:T(8,128)(2,1)}, bf16[80,256]{1,0:T(8,128)(2,1)}, u32[]{:S(2)}, u32[]{:S(2)}) collective-permute-start(bf16[80,256]{1,0:T(8,128)(2,1)} %get-tuple-element.36), channel_id=1, source_target_pairs={{0,3},{1,2},{2,1},{3,0},{4,7},{5,6},{6,5},{7,4},{8,11},{9,10},{10,... | collective-permute-start | bytes 122888 | tf_op jit(solution)/shard_map/ppermute | solution.py:391
  28.5 8.6 %collective-permute-start.5 = (bf16[720,256]{1,0:T(8,128)(2,1)}, bf16[720,256]{1,0:T(8,128)(2,1)S(1)}, u32[]{:S(2)}, u32[]{:S(2)}) collective-permute-start(bf16[720,256]{1,0:T(8,128)(2,1)} %get-tuple-element.41), channel_id=1, source_target_pairs={{0,2},{1,3},{2,0},{3,1},{4,6},{5,7},{6,4},{7,5},{8,10},{9,11},{10,... | collective-permute-start | bytes 1105928 | tf_op jit(solution)/shard_map/ppermute | solution.py:391
  28.7 8.4 %collective-permute-start.6 = (bf16[720,256]{1,0:T(8,128)(2,1)}, bf16[720,256]{1,0:T(8,128)(2,1)S(1)}, u32[]{:S(2)}, u32[]{:S(2)}) collective-permute-start(bf16[720,256]{1,0:T(8,128)(2,1)} %get-tuple-element.42), channel_id=1, source_target_pairs={{0,1},{1,0},{2,3},{3,2},{4,5},{5,4},{6,7},{7,6},{8,9},{9,8},{10,11... | collective-permute-start | bytes 1105928 | tf_op jit(solution)/shard_map/ppermute | solution.py:391
  38.1 14.6 %copy-start.5 = (bf16[128,32]{1,0:T(8,128)(2,1)S(1)}, bf16[128,32]{1,0:T(8,128)(2,1)}, u32[]{:S(2)}) copy-start(bf16[128,32]{1,0:T(8,128)(2,1)} %constant.20.clone.source_ref) | copy-start | bytes 24580
  38.1 14.6 %copy-start.6 = (bf16[128,128]{1,0:T(8,128)(2,1)S(1)}, bf16[128,128]{1,0:T(8,128)(2,1)}, u32[]{:S(2)}) copy-start(bf16[128,128]{1,0:T(8,128)(2,1)} %constant.19.clone.earlier_ref) | copy-start | bytes 98308
  38.1 12.4 %collective-permute-start.7 = (bf16[32,1440]{1,0:T(8,128)(2,1)S(1)}, bf16[32,1440]{1,0:T(8,128)(2,1)S(1)}, u32[]{:S(2)}, u32[]{:S(2)}) collective-permute-start(bf16[32,1440]{1,0:T(8,128)(2,1)S(1)} %get-tuple-element.48), channel_id=1, source_target_pairs={{0,12},{1,13},{2,14},{3,15},{4,8},{5,9},{6,10},{7,11},{8,4},{9,5},... | collective-permute-start | bytes 276488 | tf_op jit(solution)/shard_map/ppermute | solution.py:391
  41.8 8.7 %collective-permute-start.8 = (bf16[32,1440]{1,0:T(8,128)(2,1)S(1)}, bf16[32,1440]{1,0:T(8,128)(2,1)S(1)}, u32[]{:S(2)}, u32[]{:S(2)}) collective-permute-start(bf16[32,1440]{1,0:T(8,128)(2,1)S(1)} %get-tuple-element.49), channel_id=1, source_target_pairs={{0,8},{1,9},{2,10},{3,11},{4,12},{5,13},{6,14},{7,15},{8,0},{9,1},... | collective-permute-start | bytes 276488 | tf_op jit(solution)/shard_map/ppermute | solution.py:391
  41.8 8.7 %collective-permute-start.9 = (bf16[32,1440]{1,0:T(8,128)(2,1)S(1)}, bf16[32,1440]{1,0:T(8,128)(2,1)S(1)}, u32[]{:S(2)}, u32[]{:S(2)}) collective-permute-start(bf16[32,1440]{1,0:T(8,128)(2,1)S(1)} %get-tuple-element.50), channel_id=1, source_target_pairs={{0,4},{1,5},{2,6},{3,7},{4,0},{5,1},{6,2},{7,3},{8,12},{9,13},{10,... | collective-permute-start | bytes 276488 | tf_op jit(solution)/shard_map/ppermute | solution.py:391
  80.8 6.0 %copy-start.1 = (bf16[256,2880]{0,1:T(8,128)(2,1)S(1)}, bf16[256,2880]{0,1:T(8,128)(2,1)}, u32[]{:S(2)}) copy-start(bf16[256,2880]{0,1:T(8,128)(2,1)} %param.21) | copy-start | bytes 4423684

commit v5 on v4

--- a/solution.py
+++ b/solution.py
@@ -471,7 +471,7 @@
         received = [jnp.concatenate(received, axis=1)]
 
     columns = w_experts.shape[2]
-    early_rows = min(width // 2, 768)
+    early_rows = min(width // 2, 1024)
     attended, early = call(
         functools.partial(attend_kernel, len(received), lengths.shape[1], tok_dev, kv_rows),
         [

time: 87.5 us -> 86.8 us (level)
  blocking collectives: 31.5 us -> 30.3 us
    all_to_all x1, blocking collectives: 27.3 us -> 26 us  [local(): lax.all_to_all(outgoing.reshape(tensors, slot_cap, width), 'tensor', spli...]
  transfers between devices with their start and end apart: 11 -> 11, of which waited for: 2 -> 3; matrix products, arithmetic and copies ran while one was open for 2% -> 2% of each run, Pallas kernels for 19% -> 19%
where the time goes in v5:
time: 86.8 us; the launch traced here: 86.1 us
  blocking collectives  30.3 us (35%)
  Pallas kernels  24.2 us (28%)
  starting transfers between devices  19.5 us (22%)
  local copies, waits for them, and re-layouts  7.04 us (8%)
  waiting for transfers between devices  3.69 us (4%)
  between operations  1.41 us (2%)
    all_to_all x1, blocking collectives, local(): lax.all_to_all(outgoing.reshape(tensors, slot_cap, width), 'tensor', spli...  26 us
    ppermute x10, starting transfers between devices, swap(): lax.ppermute(values, 'tensor', [(i, i ^ bits) for i in range(tensors)])  14.5 us
    pallas_call x1, Pallas kernels, local(): call(load_kernel, jax.ShapeDtypeStruct((width - early_rows, columns), BF1...  7.09 us
    unnamed x19, local copies, waits for them, and re-layouts  6.16 us
    pallas_call x1, Pallas kernels, local(): call(expert_kernel, jax.ShapeDtypeStruct((tensors * slot_cap, columns //...  5.96 us
    pallas_call x1, Pallas kernels, local(): call(functools.partial(attend_kernel, len(received), lengths.shape[1], to...  5.17 us
    all_to_all x1, starting transfers between devices, local(): lax.all_to_all(owned, 'tensor', split_axis=0, concat_axis=0, tiled=True)  4.99 us
    ppermute x10, waiting for transfers between devices, swap(): lax.ppermute(values, 'tensor', [(i, i ^ bits) for i in range(tensors)])  3.68 us
  transfers between devices with their start and end apart: 11, of which 3 were waited for; matrix products, arithmetic and copies ran while one was open for 2% of the time, Pallas kernels for 19%

profile of v5, /device:TPU:0, one launch (start us, length us, event | category | flops | bytes accessed | tf_op | source)
XLA Modules:
  0.0 86.1 jit_solution(2513167441146340957)
XLA Ops:
  0.6 0.0 copy-start
  0.7 1.4 %copy-done = bf16[256,2880]{0,1:T(8,128)(2,1)S(1)} copy-done((bf16[256,2880]{0,1:T(8,128)(2,1)S(1)}, bf16[256,2880]{0,1:T(8,128)(2,1)}, u32[]{:S(2)}) %copy-start) | copy-done | bytes 1474584
  2.1 3.0 %collective-permute-start.1 = (bf16[1440,256]{1,0:T(8,128)(2,1)S(1)}, bf16[1440,256]{1,0:T(8,128)(2,1)S(1)}, u32[]{:S(2)}, u32[]{:S(2)}) collective-permute-start(bf16[1440,256]{1,0:T(8,128)(2,1)S(1)} %dynamic-slice_bitcast_fusion.refs_0_), channel_id=1, source_target_pairs={{0,2},{1,3},{2,0},{3,1},{4,6},{5,7},{6,4},{7,5},{8,10},{9,11},{10,... | collective-permute-start | bytes 2211848 | tf_op jit(solution)/shard_map/ppermute | solution.py:391
  5.1 1.5 %collective-permute-start = (bf16[1440,256]{1,0:T(8,128)(2,1)S(1)}, bf16[1440,256]{1,0:T(8,128)(2,1)S(1)}, u32[]{:S(2)}, u32[]{:S(2)}) collective-permute-start(bf16[1440,256]{1,0:T(8,128)(2,1)S(1)} %dynamic-slice_bitcast_fusion.refs_0_), channel_id=1, source_target_pairs={{0,1},{1,0},{2,3},{3,2},{4,5},{5,4},{6,7},{7,6},{8,9},{9,8},{10,11... | collective-permute-start | bytes 2211848 | tf_op jit(solution)/shard_map/ppermute | solution.py:391
  7.2 1.9 %rotate_keys.1 = bf16[16,48,256]{2,1,0:T(8,128)(2,1)} custom-call(s32[1,1]{1,0:T(1,128)S(6)} %copy.18.block_ref, bf16[16,1024]{1,0:T(8,128)(2,1)} %bitcast.21, bf16[32,1024]{1,0:T(8,128)(2,1)} %bitcast.20), custom_call_target="tpu_custom_call" | custom-call | tf_op jit(solution)/shard_map/rotate_keys/pallas_call | solution.py:407
  9.2 5.0 %all-to-all-start = ((bf16[16,48,256]{2,1,0:T(8,128)(2,1)}), bf16[16,48,256]{2,1,0:T(8,128)(2,1)S(1)}, u32[]{:S(2)}, u32[]{:S(2)}) async-start(bf16[16,48,256]{2,1,0:T(8,128)(2,1)} %rotate_keys.1), calls=%async_computation | async-start | bytes 786432 | tf_op jit(solution)/shard_map/all_to_all | solution.py:451
  14.2 0.0 copy-start.2
  14.2 0.9 %copy-done.2 = bf16[1,256,256]{2,1,0:T(8,128)(2,1)S(1)} copy-done((bf16[1,256,256]{2,1,0:T(8,128)(2,1)S(1)}, bf16[1,256,256]{2,1,0:T(8,128)(2,1)}, u32[]{:S(2)}) %copy-start.2) | copy-done | bytes 131096
  15.1 0.0 copy-start.3
  15.1 0.9 %copy-done.3 = f32[256,128]{1,0:T(8,128)S(1)} copy-done((f32[256,128]{1,0:T(8,128)S(1)}, f32[256,128]{1,0:T(8,128)}, u32[]{:S(2)}) %copy-start.3) | copy-done | bytes 131096
  16.0 0.0 copy-start.4
  16.0 0.9 %copy-done.4 = bf16[1,16,2880]{2,1,0:T(8,128)(2,1)S(1)} copy-done((bf16[1,16,2880]{2,1,0:T(8,128)(2,1)S(1)}, bf16[1,16,2880]{2,1,0:T(8,128)(2,1)}, u32[]{:S(2)}) %copy-start.4) | copy-done | bytes 92184
  16.9 0.0 copy-start.7
  16.9 0.7 copy-done.7
  17.5 0.0 copy-start.8
  17.6 0.7 copy-done.8
  18.2 1.3 %rotate_queries.1 = (bf16[80,256]{1,0:T(8,128)(2,1)S(1)}, bf16[80,256]{1,0:T(8,128)(2,1)}, bf16[80,256]{1,0:T(8,128)(2,1)}, bf16[80,256]{1,0:T(8,128)(2,1)}, bf16[48,1024]{1,0:T(8,128)(2,1)S(1)}) custom-call(s32[1,2]{1,0:T(1,128)S(1)} %copy-done.7, f32[4]{0:T(128)S(1)} %copy-done.8, f32[256,128]{1,0:T(8,128)S(1)} %copy-done.3, ...), custom_call_target="tpu_custom_call" | custom-call | tf_op jit(solution)/shard_map/rotate_queries/pallas_call | solution.py:421
  19.5 1.9 %collective-permute-start.2 = (bf16[80,256]{1,0:T(8,128)(2,1)}, bf16[80,256]{1,0:T(8,128)(2,1)S(1)}, u32[]{:S(2)}, u32[]{:S(2)}) collective-permute-start(bf16[80,256]{1,0:T(8,128)(2,1)} %get-tuple-element.34), channel_id=1, source_target_pairs={{0,1},{1,0},{2,3},{3,2},{4,5},{5,4},{6,7},{7,6},{8,9},{9,8},{10,11... | collective-permute-start | bytes 122888 | tf_op jit(solution)/shard_map/ppermute | solution.py:391
  21.4 1.5 %collective-permute-start.3 = (bf16[80,256]{1,0:T(8,128)(2,1)}, bf16[80,256]{1,0:T(8,128)(2,1)}, u32[]{:S(2)}, u32[]{:S(2)}) collective-permute-start(bf16[80,256]{1,0:T(8,128)(2,1)} %get-tuple-element.35), channel_id=1, source_target_pairs={{0,2},{1,3},{2,0},{3,1},{4,6},{5,7},{6,4},{7,5},{8,10},{9,11},{10,... | collective-permute-start | bytes 122888 | tf_op jit(solution)/shard_map/ppermute | solution.py:391
  22.9 0.1 collective-permute-start.4
  23.0 0.7 broadcast_in_dim.6.gain_ref
  23.7 0.8 copy.17
  24.5 0.1 reshape.19.names_ref
  24.6 0.8 collective-permute-done.1.bottom_ref.refs_2_
  25.4 2.2 %collective-permute-done.top_ref.refs_1_ = bf16[1440,256]{1,0:T(8,128)(2,1)S(1)} collective-permute-done((bf16[1440,256]{1,0:T(8,128)(2,1)S(1)}, bf16[1440,256]{1,0:T(8,128)(2,1)S(1)}, u32[]{:S(2)}, u32[]{:S(2)}) %collective-permute-start) | collective-permute-done | bytes 737312 | tf_op jit(solution)/shard_map/ppermute | solution.py:391
  27.6 0.9 %split.1 = (bf16[720,256]{1,0:T(8,128)(2,1)}, bf16[720,256]{1,0:T(8,128)(2,1)}) custom-call(bf16[1440,256]{1,0:T(8,128)(2,1)S(1)} %collective-permute-done.top_ref.refs_1_, bf16[1440,256]{1,0:T(8,128)(2,1)S(1)} %collective-permute-done.1.bottom_ref.refs_2_), custom_call_target="tpu_custom_call" | custom-call | tf_op jit(solution)/shard_map/split/pallas_call | solution.py:455
  28.5 0.2 collective-permute-start.5
  28.7 1.9 %collective-permute-start.6 = (bf16[720,256]{1,0:T(8,128)(2,1)}, bf16[720,256]{1,0:T(8,128)(2,1)S(1)}, u32[]{:S(2)}, u32[]{:S(2)}) collective-permute-start(bf16[720,256]{1,0:T(8,128)(2,1)} %get-tuple-element.42), channel_id=1, source_target_pairs={{0,1},{1,0},{2,3},{3,2},{4,5},{5,4},{6,7},{7,6},{8,9},{9,8},{10,11... | collective-permute-start | bytes 1105928 | tf_op jit(solution)/shard_map/ppermute | solution.py:391
  30.6 0.0 collective-permute-done.2.refs_1_
  30.6 0.0 collective-permute-done.3.refs_2_
  30.6 0.0 collective-permute-done.4.refs_3_
  30.6 0.0 all-to-all-done
  30.6 5.2 %attend.1 = (bf16[112,1024]{1,0:T(8,128)(2,1)S(1)}, bf16[1024,5760]{1,0:T(8,128)(2,1)S(1)}) custom-call(bf16[80,256]{1,0:T(8,128)(2,1)S(1)} %get-tuple-element.33.refs_0_, bf16[80,256]{1,0:T(8,128)(2,1)S(1)} %collective-permute-done.2.refs_1_, bf16[80,256]{1,0:T(8,128)(2,1)} %collective-permute-done.3.refs_2_, ...), custom_call_target="tpu_custom_call" | custom-call | flops 5000000000 | tf_op jit(solution)/shard_map/attend/pallas_call | solution.py:475
  35.8 2.1 %all_gather.6.att_ref.resid_ref = bf16[224,1024]{1,0:T(8,128)(2,1)S(1)} all-gather(bf16[112,1024]{1,0:T(8,128)(2,1)S(1)} %get-tuple-element.38), channel_id=1, replica_groups=mesh['group'=2,'tensor'=16] {'group'}, dimensions={0}, use_global_device_ids=true | all-gather | bytes 688128 | tf_op jit(solution)/shard_map/all_gather | solution.py:488
  37.9 0.0 collective-permute-done.5.refs_3_
  37.9 0.0 collective-permute-done.6.refs_4_
  37.9 1.0 %project.1 = (f32[32,1440]{1,0:T(8,128)S(1)}, bf16[32,1440]{1,0:T(8,128)(2,1)S(1)}, bf16[32,1440]{1,0:T(8,128)(2,1)S(1)}, bf16[32,1440]{1,0:T(8,128)(2,1)S(1)}) custom-call(bf16[224,1024]{1,0:T(8,128)(2,1)S(1)} %all_gather.6.att_ref.resid_ref, bf16[1440,256]{1,0:T(8,128)(2,1)S(1)} %dynamic-slice_bitcast_fusion.refs_0_, ...), custom_call_target="tpu_custom_call" | custom-call | tf_op jit(solution)/shard_map/project/pallas_call | solution.py:497
  38.9 0.0 copy-start.5
  38.9 0.0 copy-start.6
  38.9 3.7 %collective-permute-start.7 = (bf16[32,1440]{1,0:T(8,128)(2,1)S(1)}, bf16[32,1440]{1,0:T(8,128)(2,1)S(1)}, u32[]{:S(2)}, u32[]{:S(2)}) collective-permute-start(bf16[32,1440]{1,0:T(8,128)(2,1)S(1)} %get-tuple-element.48), channel_id=1, source_target_pairs={{0,12},{1,13},{2,14},{3,15},{4,8},{5,9},{6,10},{7,11},{8,4},{9,5},... | collective-permute-start | bytes 276488 | tf_op jit(solution)/shard_map/ppermute | solution.py:391
  42.6 0.0 collective-permute-start.8
  42.6 0.8 collective-permute-start.9
  43.4 7.1 %load_expert.1.late_ref = bf16[1856,5760]{1,0:T(8,128)(2,1)S(1)} custom-call(bf16[2880,5760]{1,0:T(8,128)(2,1)} %bitcast.18), custom_call_target="tpu_custom_call" | custom-call | bytes 42762240 | tf_op jit(solution)/shard_map/load_expert/pallas_call | solution.py:520
  50.5 0.0 collective-permute-done.7.refs_1_
  50.5 0.7 collective-permute-done.8.refs_2_
  51.2 0.0 collective-permute-done.9.refs_3_
  51.2 2.1 %all_gather.7.sums_ref = f32[64,1440]{1,0:T(8,128)S(1)} all-gather(f32[32,1440]{1,0:T(8,128)S(1)} %sum_planes.1), channel_id=1, replica_groups=mesh['group'=2,'tensor'=16] {'group'}, dimensions={0}, use_global_device_ids=true | all-gather | bytes 552960 | tf_op jit(solution)/shard_map/all_gather | solution.py:536
  53.3 0.0 copy-done.5
  53.3 0.0 copy-done.6
  53.3 0.8 norm_dispatch.1
  54.1 26.0 %all_to_all.10 = bf16[16,8,2880]{2,1,0:T(8,128)(2,1)S(1)} all-to-all(bf16[16,8,2880]{2,1,0:T(8,128)(2,1)S(1)} %bitcast.14), channel_id=1, replica_groups=mesh['group'=2,'tensor'=16] {'tensor'}, dimensions={0} | all-to-all | bytes 1474560 | tf_op jit(solution)/shard_map/all_to_all | solution.py:557
  80.1 0.0 copy-start.1
  80.1 6.0 %experts.1 = bf16[128,2880]{1,0:T(8,128)(2,1)} custom-call(bf16[128,2880]{1,0:T(8,128)(2,1)S(1)} %bitcast.12, bf16[1024,5760]{1,0:T(8,128)(2,1)S(1)} %get-tuple-element.58.early_ref, bf16[1856,5760]{1,0:T(8,128)(2,1)S(1)} %load_expert.1.late_ref), custom_call_target="tpu_custom_call" | custom-call | tf_op jit(solution)/shard_map/experts/pallas_call | solution.py:564
  86.1 0.0 copy-done.1
  (2 shorter events, 0.1 us)
Async XLA Ops:
  0.6 1.4 %copy-start = (bf16[256,2880]{0,1:T(8,128)(2,1)S(1)}, bf16[256,2880]{0,1:T(8,128)(2,1)}, u32[]{:S(2)}) copy-start(bf16[256,2880]{0,1:T(8,128)(2,1)} %param.21) | copy-start | bytes 4423684
  2.1 23.4 %collective-permute-start.1 = (bf16[1440,256]{1,0:T(8,128)(2,1)S(1)}, bf16[1440,256]{1,0:T(8,128)(2,1)S(1)}, u32[]{:S(2)}, u32[]{:S(2)}) collective-permute-start(bf16[1440,256]{1,0:T(8,128)(2,1)S(1)} %dynamic-slice_bitcast_fusion.refs_0_), channel_id=1, source_target_pairs={{0,2},{1,3},{2,0},{3,1},{4,6},{5,7},{6,4},{7,5},{8,10},{9,11},{10,... | collective-permute-start | bytes 2211848 | tf_op jit(solution)/shard_map/ppermute | solution.py:391
  5.1 22.5 %collective-permute-start = (bf16[1440,256]{1,0:T(8,128)(2,1)S(1)}, bf16[1440,256]{1,0:T(8,128)(2,1)S(1)}, u32[]{:S(2)}, u32[]{:S(2)}) collective-permute-start(bf16[1440,256]{1,0:T(8,128)(2,1)S(1)} %dynamic-slice_bitcast_fusion.refs_0_), channel_id=1, source_target_pairs={{0,1},{1,0},{2,3},{3,2},{4,5},{5,4},{6,7},{7,6},{8,9},{9,8},{10,11... | collective-permute-start | bytes 2211848 | tf_op jit(solution)/shard_map/ppermute | solution.py:391
  9.2 21.4 %all-to-all-start = ((bf16[16,48,256]{2,1,0:T(8,128)(2,1)}), bf16[16,48,256]{2,1,0:T(8,128)(2,1)S(1)}, u32[]{:S(2)}, u32[]{:S(2)}) async-start(bf16[16,48,256]{2,1,0:T(8,128)(2,1)} %rotate_keys.1), calls=%async_computation | async-start | bytes 786432 | tf_op jit(solution)/shard_map/all_to_all | solution.py:451
  14.2 0.9 %copy-start.2 = (bf16[1,256,256]{2,1,0:T(8,128)(2,1)S(1)}, bf16[1,256,256]{2,1,0:T(8,128)(2,1)}, u32[]{:S(2)}) copy-start(bf16[1,256,256]{2,1,0:T(8,128)(2,1)} %param.15) | copy-start | bytes 393220
  15.1 0.9 %copy-start.3 = (f32[256,128]{1,0:T(8,128)S(1)}, f32[256,128]{1,0:T(8,128)}, u32[]{:S(2)}) copy-start(f32[256,128]{1,0:T(8,128)} %constant.18.clone.turn_ref) | copy-start | bytes 393220
  16.0 0.9 %copy-start.4 = (bf16[1,16,2880]{2,1,0:T(8,128)(2,1)S(1)}, bf16[1,16,2880]{2,1,0:T(8,128)(2,1)}, u32[]{:S(2)}) copy-start(bf16[1,16,2880]{2,1,0:T(8,128)(2,1)} %param.14) | copy-start | bytes 276484
  16.9 0.7 copy-start.7
  17.5 0.7 copy-start.8
  19.5 11.1 %collective-permute-start.2 = (bf16[80,256]{1,0:T(8,128)(2,1)}, bf16[80,256]{1,0:T(8,128)(2,1)S(1)}, u32[]{:S(2)}, u32[]{:S(2)}) collective-permute-start(bf16[80,256]{1,0:T(8,128)(2,1)} %get-tuple-element.34), channel_id=1, source_target_pairs={{0,1},{1,0},{2,3},{3,2},{4,5},{5,4},{6,7},{7,6},{8,9},{9,8},{10,11... | collective-permute-start | bytes 122888 | tf_op jit(solution)/shard_map/ppermute | solution.py:391
  21.4 9.1 %collective-permute-start.3 = (bf16[80,256]{1,0:T(8,128)(2,1)}, bf16[80,256]{1,0:T(8,128)(2,1)}, u32[]{:S(2)}, u32[]{:S(2)}) collective-permute-start(bf16[80,256]{1,0:T(8,128)(2,1)} %get-tuple-element.35), channel_id=1, source_target_pairs={{0,2},{1,3},{2,0},{3,1},{4,6},{5,7},{6,4},{7,5},{8,10},{9,11},{10,... | collective-permute-start | bytes 122888 | tf_op jit(solution)/shard_map/ppermute | solution.py:391
  22.9 7.7 %collective-permute-start.4 = (bf16[80,256]{1,0:T(8,128)(2,1)}, bf16[80,256]{1,0:T(8,128)(2,1)}, u32[]{:S(2)}, u32[]{:S(2)}) collective-permute-start(bf16[80,256]{1,0:T(8,128)(2,1)} %get-tuple-element.36), channel_id=1, source_target_pairs={{0,3},{1,2},{2,1},{3,0},{4,7},{5,6},{6,5},{7,4},{8,11},{9,10},{10,... | collective-permute-start | bytes 122888 | tf_op jit(solution)/shard_map/ppermute | solution.py:391
  28.5 9.4 %collective-permute-start.5 = (bf16[720,256]{1,0:T(8,128)(2,1)}, bf16[720,256]{1,0:T(8,128)(2,1)S(1)}, u32[]{:S(2)}, u32[]{:S(2)}) collective-permute-start(bf16[720,256]{1,0:T(8,128)(2,1)} %get-tuple-element.41), channel_id=1, source_target_pairs={{0,2},{1,3},{2,0},{3,1},{4,6},{5,7},{6,4},{7,5},{8,10},{9,11},{10,... | collective-permute-start | bytes 1105928 | tf_op jit(solution)/shard_map/ppermute | solution.py:391
  28.7 9.2 %collective-permute-start.6 = (bf16[720,256]{1,0:T(8,128)(2,1)}, bf16[720,256]{1,0:T(8,128)(2,1)S(1)}, u32[]{:S(2)}, u32[]{:S(2)}) collective-permute-start(bf16[720,256]{1,0:T(8,128)(2,1)} %get-tuple-element.42), channel_id=1, source_target_pairs={{0,1},{1,0},{2,3},{3,2},{4,5},{5,4},{6,7},{7,6},{8,9},{9,8},{10,11... | collective-permute-start | bytes 1105928 | tf_op jit(solution)/shard_map/ppermute | solution.py:391
  38.9 14.4 %copy-start.5 = (bf16[128,32]{1,0:T(8,128)(2,1)S(1)}, bf16[128,32]{1,0:T(8,128)(2,1)}, u32[]{:S(2)}) copy-start(bf16[128,32]{1,0:T(8,128)(2,1)} %constant.20.clone.source_ref) | copy-start | bytes 24580
  38.9 14.4 %copy-start.6 = (bf16[128,128]{1,0:T(8,128)(2,1)S(1)}, bf16[128,128]{1,0:T(8,128)(2,1)}, u32[]{:S(2)}) copy-start(bf16[128,128]{1,0:T(8,128)(2,1)} %constant.19.clone.earlier_ref) | copy-start | bytes 98308
  38.9 11.6 %collective-permute-start.7 = (bf16[32,1440]{1,0:T(8,128)(2,1)S(1)}, bf16[32,1440]{1,0:T(8,128)(2,1)S(1)}, u32[]{:S(2)}, u32[]{:S(2)}) collective-permute-start(bf16[32,1440]{1,0:T(8,128)(2,1)S(1)} %get-tuple-element.48), channel_id=1, source_target_pairs={{0,12},{1,13},{2,14},{3,15},{4,8},{5,9},{6,10},{7,11},{8,4},{9,5},... | collective-permute-start | bytes 276488 | tf_op jit(solution)/shard_map/ppermute | solution.py:391
  42.6 8.6 %collective-permute-start.8 = (bf16[32,1440]{1,0:T(8,128)(2,1)S(1)}, bf16[32,1440]{1,0:T(8,128)(2,1)S(1)}, u32[]{:S(2)}, u32[]{:S(2)}) collective-permute-start(bf16[32,1440]{1,0:T(8,128)(2,1)S(1)} %get-tuple-element.49), channel_id=1, source_target_pairs={{0,8},{1,9},{2,10},{3,11},{4,12},{5,13},{6,14},{7,15},{8,0},{9,1},... | collective-permute-start | bytes 276488 | tf_op jit(solution)/shard_map/ppermute | solution.py:391
  42.6 8.6 %collective-permute-start.9 = (bf16[32,1440]{1,0:T(8,128)(2,1)S(1)}, bf16[32,1440]{1,0:T(8,128)(2,1)S(1)}, u32[]{:S(2)}, u32[]{:S(2)}) collective-permute-start(bf16[32,1440]{1,0:T(8,128)(2,1)S(1)} %get-tuple-element.50), channel_id=1, source_target_pairs={{0,4},{1,5},{2,6},{3,7},{4,0},{5,1},{6,2},{7,3},{8,12},{9,13},{10,... | collective-permute-start | bytes 276488 | tf_op jit(solution)/shard_map/ppermute | solution.py:391
  80.1 6.0 %copy-start.1 = (bf16[256,2880]{0,1:T(8,128)(2,1)S(1)}, bf16[256,2880]{0,1:T(8,128)(2,1)}, u32[]{:S(2)}) copy-start(bf16[256,2880]{0,1:T(8,128)(2,1)} %param.21) | copy-start | bytes 4423684

commit v6 on v5

--- a/solution.py
+++ b/solution.py
@@ -151,9 +151,16 @@
 
 def attend_kernel(blocks, requests, tok_dev, kv_rows, *refs):
     q_refs, kv_ref, w_ref = refs[:blocks], refs[blocks], refs[blocks + 1]
-    resid_refs, (out_ref, early_ref, sem) = refs[blocks + 2 : -3], refs[-3:]
-    load = pltpu.make_async_copy(w_ref.at[pl.ds(0, early_ref.shape[0])], early_ref, sem)
-    load.start()
+    resid_refs, (out_ref, early_ref, sems) = refs[blocks + 2 : -3], refs[-3:]
+    share = early_ref.shape[0] // 4
+    loads = [
+        pltpu.make_async_copy(
+            w_ref.at[pl.ds(k * share, share)], early_ref.at[pl.ds(k * share, share)], sems.at[k]
+        )
+        for k in range(4)
+    ]
+    for load in loads:
+        load.start()
     rows = q_refs[0].shape[0] - 16
     inner = lax.axis_index("tensor") & (PLANE - 1)
     plane = lax.axis_index("tensor") >> log2(PLANE)
@@ -219,7 +226,8 @@
             ).astype(BF16)
     for resid_ref in resid_refs:
         out_ref[rows:, :] = resid_ref[...]
-    load.wait()
+    for load in loads:
+        load.wait()
 
 
 def project_kernel(tok_dev, groups, att_ref, *refs):
@@ -480,7 +488,7 @@
         ],
         [VMEM] * (1 + len(received)) + [ANY] + [VMEM] * len(packed),
         "attend",
-        scratch=[pltpu.SemaphoreType.DMA],
+        scratch=[pltpu.SemaphoreType.DMA((4,))],
         limit=26,
         flops=5000000000,
     )(*received, kv, w_experts[0], *packed)

time: 86.8 us -> 87.1 us (level)
  no operation moved by 1% of the time
where the time goes in v6:
time: 87.1 us; the launch traced here: 86.4 us
  blocking collectives  30.2 us (35%)
  Pallas kernels  24.5 us (28%)
  starting transfers between devices  19.5 us (22%)
  local copies, waits for them, and re-layouts  7.04 us (8%)
  waiting for transfers between devices  3.7 us (4%)
  between operations  1.41 us (2%)
    all_to_all x1, blocking collectives, local(): lax.all_to_all(outgoing.reshape(tensors, slot_cap, width), 'tensor', spli...  26 us
    ppermute x10, starting transfers between devices, swap(): lax.ppermute(values, 'tensor', [(i, i ^ bits) for i in range(tensors)])  14.5 us
    pallas_call x1, Pallas kernels, local(): call(load_kernel, jax.ShapeDtypeStruct((width - early_rows, columns), BF1...  7.09 us
    unnamed x19, local copies, waits for them, and re-layouts  6.16 us
    pallas_call x1, Pallas kernels, local(): call(expert_kernel, jax.ShapeDtypeStruct((tensors * slot_cap, columns //...  5.96 us
    pallas_call x1, Pallas kernels, local(): call(functools.partial(attend_kernel, len(received), lengths.shape[1], to...  5.51 us
    all_to_all x1, starting transfers between devices, local(): lax.all_to_all(owned, 'tensor', split_axis=0, concat_axis=0, tiled=True)  4.99 us
    ppermute x10, waiting for transfers between devices, swap(): lax.ppermute(values, 'tensor', [(i, i ^ bits) for i in range(tensors)])  3.7 us
  transfers between devices with their start and end apart: 11, of which 3 were waited for; matrix products, arithmetic and copies ran while one was open for 2% of the time, Pallas kernels for 19%

profile of v6, /device:TPU:0, one launch (start us, length us, event | category | flops | bytes accessed | tf_op | source)
XLA Modules:
  0.0 86.4 jit_solution(7448293080604184890)
XLA Ops:
  0.6 0.0 copy-start
  0.7 1.4 %copy-done = bf16[256,2880]{0,1:T(8,128)(2,1)S(1)} copy-done((bf16[256,2880]{0,1:T(8,128)(2,1)S(1)}, bf16[256,2880]{0,1:T(8,128)(2,1)}, u32[]{:S(2)}) %copy-start) | copy-done | bytes 1474584
  2.1 3.0 %collective-permute-start.1 = (bf16[1440,256]{1,0:T(8,128)(2,1)S(1)}, bf16[1440,256]{1,0:T(8,128)(2,1)S(1)}, u32[]{:S(2)}, u32[]{:S(2)}) collective-permute-start(bf16[1440,256]{1,0:T(8,128)(2,1)S(1)} %dynamic-slice_bitcast_fusion.refs_0_), channel_id=1, source_target_pairs={{0,2},{1,3},{2,0},{3,1},{4,6},{5,7},{6,4},{7,5},{8,10},{9,11},{10,... | collective-permute-start | bytes 2211848 | tf_op jit(solution)/shard_map/ppermute | solution.py:399
  5.1 1.5 %collective-permute-start = (bf16[1440,256]{1,0:T(8,128)(2,1)S(1)}, bf16[1440,256]{1,0:T(8,128)(2,1)S(1)}, u32[]{:S(2)}, u32[]{:S(2)}) collective-permute-start(bf16[1440,256]{1,0:T(8,128)(2,1)S(1)} %dynamic-slice_bitcast_fusion.refs_0_), channel_id=1, source_target_pairs={{0,1},{1,0},{2,3},{3,2},{4,5},{5,4},{6,7},{7,6},{8,9},{9,8},{10,11... | collective-permute-start | bytes 2211848 | tf_op jit(solution)/shard_map/ppermute | solution.py:399
  7.2 1.9 %rotate_keys.1 = bf16[16,48,256]{2,1,0:T(8,128)(2,1)} custom-call(s32[1,1]{1,0:T(1,128)S(6)} %copy.18.block_ref, bf16[16,1024]{1,0:T(8,128)(2,1)} %bitcast.21, bf16[32,1024]{1,0:T(8,128)(2,1)} %bitcast.20), custom_call_target="tpu_custom_call" | custom-call | tf_op jit(solution)/shard_map/rotate_keys/pallas_call | solution.py:415
  9.2 5.0 %all-to-all-start = ((bf16[16,48,256]{2,1,0:T(8,128)(2,1)}), bf16[16,48,256]{2,1,0:T(8,128)(2,1)S(1)}, u32[]{:S(2)}, u32[]{:S(2)}) async-start(bf16[16,48,256]{2,1,0:T(8,128)(2,1)} %rotate_keys.1), calls=%async_computation | async-start | bytes 786432 | tf_op jit(solution)/shard_map/all_to_all | solution.py:459
  14.2 0.0 copy-start.2
  14.2 0.9 %copy-done.2 = bf16[1,256,256]{2,1,0:T(8,128)(2,1)S(1)} copy-done((bf16[1,256,256]{2,1,0:T(8,128)(2,1)S(1)}, bf16[1,256,256]{2,1,0:T(8,128)(2,1)}, u32[]{:S(2)}) %copy-start.2) | copy-done | bytes 131096
  15.1 0.0 copy-start.3
  15.1 0.9 %copy-done.3 = f32[256,128]{1,0:T(8,128)S(1)} copy-done((f32[256,128]{1,0:T(8,128)S(1)}, f32[256,128]{1,0:T(8,128)}, u32[]{:S(2)}) %copy-start.3) | copy-done | bytes 131096
  16.0 0.0 copy-start.4
  16.0 0.9 %copy-done.4 = bf16[1,16,2880]{2,1,0:T(8,128)(2,1)S(1)} copy-done((bf16[1,16,2880]{2,1,0:T(8,128)(2,1)S(1)}, bf16[1,16,2880]{2,1,0:T(8,128)(2,1)}, u32[]{:S(2)}) %copy-start.4) | copy-done | bytes 92184
  16.9 0.0 copy-start.7
  16.9 0.7 copy-done.7
  17.5 0.0 copy-start.8
  17.6 0.7 copy-done.8
  18.2 1.3 %rotate_queries.1 = (bf16[80,256]{1,0:T(8,128)(2,1)S(1)}, bf16[80,256]{1,0:T(8,128)(2,1)}, bf16[80,256]{1,0:T(8,128)(2,1)}, bf16[80,256]{1,0:T(8,128)(2,1)}, bf16[48,1024]{1,0:T(8,128)(2,1)S(1)}) custom-call(s32[1,2]{1,0:T(1,128)S(1)} %copy-done.7, f32[4]{0:T(128)S(1)} %copy-done.8, f32[256,128]{1,0:T(8,128)S(1)} %copy-done.3, ...), custom_call_target="tpu_custom_call" | custom-call | tf_op jit(solution)/shard_map/rotate_queries/pallas_call | solution.py:429
  19.5 1.9 %collective-permute-start.2 = (bf16[80,256]{1,0:T(8,128)(2,1)}, bf16[80,256]{1,0:T(8,128)(2,1)S(1)}, u32[]{:S(2)}, u32[]{:S(2)}) collective-permute-start(bf16[80,256]{1,0:T(8,128)(2,1)} %get-tuple-element.34), channel_id=1, source_target_pairs={{0,1},{1,0},{2,3},{3,2},{4,5},{5,4},{6,7},{7,6},{8,9},{9,8},{10,11... | collective-permute-start | bytes 122888 | tf_op jit(solution)/shard_map/ppermute | solution.py:399
  21.4 1.5 %collective-permute-start.3 = (bf16[80,256]{1,0:T(8,128)(2,1)}, bf16[80,256]{1,0:T(8,128)(2,1)}, u32[]{:S(2)}, u32[]{:S(2)}) collective-permute-start(bf16[80,256]{1,0:T(8,128)(2,1)} %get-tuple-element.35), channel_id=1, source_target_pairs={{0,2},{1,3},{2,0},{3,1},{4,6},{5,7},{6,4},{7,5},{8,10},{9,11},{10,... | collective-permute-start | bytes 122888 | tf_op jit(solution)/shard_map/ppermute | solution.py:399
  22.9 0.1 collective-permute-start.4
  23.0 0.7 broadcast_in_dim.6.gain_ref
  23.7 0.8 copy.17
  24.5 0.1 reshape.19.names_ref
  24.6 0.8 collective-permute-done.1.bottom_ref.refs_2_
  25.4 2.2 %collective-permute-done.top_ref.refs_1_ = bf16[1440,256]{1,0:T(8,128)(2,1)S(1)} collective-permute-done((bf16[1440,256]{1,0:T(8,128)(2,1)S(1)}, bf16[1440,256]{1,0:T(8,128)(2,1)S(1)}, u32[]{:S(2)}, u32[]{:S(2)}) %collective-permute-start) | collective-permute-done | bytes 737312 | tf_op jit(solution)/shard_map/ppermute | solution.py:399
  27.6 0.9 %split.1 = (bf16[720,256]{1,0:T(8,128)(2,1)}, bf16[720,256]{1,0:T(8,128)(2,1)}) custom-call(bf16[1440,256]{1,0:T(8,128)(2,1)S(1)} %collective-permute-done.top_ref.refs_1_, bf16[1440,256]{1,0:T(8,128)(2,1)S(1)} %collective-permute-done.1.bottom_ref.refs_2_), custom_call_target="tpu_custom_call" | custom-call | tf_op jit(solution)/shard_map/split/pallas_call | solution.py:463
  28.5 0.2 collective-permute-start.5
  28.7 1.9 %collective-permute-start.6 = (bf16[720,256]{1,0:T(8,128)(2,1)}, bf16[720,256]{1,0:T(8,128)(2,1)S(1)}, u32[]{:S(2)}, u32[]{:S(2)}) collective-permute-start(bf16[720,256]{1,0:T(8,128)(2,1)} %get-tuple-element.42), channel_id=1, source_target_pairs={{0,1},{1,0},{2,3},{3,2},{4,5},{5,4},{6,7},{7,6},{8,9},{9,8},{10,11... | collective-permute-start | bytes 1105928 | tf_op jit(solution)/shard_map/ppermute | solution.py:399
  30.6 0.0 collective-permute-done.2.refs_1_
  30.6 0.0 collective-permute-done.3.refs_2_
  30.6 0.0 collective-permute-done.4.refs_3_
  30.6 0.0 all-to-all-done
  30.6 5.5 %attend.1 = (bf16[112,1024]{1,0:T(8,128)(2,1)S(1)}, bf16[1024,5760]{1,0:T(8,128)(2,1)S(1)}) custom-call(bf16[80,256]{1,0:T(8,128)(2,1)S(1)} %get-tuple-element.33.refs_0_, bf16[80,256]{1,0:T(8,128)(2,1)S(1)} %collective-permute-done.2.refs_1_, bf16[80,256]{1,0:T(8,128)(2,1)} %collective-permute-done.3.refs_2_, ...), custom_call_target="tpu_custom_call" | custom-call | flops 5000000000 | tf_op jit(solution)/shard_map/attend/pallas_call | solution.py:483
  36.1 2.1 %all_gather.6.att_ref.resid_ref = bf16[224,1024]{1,0:T(8,128)(2,1)S(1)} all-gather(bf16[112,1024]{1,0:T(8,128)(2,1)S(1)} %get-tuple-element.38), channel_id=1, replica_groups=mesh['group'=2,'tensor'=16] {'group'}, dimensions={0}, use_global_device_ids=true | all-gather | bytes 688128 | tf_op jit(solution)/shard_map/all_gather | solution.py:496
  38.2 0.0 collective-permute-done.5.refs_3_
  38.2 0.0 collective-permute-done.6.refs_4_
  38.2 1.0 %project.1 = (f32[32,1440]{1,0:T(8,128)S(1)}, bf16[32,1440]{1,0:T(8,128)(2,1)S(1)}, bf16[32,1440]{1,0:T(8,128)(2,1)S(1)}, bf16[32,1440]{1,0:T(8,128)(2,1)S(1)}) custom-call(bf16[224,1024]{1,0:T(8,128)(2,1)S(1)} %all_gather.6.att_ref.resid_ref, bf16[1440,256]{1,0:T(8,128)(2,1)S(1)} %dynamic-slice_bitcast_fusion.refs_0_, ...), custom_call_target="tpu_custom_call" | custom-call | tf_op jit(solution)/shard_map/project/pallas_call | solution.py:505
  39.2 0.0 copy-start.5
  39.3 0.0 copy-start.6
  39.3 3.7 %collective-permute-start.7 = (bf16[32,1440]{1,0:T(8,128)(2,1)S(1)}, bf16[32,1440]{1,0:T(8,128)(2,1)S(1)}, u32[]{:S(2)}, u32[]{:S(2)}) collective-permute-start(bf16[32,1440]{1,0:T(8,128)(2,1)S(1)} %get-tuple-element.48), channel_id=1, source_target_pairs={{0,12},{1,13},{2,14},{3,15},{4,8},{5,9},{6,10},{7,11},{8,4},{9,5},... | collective-permute-start | bytes 276488 | tf_op jit(solution)/shard_map/ppermute | solution.py:399
  42.9 0.0 collective-permute-start.8
  43.0 0.8 collective-permute-start.9
  43.7 7.1 %load_expert.1.late_ref = bf16[1856,5760]{1,0:T(8,128)(2,1)S(1)} custom-call(bf16[2880,5760]{1,0:T(8,128)(2,1)} %bitcast.18), custom_call_target="tpu_custom_call" | custom-call | bytes 42762240 | tf_op jit(solution)/shard_map/load_expert/pallas_call | solution.py:528
  50.8 0.0 collective-permute-done.7.refs_1_
  50.8 0.7 collective-permute-done.8.refs_2_
  51.5 0.0 collective-permute-done.9.refs_3_
  51.6 2.1 %all_gather.7.sums_ref = f32[64,1440]{1,0:T(8,128)S(1)} all-gather(f32[32,1440]{1,0:T(8,128)S(1)} %sum_planes.1), channel_id=1, replica_groups=mesh['group'=2,'tensor'=16] {'group'}, dimensions={0}, use_global_device_ids=true | all-gather | bytes 552960 | tf_op jit(solution)/shard_map/all_gather | solution.py:544
  53.6 0.0 copy-done.5
  53.7 0.0 copy-done.6
  53.7 0.8 norm_dispatch.1
  54.4 26.0 %all_to_all.10 = bf16[16,8,2880]{2,1,0:T(8,128)(2,1)S(1)} all-to-all(bf16[16,8,2880]{2,1,0:T(8,128)(2,1)S(1)} %bitcast.14), channel_id=1, replica_groups=mesh['group'=2,'tensor'=16] {'tensor'}, dimensions={0} | all-to-all | bytes 1474560 | tf_op jit(solution)/shard_map/all_to_all | solution.py:565
  80.5 0.0 copy-start.1
  80.5 6.0 %experts.1 = bf16[128,2880]{1,0:T(8,128)(2,1)} custom-call(bf16[128,2880]{1,0:T(8,128)(2,1)S(1)} %bitcast.12, bf16[1024,5760]{1,0:T(8,128)(2,1)S(1)} %get-tuple-element.58.early_ref, bf16[1856,5760]{1,0:T(8,128)(2,1)S(1)} %load_expert.1.late_ref), custom_call_target="tpu_custom_call" | custom-call | tf_op jit(solution)/shard_map/experts/pallas_call | solution.py:572
  86.4 0.0 copy-done.1
  (2 shorter events, 0.1 us)
Async XLA Ops:
  0.6 1.4 %copy-start = (bf16[256,2880]{0,1:T(8,128)(2,1)S(1)}, bf16[256,2880]{0,1:T(8,128)(2,1)}, u32[]{:S(2)}) copy-start(bf16[256,2880]{0,1:T(8,128)(2,1)} %param.21) | copy-start | bytes 4423684
  2.1 23.4 %collective-permute-start.1 = (bf16[1440,256]{1,0:T(8,128)(2,1)S(1)}, bf16[1440,256]{1,0:T(8,128)(2,1)S(1)}, u32[]{:S(2)}, u32[]{:S(2)}) collective-permute-start(bf16[1440,256]{1,0:T(8,128)(2,1)S(1)} %dynamic-slice_bitcast_fusion.refs_0_), channel_id=1, source_target_pairs={{0,2},{1,3},{2,0},{3,1},{4,6},{5,7},{6,4},{7,5},{8,10},{9,11},{10,... | collective-permute-start | bytes 2211848 | tf_op jit(solution)/shard_map/ppermute | solution.py:399
  5.1 22.5 %collective-permute-start = (bf16[1440,256]{1,0:T(8,128)(2,1)S(1)}, bf16[1440,256]{1,0:T(8,128)(2,1)S(1)}, u32[]{:S(2)}, u32[]{:S(2)}) collective-permute-start(bf16[1440,256]{1,0:T(8,128)(2,1)S(1)} %dynamic-slice_bitcast_fusion.refs_0_), channel_id=1, source_target_pairs={{0,1},{1,0},{2,3},{3,2},{4,5},{5,4},{6,7},{7,6},{8,9},{9,8},{10,11... | collective-permute-start | bytes 2211848 | tf_op jit(solution)/shard_map/ppermute | solution.py:399
  9.2 21.4 %all-to-all-start = ((bf16[16,48,256]{2,1,0:T(8,128)(2,1)}), bf16[16,48,256]{2,1,0:T(8,128)(2,1)S(1)}, u32[]{:S(2)}, u32[]{:S(2)}) async-start(bf16[16,48,256]{2,1,0:T(8,128)(2,1)} %rotate_keys.1), calls=%async_computation | async-start | bytes 786432 | tf_op jit(solution)/shard_map/all_to_all | solution.py:459
  14.2 0.9 %copy-start.2 = (bf16[1,256,256]{2,1,0:T(8,128)(2,1)S(1)}, bf16[1,256,256]{2,1,0:T(8,128)(2,1)}, u32[]{:S(2)}) copy-start(bf16[1,256,256]{2,1,0:T(8,128)(2,1)} %param.15) | copy-start | bytes 393220
  15.1 0.9 %copy-start.3 = (f32[256,128]{1,0:T(8,128)S(1)}, f32[256,128]{1,0:T(8,128)}, u32[]{:S(2)}) copy-start(f32[256,128]{1,0:T(8,128)} %constant.18.clone.turn_ref) | copy-start | bytes 393220
  16.0 0.9 %copy-start.4 = (bf16[1,16,2880]{2,1,0:T(8,128)(2,1)S(1)}, bf16[1,16,2880]{2,1,0:T(8,128)(2,1)}, u32[]{:S(2)}) copy-start(bf16[1,16,2880]{2,1,0:T(8,128)(2,1)} %param.14) | copy-start | bytes 276484
  16.9 0.7 copy-start.7
  17.5 0.7 copy-start.8
  19.5 11.1 %collective-permute-start.2 = (bf16[80,256]{1,0:T(8,128)(2,1)}, bf16[80,256]{1,0:T(8,128)(2,1)S(1)}, u32[]{:S(2)}, u32[]{:S(2)}) collective-permute-start(bf16[80,256]{1,0:T(8,128)(2,1)} %get-tuple-element.34), channel_id=1, source_target_pairs={{0,1},{1,0},{2,3},{3,2},{4,5},{5,4},{6,7},{7,6},{8,9},{9,8},{10,11... | collective-permute-start | bytes 122888 | tf_op jit(solution)/shard_map/ppermute | solution.py:399
  21.4 9.1 %collective-permute-start.3 = (bf16[80,256]{1,0:T(8,128)(2,1)}, bf16[80,256]{1,0:T(8,128)(2,1)}, u32[]{:S(2)}, u32[]{:S(2)}) collective-permute-start(bf16[80,256]{1,0:T(8,128)(2,1)} %get-tuple-element.35), channel_id=1, source_target_pairs={{0,2},{1,3},{2,0},{3,1},{4,6},{5,7},{6,4},{7,5},{8,10},{9,11},{10,... | collective-permute-start | bytes 122888 | tf_op jit(solution)/shard_map/ppermute | solution.py:399
  22.9 7.7 %collective-permute-start.4 = (bf16[80,256]{1,0:T(8,128)(2,1)}, bf16[80,256]{1,0:T(8,128)(2,1)}, u32[]{:S(2)}, u32[]{:S(2)}) collective-permute-start(bf16[80,256]{1,0:T(8,128)(2,1)} %get-tuple-element.36), channel_id=1, source_target_pairs={{0,3},{1,2},{2,1},{3,0},{4,7},{5,6},{6,5},{7,4},{8,11},{9,10},{10,... | collective-permute-start | bytes 122888 | tf_op jit(solution)/shard_map/ppermute | solution.py:399
  28.5 9.7 %collective-permute-start.5 = (bf16[720,256]{1,0:T(8,128)(2,1)}, bf16[720,256]{1,0:T(8,128)(2,1)S(1)}, u32[]{:S(2)}, u32[]{:S(2)}) collective-permute-start(bf16[720,256]{1,0:T(8,128)(2,1)} %get-tuple-element.41), channel_id=1, source_target_pairs={{0,2},{1,3},{2,0},{3,1},{4,6},{5,7},{6,4},{7,5},{8,10},{9,11},{10,... | collective-permute-start | bytes 1105928 | tf_op jit(solution)/shard_map/ppermute | solution.py:399
  28.7 9.6 %collective-permute-start.6 = (bf16[720,256]{1,0:T(8,128)(2,1)}, bf16[720,256]{1,0:T(8,128)(2,1)S(1)}, u32[]{:S(2)}, u32[]{:S(2)}) collective-permute-start(bf16[720,256]{1,0:T(8,128)(2,1)} %get-tuple-element.42), channel_id=1, source_target_pairs={{0,1},{1,0},{2,3},{3,2},{4,5},{5,4},{6,7},{7,6},{8,9},{9,8},{10,11... | collective-permute-start | bytes 1105928 | tf_op jit(solution)/shard_map/ppermute | solution.py:399
  39.2 14.4 %copy-start.5 = (bf16[128,32]{1,0:T(8,128)(2,1)S(1)}, bf16[128,32]{1,0:T(8,128)(2,1)}, u32[]{:S(2)}) copy-start(bf16[128,32]{1,0:T(8,128)(2,1)} %constant.20.clone.source_ref) | copy-start | bytes 24580
  39.3 14.4 %copy-start.6 = (bf16[128,128]{1,0:T(8,128)(2,1)S(1)}, bf16[128,128]{1,0:T(8,128)(2,1)}, u32[]{:S(2)}) copy-start(bf16[128,128]{1,0:T(8,128)(2,1)} %constant.19.clone.earlier_ref) | copy-start | bytes 98308
  39.3 11.6 %collective-permute-start.7 = (bf16[32,1440]{1,0:T(8,128)(2,1)S(1)}, bf16[32,1440]{1,0:T(8,128)(2,1)S(1)}, u32[]{:S(2)}, u32[]{:S(2)}) collective-permute-start(bf16[32,1440]{1,0:T(8,128)(2,1)S(1)} %get-tuple-element.48), channel_id=1, source_target_pairs={{0,12},{1,13},{2,14},{3,15},{4,8},{5,9},{6,10},{7,11},{8,4},{9,5},... | collective-permute-start | bytes 276488 | tf_op jit(solution)/shard_map/ppermute | solution.py:399
  42.9 8.6 %collective-permute-start.8 = (bf16[32,1440]{1,0:T(8,128)(2,1)S(1)}, bf16[32,1440]{1,0:T(8,128)(2,1)S(1)}, u32[]{:S(2)}, u32[]{:S(2)}) collective-permute-start(bf16[32,1440]{1,0:T(8,128)(2,1)S(1)} %get-tuple-element.49), channel_id=1, source_target_pairs={{0,8},{1,9},{2,10},{3,11},{4,12},{5,13},{6,14},{7,15},{8,0},{9,1},... | collective-permute-start | bytes 276488 | tf_op jit(solution)/shard_map/ppermute | solution.py:399
  43.0 8.6 %collective-permute-start.9 = (bf16[32,1440]{1,0:T(8,128)(2,1)S(1)}, bf16[32,1440]{1,0:T(8,128)(2,1)S(1)}, u32[]{:S(2)}, u32[]{:S(2)}) collective-permute-start(bf16[32,1440]{1,0:T(8,128)(2,1)S(1)} %get-tuple-element.50), channel_id=1, source_target_pairs={{0,4},{1,5},{2,6},{3,7},{4,0},{5,1},{6,2},{7,3},{8,12},{9,13},{10,... | collective-permute-start | bytes 276488 | tf_op jit(solution)/shard_map/ppermute | solution.py:399
  80.5 6.0 %copy-start.1 = (bf16[256,2880]{0,1:T(8,128)(2,1)S(1)}, bf16[256,2880]{0,1:T(8,128)(2,1)}, u32[]{:S(2)}) copy-start(bf16[256,2880]{0,1:T(8,128)(2,1)} %param.21) | copy-start | bytes 4423684
